TPU v7x, 256 devices: a whole 4x4x8 slice. The times are simulated.
256 devices in a mesh: seq: 16 (over z, y_lo), head: 8 (over x, y_hi), rows: 2 (over core).
Axes of the slice: x: 4, y: 4 (y_hi: 2, y_lo: 2; y = y_hi * 2 + y_lo), z: 8, core: 2. Of those that a mesh axis runs over, the one named last changes fastest.
Arguments:
- queries: bfloat16 [512, 64, 128], P(('rows', 'seq'), 'head'), may hold values from -15 to 15
- row_adapter: int32 [512], P(('rows', 'seq')), may hold values from 0 to 63
- doc_keys: bfloat16 [65536, 8, 128], P('seq', 'head'), may hold values from -6 to 6
- doc_values: bfloat16 [65536, 8, 128], P('seq', 'head'), may hold values from -6 to 6
- patch_keys: bfloat16 [256, 128, 8, 128], P('seq', None, 'head'), may hold values from -8 to 8
- patch_values: bfloat16 [256, 128, 8, 128], P('seq', None, 'head'), may hold values from -6 to 6
- patch_block: int32 [256], replicated, may hold values from 0 to 511, as said below
- patch_slot: int32 [256], replicated, may hold values from 0 to 255, each once
- out_weight: bfloat16 [8192, 8192], P('head', 'seq'), may hold values from -0.0625 to 0.0625
Outputs:
- mixed: float32 [512, 8192], P(('rows', 'head'), 'seq')
Inputs may be any that keep to these rules, and one draw needn't show every extreme that they name: `patch_block`: the 4 entries of one adapter name different blocks. `patch_slot`: each slot is named by one entry.
All inputs are finite; a program needn't handle non-finite values.
Results may differ from a plain program's by a relative error of at most 0.004.
Values may be sent and summed in bfloat16 or wider, within the bound.
No kernel may reach another device: no remote copies, remote signals or barrier semaphores. Data moves between devices by JAX's collectives and lax.ppermute only.
A program may use at most 64 MiB of HBM per device.

v0:
```python
import math

import jax
import jax.numpy as jnp
from jax import lax
from jax.sharding import PartitionSpec as P

BLK = 128
ADAPTERS = 64
PATCHES = 4


masked_score = -1e30


def per_device(
    queries,
    row_adapter,
    doc_keys,
    doc_values,
    patch_keys,
    patch_values,
    patch_block,
    patch_slot,
    out_weight,
):
    gathered, adapters_all = (
        lax.all_gather(queries, "seq", axis=0, tiled=True),
        lax.all_gather(row_adapter, "seq", axis=0, tiled=True),
    )
    count = gathered.shape[0]
    heads = gathered.shape[1]
    width = gathered.shape[2]
    kv_heads = doc_keys.shape[1]
    group = heads // kv_heads
    scale = width ** (-0.5)
    grouped = gathered.reshape(count, kv_heads, group, width)
    seq_index = lax.axis_index("seq")
    doc_len = doc_keys.shape[0]
    blocks_here = doc_len // BLK
    adapter_ids = jnp.arange(ADAPTERS, dtype=jnp.int32)
    onehot = (adapters_all[:, None] == adapter_ids[None, :]).astype(jnp.int32)
    row_blocks = jnp.dot(onehot, patch_block.reshape(ADAPTERS, PATCHES))
    local_ids = seq_index * blocks_here + jnp.arange(blocks_here, dtype=jnp.int32)
    hidden_blocks = jnp.any(row_blocks[:, :, None] == local_ids[None, None, :], axis=1)
    live_blocks = jnp.logical_not(hidden_blocks)
    slot_count = patch_keys.shape[0]
    slot_ids = seq_index * slot_count + jnp.arange(slot_count, dtype=jnp.int32)
    entry_owner = jnp.arange(patch_slot.shape[0], dtype=jnp.int32) // PATCHES
    slot_adapter = jnp.sum(
        jnp.where(patch_slot[:, None] == slot_ids[None, :], entry_owner[:, None], 0), axis=0
    )
    patch_live = adapters_all[:, None] == slot_adapter[None, :]
    span = math.gcd(doc_len, 1024)
    spans = doc_len // span
    per_span = span // BLK

    def doc_scores(index):
        keys = lax.dynamic_slice_in_dim(doc_keys, index * span, span, 0)
        scores = (
            jnp.einsum("nkgd,tkd->nkgt", grouped, keys, preferred_element_type=jnp.float32) * scale
        )
        live = lax.dynamic_slice_in_dim(live_blocks, index * per_span, per_span, 1)
        scores = scores.reshape(count, kv_heads, group, per_span, BLK)
        return jnp.where(live[:, None, None, :, None], scores, masked_score)

    patch_scores = (
        jnp.einsum("nkgd,sbkd->nkgsb", grouped, patch_keys, preferred_element_type=jnp.float32)
        * scale
    )
    patch_scores = jnp.where(patch_live[:, None, None, :, None], patch_scores, masked_score)

    def max_step(index, running):
        return jnp.maximum(running, jnp.max(doc_scores(index), axis=(3, 4)))

    local_peak = lax.fori_loop(0, spans, max_step, jnp.max(patch_scores, axis=(3, 4)))
    peak = lax.pmax(local_peak, "seq")
    patch_weights = jnp.exp(patch_scores - peak[:, :, :, None, None]).astype(jnp.bfloat16)
    start = (
        jnp.sum(patch_weights.astype(jnp.float32), axis=(3, 4)),
        jnp.einsum(
            "nkgsb,sbkd->nkgd", patch_weights, patch_values, preferred_element_type=jnp.float32
        ),
    )

    def sum_step(index, carry):
        total, accum = carry
        weights = jnp.exp(doc_scores(index) - peak[:, :, :, None, None]).astype(jnp.bfloat16)
        values = lax.dynamic_slice_in_dim(doc_values, index * span, span, 0).reshape(
            per_span, BLK, kv_heads, width
        )
        total = total + jnp.sum(weights.astype(jnp.float32), axis=(3, 4))
        accum = accum + jnp.einsum(
            "nkgsb,sbkd->nkgd", weights, values, preferred_element_type=jnp.float32
        )
        return (total, accum)

    total, accum = lax.fori_loop(0, spans, sum_step, start)
    total_own, accum_own = (
        lax.psum_scatter(total, "seq", scatter_dimension=0, tiled=True),
        lax.psum_scatter(accum, "seq", scatter_dimension=0, tiled=True),
    )
    attended = (
        (accum_own / total_own[..., None])
        .astype(jnp.bfloat16)
        .reshape(total_own.shape[0], heads * width)
    )
    partial_value = jnp.dot(
        lax.all_gather(attended, "seq", axis=0, tiled=True),
        out_weight,
        preferred_element_type=jnp.float32,
    )
    return lax.psum_scatter(partial_value, "head", scatter_dimension=0, tiled=True)


def solution(mesh):
    placed = (
        P(("rows", "seq"), "head", None),
        P(("rows", "seq")),
        P("seq", "head", None),
        P("seq", "head", None),
        P("seq", None, "head", None),
        P("seq", None, "head", None),
        P(),
        P(),
        P("head", "seq"),
    )
    return jax.shard_map(
        per_device,
        mesh=mesh,
        in_specs=placed,
        out_specs=P(("rows", "head"), "seq"),
        check_vma=False,
    )
```

profile of v0, /device:TPU:8, one launch (start us, length us, event | category | flops | bytes accessed | tf_op | source)
XLA Modules:
  0.0 477.4 jit_solution(18207403377655773517)
XLA Ops:
  6.5 0.0 copy-start
  6.5 0.0 reduce-scatter.10.cloned.1.call-start
  6.5 1.4 dynamic-slice
  8.7 0.9 dynamic-update-slice
  9.5 18.8 %all-reduce = s32[256]{0:T(256)S(1)} all-reduce(s32[256]{0:T(256)S(1)} %dynamic-update-slice), channel_id=1, replica_groups=mesh['seq'=16,'head'=8,'rows'=2] {'seq'}, use_global_device_ids=true, to_apply=%add | all-reduce | flops 256 | bytes 2048
  28.3 0.8 copy.31
  29.1 32.7 %all_gather.10 = bf16[256,8,128]{2,0,1:T(8,128)(2,1)S(1)} all-gather(bf16[16,8,128]{2,0,1:T(8,128)(2,1)S(1)} %copy.31), channel_id=1, replica_groups=mesh['seq'=16,'head'=8,'rows'=2] {'seq'}, dimensions={0}, use_global_device_ids=true | all-gather | bytes 557056 | tf_op jit(solution)/shard_map/all_gather | solution.py:28
  61.8 0.8 reshape.172
  62.6 0.9 select_reduce_fusion
  63.4 0.1 broadcast_compare_fusion
  63.5 0.3 fusion.29
  63.8 0.1 compare_reduce_fusion
  63.9 8.0 %fusion.19 = (f32[256,8]{0,1:T(8,128)S(1)}, f32[16,128,256,8]{2,1,3,0:T(8,128)}) fusion(pred[256,16]{0,1:T(8,128)(4,1)S(1)} %broadcast_compare_fusion, bf16[256,8,128]{2,0,1:T(8,128)(2,1)S(1)} %all_gather.10, bf16[16,128,1,128]{3,1,2,0:T(8,128)(2,1)} %param.17), kind=kOutput, calls=%fused_computation.32 | convolution fusion | flops 1086322688 | bytes 17838080 | tf_op jit(solution)/shard_map/nkgd,sbkd->nkgsb/dot_general | solution.py:68
  72.0 9.7 %while.28 = (s32[]{:T(128)}, f32[256,1,8]{0,2,1:T(8,128)S(1)}, pred[256,32]{0,1:T(8,128)(4,1)S(1)}, bf16[4096,1,128]{2,0,1:T(8,128)(2,1)}, bf16[256,1,8,128]{3,0...) while((s32[]{:T(128)}, f32[256,1,8]{0,2,1:T(8,128)S(1)}, ...), condition=%wide.region_5.6_spmd, body=%wide.region_3.5_spmd.sunk | while | flops 543162368 | bytes 1349841 | solution.py:76
  72.0 0.1 broadcast_in_dim.143
  72.0 2.3 fusion.45
  74.4 0.1 broadcast_in_dim.143
  74.5 2.3 fusion.45
  76.8 0.1 broadcast_in_dim.143
  76.9 2.3 fusion.45
  79.2 0.1 broadcast_in_dim.143
  79.3 2.3 fusion.45
  81.6 32.9 %pmax.7 = f32[256,1,8]{0,2,1:T(8,128)S(1)} all-reduce(f32[256,1,8]{0,2,1:T(8,128)S(1)} %get-tuple-element.239), channel_id=1, replica_groups=mesh['seq'=16,'head'=8,'rows'=2] {'seq'}, use_global_device_ids=true, to_apply=%region_6.7 | all-reduce | flops 2048 | bytes 16384 | tf_op jit(solution)/shard_map/pmax | solution.py:77
  114.6 0.0 copy-start.1
  114.6 9.1 %convert_reduce_fusion.1 = f32[256,8]{0,1:T(8,128)S(1)} fusion(f32[256,8]{0,1:T(8,128)S(1)} %bitcast.160, f32[16,128,256,8]{2,1,3,0:T(8,128)} %get-tuple-element.303, pred[256,16]{0,1:T(8,128)(4,1)S(1)} %broadcast_compare_fusion), kind=kLoop, calls=%fused_computation.30 | loop fusion | flops 25163776 | bytes 16797696 | tf_op jit(solution)/shard_map/reduce_sum | solution.py:80
  123.7 0.0 copy-done.1
  123.7 7.7 %fusion.22 = f32[256,1,8,128]{0,3,2,1:T(8,128)S(1)} fusion(bf16[16,128,1,128]{3,1,2,0:T(8,128)(2,1)S(1)} %copy-done.1, f32[16,128,256,8]{2,1,3,0:T(8,128)} %get-tuple-element.303, f32[256,8]{0,1:T(8,128)S(1)} %bitcast.161, pred[256,16]{0,1:T(8,128)(4,1)S(1)} %broadcast_compare_fusion), kind=kOutput, calls=%fused_computation.35 | convolution fusion | flops 1090519040 | bytes 18362368 | tf_op jit(solution)/shard_map/nkgsb,sbkd->nkgd/dot_general | solution.py:81
  131.4 85.4 %while.29 = (s32[]{:T(128)}, f32[256,1,8]{0,2,1:T(8,128)S(1)}, f32[256,1,8,128]{0,3,2,1:T(8,128)S(1)}, pred[256,32]{0,1:T(8,128)(4,1)S(1)}, bf16[4096,1,128]{2,0...) while((s32[]{:T(128)}, f32[256,1,8]{0,2,1:T(8,128)S(1)}, ...), condition=%wide.region_10.11_spmd, body=%wide.region_8.10_spmd.sunk | while | flops 1092878336 | bytes 37806316 | solution.py:98
  131.5 0.1 broadcast_in_dim.148
  131.6 6.4 %convert_reduce_fusion.3 = (f32[256,8]{0,1:T(8,128)S(1)}, f32[1024,256,8]{1,0,2:T(8,128)}) fusion(f32[256,8]{0,1:T(8,128)S(1)} %bitcast.162, pred[256,1024]{0,1:T(8,128)(4,1)S(1)} %bitcast.156, bf16[256,1,8,128]{3,0,2,1:T(8,128)(2,1)S(1)} %get-tuple-element.454, bf16[4096,1,128]{2,0,1:T(8,128)(2,1)} %get-tuple-element.453, s32[]{:T(128)S(6)} %select_n.119), kind=kOutput, calls=%fused_computation.13.clone.1 | convolution fusion | flops 549451776 | bytes 9453572 | tf_op jit(solution)/shard_map/while/body/eval_jaxpr/nkgd,tkd->nkgt/dot_general | solution.py:61
  138.0 9.1 %copy.49 = f32[256,8,8,128]{3,0,2,1:T(8,128)} copy(f32[256,8,8,128]{0,3,2,1:T(8,128)} %bitcast.154) | data formatting | bytes 16777216 | tf_op jit(solution)/shard_map/while/body/eval_jaxpr/reshape | solution.py:64
  147.1 1.0 constant_dynamic-slice_fusion.8
  148.1 4.7 fusion.47
  152.8 0.1 broadcast_in_dim.148
  152.9 6.4 %convert_reduce_fusion.3 = (f32[256,8]{0,1:T(8,128)S(1)}, f32[1024,256,8]{1,0,2:T(8,128)}) fusion(f32[256,8]{0,1:T(8,128)S(1)} %bitcast.162, pred[256,1024]{0,1:T(8,128)(4,1)S(1)} %bitcast.156, bf16[256,1,8,128]{3,0,2,1:T(8,128)(2,1)S(1)} %get-tuple-element.454, bf16[4096,1,128]{2,0,1:T(8,128)(2,1)} %get-tuple-element.453, s32[]{:T(128)S(6)} %select_n.119), kind=kOutput, calls=%fused_computation.13.clone.1 | convolution fusion | flops 549451776 | bytes 9453572 | tf_op jit(solution)/shard_map/while/body/eval_jaxpr/nkgd,tkd->nkgt/dot_general | solution.py:61
  159.3 9.1 %copy.49 = f32[256,8,8,128]{3,0,2,1:T(8,128)} copy(f32[256,8,8,128]{0,3,2,1:T(8,128)} %bitcast.154) | data formatting | bytes 16777216 | tf_op jit(solution)/shard_map/while/body/eval_jaxpr/reshape | solution.py:64
  168.4 1.0 constant_dynamic-slice_fusion.8
  169.4 4.7 fusion.47
  174.1 0.1 broadcast_in_dim.148
  174.2 6.4 %convert_reduce_fusion.3 = (f32[256,8]{0,1:T(8,128)S(1)}, f32[1024,256,8]{1,0,2:T(8,128)}) fusion(f32[256,8]{0,1:T(8,128)S(1)} %bitcast.162, pred[256,1024]{0,1:T(8,128)(4,1)S(1)} %bitcast.156, bf16[256,1,8,128]{3,0,2,1:T(8,128)(2,1)S(1)} %get-tuple-element.454, bf16[4096,1,128]{2,0,1:T(8,128)(2,1)} %get-tuple-element.453, s32[]{:T(128)S(6)} %select_n.119), kind=kOutput, calls=%fused_computation.13.clone.1 | convolution fusion | flops 549451776 | bytes 9453572 | tf_op jit(solution)/shard_map/while/body/eval_jaxpr/nkgd,tkd->nkgt/dot_general | solution.py:61
  180.6 9.1 %copy.49 = f32[256,8,8,128]{3,0,2,1:T(8,128)} copy(f32[256,8,8,128]{0,3,2,1:T(8,128)} %bitcast.154) | data formatting | bytes 16777216 | tf_op jit(solution)/shard_map/while/body/eval_jaxpr/reshape | solution.py:64
  189.8 1.0 constant_dynamic-slice_fusion.8
  190.7 4.7 fusion.47
  195.5 0.1 broadcast_in_dim.148
  195.6 6.4 %convert_reduce_fusion.3 = (f32[256,8]{0,1:T(8,128)S(1)}, f32[1024,256,8]{1,0,2:T(8,128)}) fusion(f32[256,8]{0,1:T(8,128)S(1)} %bitcast.162, pred[256,1024]{0,1:T(8,128)(4,1)S(1)} %bitcast.156, bf16[256,1,8,128]{3,0,2,1:T(8,128)(2,1)S(1)} %get-tuple-element.454, bf16[4096,1,128]{2,0,1:T(8,128)(2,1)} %get-tuple-element.453, s32[]{:T(128)S(6)} %select_n.119), kind=kOutput, calls=%fused_computation.13.clone.1 | convolution fusion | flops 549451776 | bytes 9453572 | tf_op jit(solution)/shard_map/while/body/eval_jaxpr/nkgd,tkd->nkgt/dot_general | solution.py:61
  202.0 9.1 %copy.49 = f32[256,8,8,128]{3,0,2,1:T(8,128)} copy(f32[256,8,8,128]{0,3,2,1:T(8,128)} %bitcast.154) | data formatting | bytes 16777216 | tf_op jit(solution)/shard_map/while/body/eval_jaxpr/reshape | solution.py:64
  211.1 1.0 constant_dynamic-slice_fusion.8
  212.1 4.7 fusion.47
  216.8 0.8 copy.42
  217.6 0.0 reduce-scatter.10.cloned.1.call-update
  217.6 0.0 reduce-scatter.6.cloned.1.call-start
  217.7 1.3 copy.34
  219.0 0.0 reduce-scatter.6.cloned.1.call-update
  219.0 0.0 reduce-scatter.8.cloned.1.call-start
  219.1 64.7 %reduce-scatter.10.cloned.1.call-done = f32[16,8]{1,0:T(8,128)} async-done(((f32[256,8]{1,0:T(8,128)}), f32[16,8]{1,0:T(8,128)}) %reduce-scatter.10.cloned.1.call-update) | async-done | bytes 528 | tf_op jit(solution)/shard_map/div | solution.py:104
  283.8 72.6 %reduce-scatter.6.cloned.1.call-done = f32[16,1,8,128]{3,2,1,0:T(8,128)} async-done(((f32[256,1,8,128]{3,2,1,0:T(8,128)}), f32[16,1,8,128]{3,2,1,0:T(8,128)}) %reduce-scatter.6.cloned.1.call-update) | async-done | bytes 65552 | tf_op jit(solution)/shard_map/reduce_scatter | solution.py:101
  356.3 0.9 divide_convert_fusion
  357.3 36.2 %all_gather.11 = bf16[256,1024]{1,0:T(8,128)(2,1)S(1)} all-gather(bf16[16,1024]{1,0:T(8,128)(2,1)S(1)} %bitcast.166), channel_id=1, replica_groups=mesh['seq'=16,'head'=8,'rows'=2] {'seq'}, dimensions={0}, use_global_device_ids=true | all-gather | bytes 557056 | tf_op jit(solution)/shard_map/all_gather | solution.py:109
  393.5 0.0 copy-done
  393.5 1.2 fusion.33
  394.7 0.0 reduce-scatter.8.cloned.1.call-update
  394.8 76.1 %reduce-scatter.8.cloned.1.call-done = f32[32,512]{1,0:T(8,128)} async-done(((f32[256,512]{1,0:T(8,128)}), f32[32,512]{1,0:T(8,128)}) %reduce-scatter.8.cloned.1.call-update) | async-done | bytes 65552 | tf_op jit(solution)/shard_map/reduce_scatter | solution.py:113
  (22 shorter events, 0.1 us)
Async XLA Ops:
  6.5 386.9 %copy-start = (bf16[1024,512]{1,0:T(8,128)(2,1)S(1)}, bf16[1024,512]{1,0:T(8,128)(2,1)}, u32[]{:S(2)}) copy-start(bf16[1024,512]{1,0:T(8,128)(2,1)} %param.21) | copy-start | bytes 3145732
  6.5 277.2 %reduce-scatter.10.cloned.1.call-start = ((), (), s32[]{:S(2)}) async-start(), calls=%async_computation.5 | async-start | bytes 139264 | tf_op jit(solution)/shard_map/div | solution.py:104
  114.6 9.1 %copy-start.1 = (bf16[16,128,1,128]{3,1,2,0:T(8,128)(2,1)S(1)}, bf16[16,128,1,128]{3,1,2,0:T(8,128)(2,1)}, u32[]{:S(2)}) copy-start(bf16[16,128,1,128]{3,1,2,0:T(8,128)(2,1)} %param.18) | copy-start | bytes 1572868
  217.6 138.7 %reduce-scatter.6.cloned.1.call-start = ((), (), s32[]{:S(2)}) async-start(), calls=%async_computation.3 | async-start | bytes 1114112 | tf_op jit(solution)/shard_map/reduce_scatter | solution.py:101
  219.0 251.8 %reduce-scatter.8.cloned.1.call-start = ((), (), s32[]{:S(2)}) async-start(), calls=%async_computation.4 | async-start | bytes 589824 | tf_op jit(solution)/shard_map/reduce_scatter | solution.py:113
Sparse Core Ops, SparseCore 0:
  217.7 65.9 reduce-scatter.9
  286.4 69.8 reduce-scatter.5
  394.9 75.9 reduce-scatter.7
where the time goes:
time: 479 us; the launch traced here: 477 us
  waiting for transfers between devices  213 us (44%)
  blocking collectives  121 us (25%)
  matrix products  70.8 us (15%)
  local copies, waits for them, and re-layouts  47 us (10%)
  between operations  13.9 us (3%)
  other arithmetic  11.1 us (2%)
    reduce_scatter x1, waiting for transfers between devices, per_device(): lax.psum_scatter(partial_value, 'head', scatter_dimension=0, tiled=True)  76.1 us
    reduce_scatter x1, waiting for transfers between devices, per_device(): lax.psum_scatter(accum, 'seq', scatter_dimension=0, tiled=True)  72.6 us
    div x1, waiting for transfers between devices, per_device(): accum_own / total_own[..., None]  64.7 us
    reshape x4, local copies, waits for them, and re-layouts, doc_scores(): scores = scores.reshape(count, kv_heads, group, per_span, BLK)  36.5 us
    all_gather x1, blocking collectives, per_device(): lax.all_gather(attended, 'seq', axis=0, tiled=True)  36.2 us
    dot_general x8, matrix products, doc_scores(): jnp.einsum('nkgd,tkd->nkgt', grouped, keys, preferred_element_type=jnp.fl...  34.7 us
    pmax x1, blocking collectives, per_device(): peak = lax.pmax(local_peak, 'seq')  32.9 us
    all_gather x1, blocking collectives, per_device(): lax.all_gather(queries, 'seq', axis=0, tiled=True)  32.7 us
  transfers between devices with their start and end apart: 3, of which 3 were waited for; matrix products, arithmetic and copies ran while one was open for 0% of the time, Pallas kernels for 0%

commit v1 on v0

v1 whole, which is shorter than its diff:
```python
import functools
import math

import jax
import jax.numpy as jnp
from jax import lax
from jax.experimental import pallas as pl
from jax.experimental.pallas import tpu as pltpu
from jax.sharding import PartitionSpec as P

BLK = 128
ADAPTERS = 64
PATCHES = 4
HD = 128
RATE = math.log2(math.e) / math.sqrt(HD)
HIDDEN = -1e30
TAIL = 16
SPAN = 512
VMEM = 24 * 2**20


def pack(query_ref, adapter_ref, out_ref):
    rows, heads, width = query_ref.shape
    query = query_ref[...].astype(jnp.float32)
    line = lax.broadcasted_iota(jnp.int32, (rows, width), 0)
    lane = lax.broadcasted_iota(jnp.int32, (rows, width), 1)
    onehot = jnp.zeros((rows, width), jnp.float32)
    for r in range(rows):
        onehot = jnp.where((line == r) & (lane == adapter_ref[r]), 1.0, onehot)
    lines = [query[:, h, :] for h in range(heads)] + [onehot]
    message = jnp.concatenate(lines, 0).astype(jnp.bfloat16)
    for i in range(out_ref.shape[0]):
        out_ref[i] = message


def store_part(out_ref, i, mean, logsum):
    lines = mean.shape[0]
    line = lax.broadcasted_iota(jnp.int32, (TAIL, lines), 0)
    out_ref[i, :lines, :] = mean.astype(jnp.bfloat16)
    flat = jnp.transpose(logsum)[:TAIL, :]
    first = flat.astype(jnp.bfloat16).astype(jnp.float32)
    second = (flat - first).astype(jnp.bfloat16).astype(jnp.float32)
    third = flat - first - second
    tail = jnp.where(
        line == 0, first, jnp.where(line == 1, second, jnp.where(line == 2, third, 0.0))
    )
    out_ref[i, lines:, :] = tail.astype(jnp.bfloat16)


def local_attention(msg_ref, keys_ref, values_ref):
    count = msg_ref.shape[0]
    lines = msg_ref.shape[1] - TAIL
    heads = lines // TAIL
    tokens = keys_ref.shape[0]
    parts = []
    for i in range(count):
        onehot = msg_ref[i, lines:, :]
        parts.append(
            jnp.concatenate(
                [msg_ref[i, :lines, :], jnp.concatenate([onehot] * heads, 0)], 1
            )
        )
    query = jnp.concatenate(parts, 0)
    peak = accum = None
    for start in range(0, tokens, SPAN):
        scores = lax.dot_general(
            query,
            keys_ref[start : start + SPAN, :],
            (((1,), (1,)), ((), ())),
            preferred_element_type=jnp.float32,
        )
        top = jnp.max(scores, axis=1, keepdims=True)
        if accum is not None:
            top = jnp.maximum(peak, top)
        weights = jnp.exp2((scores - top) * RATE).astype(jnp.bfloat16)
        added = jnp.dot(
            weights, values_ref[start : start + SPAN, :], preferred_element_type=jnp.float32
        )
        accum = added if accum is None else accum * jnp.exp2((peak - top) * RATE) + added
        peak = top
    total = accum[:, HD:]
    mean = accum[:, :HD] / total
    return mean, peak * RATE + jnp.log2(total)


def attend_sent(msg_ref, keys_ref, values_ref, out_ref):
    mean, logsum = local_attention(msg_ref, keys_ref, values_ref)
    lines = msg_ref.shape[1] - TAIL
    for i in range(msg_ref.shape[0]):
        store_part(
            out_ref, i, mean[i * lines : (i + 1) * lines], logsum[i * lines : (i + 1) * lines]
        )


def attend_kept(msg_ref, keys_ref, values_ref, mean_ref, logsum_ref):
    mean, logsum = local_attention(msg_ref, keys_ref, values_ref)
    lines = msg_ref.shape[1] - TAIL
    for i in range(msg_ref.shape[0]):
        mean_ref[i] = mean[i * lines : (i + 1) * lines]
        logsum_ref[i] = logsum[i * lines : (i + 1) * lines]


def columns(flat, lines):
    count = flat.shape[0]
    return jnp.transpose(
        jnp.concatenate([flat, jnp.zeros((lines - count, lines), jnp.float32)], 0)
    )


def merge(mean_ref, logsum_ref, two_ref, out_ref):
    count = two_ref.shape[0]
    lines = two_ref.shape[1] - TAIL
    others = columns(jnp.sum(two_ref[:, lines:, :].astype(jnp.float32), axis=1), lines)
    for i in range(count):
        one, two = logsum_ref[i], others[:, i : i + 1]
        top = jnp.maximum(one, two)
        first, second = jnp.exp2(one - top), jnp.exp2(two - top)
        both = first + second
        mean = (mean_ref[i] * first + two_ref[i, :lines, :].astype(jnp.float32) * second) / both
        store_part(out_ref, i, mean, top + jnp.log2(both))


def combine(parts_ref, out_ref):
    count = parts_ref.shape[0]
    lines = parts_ref.shape[1] - TAIL
    heads = lines // TAIL
    logsum = jnp.sum(parts_ref[:, lines:, :].astype(jnp.float32), axis=1)
    share = jnp.exp2(logsum - jnp.max(logsum, axis=0, keepdims=True))
    share = columns(share / jnp.sum(share, axis=0, keepdims=True), lines)
    mixed = None
    for i in range(count):
        term = parts_ref[i, :lines, :].astype(jnp.float32) * share[:, i : i + 1]
        mixed = term if mixed is None else mixed + term
    attended = mixed.astype(jnp.bfloat16)
    wide = jnp.concatenate([attended[h * TAIL : (h + 1) * TAIL] for h in range(heads)], 1)
    for i in range(out_ref.shape[0]):
        out_ref[i] = wide


def project(side_ref, rows_ref, own_ref, other_ref, out_ref):
    side = side_ref[0]
    count, own = rows_ref.shape[0], rows_ref.shape[1]
    rows = jnp.concatenate([rows_ref[i] for i in range(count)], 0)
    for weight_ref, place in ((own_ref, 1 - side), (other_ref, side)):
        product = jnp.dot(rows, weight_ref[...], preferred_element_type=jnp.float32)
        product = product.astype(jnp.bfloat16)
        for i in range(count):
            out_ref[i, place] = product[i * own : (i + 1) * own]


def per_device(
    queries,
    row_adapter,
    doc_keys,
    doc_values,
    patch_keys,
    patch_values,
    patch_block,
    patch_slot,
    out_weight,
):
    seqs = lax.axis_size("seq")
    groups = lax.axis_size("head")
    pairs = seqs // 2
    own, heads, width = queries.shape
    lines = own * heads
    seq_index = lax.axis_index("seq")
    side = lax.rem(seq_index, 2)
    adapter_ids = jnp.arange(HD, dtype=jnp.int32)
    levels = [[2 * level + at for level in range(pairs)] for at in range(2)]
    corners = [
        [head * seqs + 2 * level + at for head in range(groups) for at in (1, 0)]
        for level in range(pairs)
    ]

    def partner(array):
        return lax.ppermute(array, "seq", [(i, i ^ 1) for i in range(seqs)])

    def along_levels(array):
        return lax.all_to_all(array, "seq", 0, 0, tiled=True, axis_index_groups=levels)

    vmem = pltpu.CompilerParams(vmem_limit_bytes=VMEM)
    small = pltpu.CompilerParams(vmem_limit_bytes=16 * 2**20)
    part_shape = jax.ShapeDtypeStruct((pairs, lines + TAIL, width), jnp.bfloat16)

    message = pl.pallas_call(
        pack,
        in_specs=[
            pl.BlockSpec(memory_space=pltpu.VMEM),
            pl.BlockSpec(memory_space=pltpu.SMEM),
        ],
        out_shape=part_shape,
        compiler_params=small,
        name="pack",
    )(queries, row_adapter)
    with jax.named_scope("gather_queries"):
        near = along_levels(message)
        far = partner(near)
    with jax.named_scope("local_tokens"):
        doc_len = doc_keys.shape[0]
        blocks_here = doc_len // BLK
        slots_here = patch_keys.shape[0]
        block_ids = seq_index * blocks_here + jnp.arange(blocks_here, dtype=jnp.int32)
        replaced = jnp.pad(
            patch_block.reshape(ADAPTERS, PATCHES),
            ((0, HD - ADAPTERS), (0, 0)),
            constant_values=-1,
        )
        hides = jnp.any(block_ids[:, None, None] == replaced[None, :, :], axis=2)
        slot_ids = seq_index * slots_here + jnp.arange(slots_here, dtype=jnp.int32)
        entry_owner = jnp.arange(patch_slot.shape[0], dtype=jnp.int32) // PATCHES
        slot_adapter = jnp.sum(
            jnp.where(slot_ids[:, None] == patch_slot[None, :], entry_owner[None, :], 0), axis=1
        )
        hides = jnp.concatenate([hides, slot_adapter[:, None] != adapter_ids[None, :]], 0)
        bars = jnp.where(hides, HIDDEN, 0.0).astype(jnp.bfloat16)
        bars = jnp.broadcast_to(bars[:, None, :], (blocks_here + slots_here, BLK, HD))
        tokens = doc_len + slots_here * BLK
        keys = jnp.concatenate(
            [doc_keys.reshape(doc_len, width), patch_keys.reshape(slots_here * BLK, width)], 0
        )
        keys = jnp.concatenate([keys, bars.reshape(tokens, HD)], 1)
        values = jnp.concatenate(
            [doc_values.reshape(doc_len, width), patch_values.reshape(slots_here * BLK, width)], 0
        )
        values = jnp.concatenate([values, jnp.ones((tokens, HD), jnp.bfloat16)], 1)

    kept_shape = jax.ShapeDtypeStruct((pairs, lines, width), jnp.float32)

    def attend_lines(body, out_shape):
        return pl.pallas_call(
            body,
            out_shape=out_shape,
            compiler_params=vmem,
            cost_estimate=pl.CostEstimate(
                flops=8 * pairs * lines * tokens * HD,
                bytes_accessed=8 * tokens * HD + 4 * pairs * lines * width,
                transcendentals=pairs * lines * tokens,
            ),
            name=body.__name__,
        )

    near_part = attend_lines(attend_sent, part_shape)(near, keys, values)
    with jax.named_scope("swap_parts"):
        far_part = partner(near_part)
    mean, logsum = attend_lines(attend_kept, (kept_shape, kept_shape))(far, keys, values)
    merged = pl.pallas_call(merge, out_shape=part_shape, compiler_params=small, name="merge")(
        mean, logsum, far_part
    )
    late_weight, merged = lax.optimization_barrier((out_weight, merged))
    other_weight = partner(late_weight)
    with jax.named_scope("scatter_rows"):
        parts = along_levels(merged)
    copies = pl.pallas_call(
        combine,
        out_shape=jax.ShapeDtypeStruct((pairs, own, heads * width), jnp.bfloat16),
        compiler_params=small,
        name="combine",
    )(parts)
    with jax.named_scope("gather_attended"):
        attended = along_levels(copies)
    in_vmem = pl.BlockSpec(memory_space=pltpu.VMEM)
    products = pl.pallas_call(
        project,
        in_specs=[pl.BlockSpec(memory_space=pltpu.SMEM), in_vmem, in_vmem, in_vmem],
        out_shape=jax.ShapeDtypeStruct((pairs, 2, own, out_weight.shape[1]), jnp.bfloat16),
        compiler_params=small,
        name="project",
    )(side.reshape(1), attended, out_weight, other_weight)
    with jax.named_scope("sum_heads"):
        shares = lax.all_to_all(
            products.reshape(2 * pairs, own, out_weight.shape[1]),
            ("head", "seq"),
            0,
            0,
            tiled=True,
            axis_index_groups=corners,
        )
        shares = shares.reshape(groups, 2 * own, out_weight.shape[1])
        return jnp.sum(shares.astype(jnp.float32), axis=0)


def solution(mesh):
    placed = (
        P(("rows", "seq"), "head", None),
        P(("rows", "seq")),
        P("seq", "head", None),
        P("seq", "head", None),
        P("seq", None, "head", None),
        P("seq", None, "head", None),
        P(),
        P(),
        P("head", "seq"),
    )
    return jax.shard_map(
        per_device,
        mesh=mesh,
        in_specs=placed,
        out_specs=P(("rows", "head"), "seq"),
        check_vma=False,
    )
```

time: 479 us -> 89.9 us (0.19)
  waiting for transfers between devices: 213 us -> 16.4 us
  blocking collectives: 121 us -> 27.8 us
  matrix products: 70.8 us -> 0 us
  local copies, waits for them, and re-layouts: 47 us -> 4.37 us
  Pallas kernels: 0 us -> 19.9 us
  starting transfers between devices: 0.09 us -> 14.7 us
  between operations: 13.9 us -> 0.11 us
  other arithmetic: 11.1 us -> 6.15 us
    reduce_scatter x2 -> x0, waiting for transfers between devices: 149 us -> none  [the longest x1 76.1 us: per_device(): lax.psum_scatter(partial_value, 'head', scatter_dimension=0, tiled=True)]
    dot_general x16 -> x0, matrix products: 70.8 us -> none  [the longest x8 34.7 us: doc_scores(): jnp.einsum('nkgd,tkd->nkgt', grouped, keys, preferred_element_type=jnp.fl...]
    all_gather x2 -> x0, blocking collectives: 68.9 us -> none  [the longest x1 36.2 us: per_device(): lax.all_gather(attended, 'seq', axis=0, tiled=True)]
    div x1 -> x0, waiting for transfers between devices: 64.7 us -> none  [per_device(): accum_own / total_own[..., None]]
    reshape x5 -> x1, local copies, waits for them, and re-layouts: 37.3 us -> 0.78 us  [per_device(): patch_block.reshape(ADAPTERS, PATCHES)]
    pmax x1 -> x0, blocking collectives: 32.9 us -> none  [per_device(): peak = lax.pmax(local_peak, 'seq')]
    all_to_all x0 -> x2, blocking collectives: none -> 27.8 us  [the longest x1 14.6 us: per_device(): lax.all_to_all(products.reshape(2 * pairs, own, out_weight.shape[1]), ('h...]
    pallas_call x0 -> x6, Pallas kernels: none -> 19.9 us  [the longest x1 7.71 us: per_device(): near_part = attend_lines(attend_sent, part_shape)(near, keys, values)]
  transfers between devices with their start and end apart: 3 -> 5, of which waited for: 3 -> 2; matrix products, arithmetic and copies ran while one was open for 0% -> 7% of each run, Pallas kernels for 0% -> 18%
where the time goes in v1:
time: 89.9 us; the launch traced here: 89.3 us
  blocking collectives  27.8 us (31%)
  Pallas kernels  19.9 us (22%)
  waiting for transfers between devices  16.4 us (18%)
  starting transfers between devices  14.7 us (16%)
  other arithmetic  6.15 us (7%)
  local copies, waits for them, and re-layouts  4.37 us (5%)
    all_to_all x2, waiting for transfers between devices, along_levels(): lax.all_to_all(array, 'seq', 0, 0, tiled=True, axis_index_groups=levels)  16.4 us
    all_to_all x1, blocking collectives, per_device(): lax.all_to_all(products.reshape(2 * pairs, own, out_weight.shape[1]), ('h...  14.6 us
    all_to_all x1, blocking collectives, along_levels(): lax.all_to_all(array, 'seq', 0, 0, tiled=True, axis_index_groups=levels)  13.2 us
    all_to_all x2, starting transfers between devices, along_levels(): lax.all_to_all(array, 'seq', 0, 0, tiled=True, axis_index_groups=levels)  11.9 us
    pallas_call x1, Pallas kernels, per_device(): near_part = attend_lines(attend_sent, part_shape)(near, keys, values)  7.71 us
    pallas_call x1, Pallas kernels, per_device(): attend_lines(attend_kept, (kept_shape, kept_shape))(far, keys, values)  7.65 us
    concatenate x1, other arithmetic, per_device(): jnp.concatenate([doc_values.reshape(doc_len, width), patch_values.reshape...  4.44 us
    unnamed x9, local copies, waits for them, and re-layouts  3.38 us
  transfers between devices with their start and end apart: 5, of which 2 were waited for; matrix products, arithmetic and copies ran while one was open for 7% of the time, Pallas kernels for 18%

profile of v1, /device:TPU:8, one launch (start us, length us, event | category | flops | bytes accessed | tf_op | source)
XLA Modules:
  0.0 89.3 jit_solution(8097658743645430236)
XLA Ops:
  0.0 0.0 copy-start.2
  0.0 0.8 copy-done.2
  0.8 0.0 copy-start.3
  0.8 0.7 copy-done.3
  1.4 1.3 %pack.1 = bf16[8,144,128]{2,1,0:T(8,128)(2,1)} custom-call(bf16[16,8,128]{2,1,0:T(8,128)(2,1)S(1)} %copy-done.2, s32[16]{0:T(128)S(1)} %copy-done.3), custom_call_target="tpu_custom_call" | custom-call | tf_op jit(solution)/shard_map/pack/pallas_call | solution.py:186
  2.7 8.5 %all-to-all-start = ((bf16[8,144,128]{2,1,0:T(8,128)(2,1)}), bf16[8,144,128]{2,1,0:T(8,128)(2,1)S(1)}, u32[]{:S(2)}, u32[]{:S(2)}) async-start(bf16[8,144,128]{2,1,0:T(8,128)(2,1)} %pack.1), calls=%async_computation | async-start | bytes 589824 | tf_op jit(solution)/shard_map/gather_queries/all_to_all | solution.py:180
  11.2 0.8 reshape.74
  12.0 0.1 copy.11
  12.1 0.9 select_reduce_fusion
  12.9 0.1 iota_compare_fusion.1
  13.0 0.1 compare_reduce_fusion
  13.1 0.2 broadcast_in_dim.38
  13.3 4.4 %fusion.2 = (bf16[6144,256]{1,0:T(8,128)(2,1)S(1)}, bf16[6144,256]{1,0:T(8,128)(2,1)}) fusion(bf16[2048,128]{1,0:T(8,128)(2,1)} %bitcast.16, bf16[4096,128]{1,0:T(8,128)(2,1)} %bitcast.14, bf16[6144,128]{1,0:T(8,128)(2,1)S(1)} %bitcast.12, bf16[2048,128]{1,0:T(8,128)(2,1)} %bitcast.17, bf16[4096,128]{1,0:T(8,128)(2,1)} %bitcast.15), kind=kLoop, calls=%fused_computation.3 | loop fusion | flops 20447232 | bytes 11010048 | tf_op jit(solution)/shard_map/local_tokens/concatenate | solution.py:223
  17.8 6.0 %all-to-all-done.msg_ref = bf16[8,144,128]{2,1,0:T(8,128)(2,1)S(1)} async-done(((bf16[8,144,128]{2,1,0:T(8,128)(2,1)}), bf16[8,144,128]{2,1,0:T(8,128)(2,1)S(1)}, u32[]{:S(2)}, u32[]{:S(2)}) %all-to-all-start) | async-done | bytes 294944 | tf_op jit(solution)/shard_map/gather_queries/all_to_all | solution.py:180
  23.8 0.4 collective-permute-start
  24.2 0.0 copy-start
  24.2 1.9 %copy-done = bf16[6144,256]{1,0:T(8,128)(2,1)S(1)} copy-done((bf16[6144,256]{1,0:T(8,128)(2,1)S(1)}, bf16[6144,256]{1,0:T(8,128)(2,1)}, u32[]{:S(2)}) %copy-start) | copy-done | bytes 3145752
  26.1 0.0 copy-start.1
  26.1 7.7 %attend_sent.1 = bf16[8,144,128]{2,1,0:T(8,128)(2,1)S(1)} custom-call(bf16[8,144,128]{2,1,0:T(8,128)(2,1)S(1)} %all-to-all-done.msg_ref, bf16[6144,256]{1,0:T(8,128)(2,1)S(1)} %copy-done, bf16[6144,256]{1,0:T(8,128)(2,1)S(1)} %get-tuple-element.13.values_ref), custom_call_target="tpu_custom_call" | custom-call | flops 6442450944 | bytes 6815744 | tf_op jit(solution)/shard_map/attend_sent/pallas_call | solution.py:243
  33.8 1.8 %collective-permute-start.1 = (bf16[8,144,128]{2,1,0:T(8,128)(2,1)S(1)}, bf16[8,144,128]{2,1,0:T(8,128)(2,1)S(1)}, u32[]{:S(2)}, u32[]{:S(2)}) collective-permute-start(bf16[8,144,128]{2,1,0:T(8,128)(2,1)S(1)} %attend_sent.1), channel_id=1, source_target_pairs={{0,16},{16,0},{32,48},{48,32},{64,80},{80,64},{96,112},{112,96},{1... | collective-permute-start | bytes 884744 | tf_op jit(solution)/shard_map/swap_parts/ppermute | solution.py:177
  35.6 0.0 collective-permute-done.msg_ref
  35.6 0.0 copy-done.1
  35.6 7.6 %attend_kept.1 = (f32[8,128,128]{2,1,0:T(8,128)S(1)}, f32[8,128,128]{2,1,0:T(8,128)S(1)}) custom-call(bf16[8,144,128]{2,1,0:T(8,128)(2,1)S(1)} %collective-permute-done.msg_ref, bf16[6144,256]{1,0:T(8,128)(2,1)S(1)} %copy-done.1, bf16[6144,256]{1,0:T(8,128)(2,1)S(1)} %get-tuple-element.13.values_ref), custom_call_target="tpu_custom_call" | custom-call | flops 6442450944 | bytes 6815744 | tf_op jit(solution)/shard_map/attend_kept/pallas_call | solution.py:246
  43.3 0.0 collective-permute-done.1.two_ref
  43.3 0.5 merge.1
  43.8 0.5 collective-permute-start.2
  44.3 13.2 %all_to_all.20.parts_ref = bf16[8,144,128]{2,1,0:T(8,128)(2,1)S(1)} all-to-all(bf16[8,144,128]{2,1,0:T(8,128)(2,1)S(1)} %merge.1), channel_id=1, replica_groups={{0,32,64,96,128,160,192,224},{16,48,80,112,144,176,208,240},{1,33,65,97..., dimensions={0} | all-to-all | bytes 589824 | tf_op jit(solution)/shard_map/scatter_rows/all_to_all | solution.py:180
  57.5 1.1 %combine.1 = bf16[8,16,1024]{2,1,0:T(8,128)(2,1)} custom-call(bf16[8,144,128]{2,1,0:T(8,128)(2,1)S(1)} %all_to_all.20.parts_ref), custom_call_target="tpu_custom_call" | custom-call | tf_op jit(solution)/shard_map/combine/pallas_call | solution.py:254
  58.6 3.4 %all-to-all-start.2 = ((bf16[8,16,1024]{2,1,0:T(8,128)(2,1)}), bf16[8,16,1024]{2,1,0:T(8,128)(2,1)S(1)}, u32[]{:S(2)}, u32[]{:S(2)}) async-start(bf16[8,16,1024]{2,1,0:T(8,128)(2,1)} %combine.1), calls=%async_computation.2 | async-start | bytes 524288 | tf_op jit(solution)/shard_map/gather_attended/all_to_all | solution.py:180
  62.0 10.4 %all-to-all-done.2.rows_ref = bf16[8,16,1024]{2,1,0:T(8,128)(2,1)S(1)} async-done(((bf16[8,16,1024]{2,1,0:T(8,128)(2,1)}), bf16[8,16,1024]{2,1,0:T(8,128)(2,1)S(1)}, u32[]{:S(2)}, u32[]{:S(2)}) %all-to-all-start.2) | async-done | bytes 262176 | tf_op jit(solution)/shard_map/gather_attended/all_to_all | solution.py:180
  72.4 0.0 collective-permute-done.2.other_ref
  72.4 1.7 %project.1 = bf16[8,2,16,512]{3,2,1,0:T(8,128)(2,1)S(1)} custom-call(s32[1]{0:T(128)} %bitcast.side_ref, bf16[8,16,1024]{2,1,0:T(8,128)(2,1)S(1)} %all-to-all-done.2.rows_ref, bf16[1024,512]{1,0:T(8,128)(2,1)} %own_ref.1, bf16[1024,512]{1,0:T(8,128)(2,1)S(1)} %collective-permute-done.2.other_ref), custom_call_target="tpu_custom_call" | custom-call | tf_op jit(solution)/shard_map/project/pallas_call | solution.py:263
  74.1 14.6 %all_to_all.21 = bf16[16,16,512]{2,1,0:T(8,128)(2,1)S(1)} all-to-all(bf16[16,16,512]{2,1,0:T(8,128)(2,1)S(1)} %bitcast.11), channel_id=1, replica_groups={{16,0,18,2,20,4,22,6,24,8,26,10,28,12,30,14},{48,32,50,34,52,36,54,38,5..., dimensions={0} | all-to-all | bytes 524288 | tf_op jit(solution)/shard_map/sum_heads/all_to_all | solution.py:271
  88.6 0.7 convert_reduce_fusion
  (5 shorter events, 0.0 us)
Async XLA Ops:
  0.0 0.8 copy-start.2
  0.8 0.7 copy-start.3
  2.7 21.0 %all-to-all-start = ((bf16[8,144,128]{2,1,0:T(8,128)(2,1)}), bf16[8,144,128]{2,1,0:T(8,128)(2,1)S(1)}, u32[]{:S(2)}, u32[]{:S(2)}) async-start(bf16[8,144,128]{2,1,0:T(8,128)(2,1)} %pack.1), calls=%async_computation | async-start | bytes 589824 | tf_op jit(solution)/shard_map/gather_queries/all_to_all | solution.py:180
  23.8 11.9 %collective-permute-start = (bf16[8,144,128]{2,1,0:T(8,128)(2,1)S(1)}, bf16[8,144,128]{2,1,0:T(8,128)(2,1)S(1)}, u32[]{:S(2)}, u32[]{:S(2)}) collective-permute-start(bf16[8,144,128]{2,1,0:T(8,128)(2,1)S(1)} %all-to-all-done.msg_ref), channel_id=1, source_target_pairs={{0,16},{16,0},{32,48},{48,32},{64,80},{80,64},{96,112},{112,96},{1... | collective-permute-start | bytes 884744 | tf_op jit(solution)/shard_map/gather_queries/ppermute | solution.py:177
  24.2 1.9 %copy-start = (bf16[6144,256]{1,0:T(8,128)(2,1)S(1)}, bf16[6144,256]{1,0:T(8,128)(2,1)}, u32[]{:S(2)}) copy-start(bf16[6144,256]{1,0:T(8,128)(2,1)} %get-tuple-element.14.keys_ref) | copy-start | bytes 9437188
  26.1 9.5 %copy-start.1 = (bf16[6144,256]{1,0:T(8,128)(2,1)S(1)}, bf16[6144,256]{1,0:T(8,128)(2,1)}, u32[]{:S(2)}) copy-start(bf16[6144,256]{1,0:T(8,128)(2,1)} %get-tuple-element.14.keys_ref) | copy-start | bytes 9437188
  33.8 9.5 %collective-permute-start.1 = (bf16[8,144,128]{2,1,0:T(8,128)(2,1)S(1)}, bf16[8,144,128]{2,1,0:T(8,128)(2,1)S(1)}, u32[]{:S(2)}, u32[]{:S(2)}) collective-permute-start(bf16[8,144,128]{2,1,0:T(8,128)(2,1)S(1)} %attend_sent.1), channel_id=1, source_target_pairs={{0,16},{16,0},{32,48},{48,32},{64,80},{80,64},{96,112},{112,96},{1... | collective-permute-start | bytes 884744 | tf_op jit(solution)/shard_map/swap_parts/ppermute | solution.py:177
  43.8 28.6 %collective-permute-start.2 = (bf16[1024,512]{1,0:T(8,128)(2,1)}, bf16[1024,512]{1,0:T(8,128)(2,1)S(1)}, u32[]{:S(2)}, u32[]{:S(2)}) collective-permute-start(bf16[1024,512]{1,0:T(8,128)(2,1)} %own_ref.1), channel_id=1, source_target_pairs={{0,16},{16,0},{32,48},{48,32},{64,80},{80,64},{96,112},{112,96},{1... | collective-permute-start | bytes 3145736 | tf_op jit(solution)/shard_map/ppermute | solution.py:177
  58.6 13.8 %all-to-all-start.2 = ((bf16[8,16,1024]{2,1,0:T(8,128)(2,1)}), bf16[8,16,1024]{2,1,0:T(8,128)(2,1)S(1)}, u32[]{:S(2)}, u32[]{:S(2)}) async-start(bf16[8,16,1024]{2,1,0:T(8,128)(2,1)} %combine.1), calls=%async_computation.2 | async-start | bytes 524288 | tf_op jit(solution)/shard_map/gather_attended/all_to_all | solution.py:180

commit v2 on v1

--- a/solution.py
+++ b/solution.py
@@ -33,11 +33,38 @@
         out_ref[i] = message
 
 
+def bar(slots, seq_ref, block_ref, slot_ref, *refs):
+    out_ref = refs[-1]
+    entries = block_ref.shape[1]
+    blocks = out_ref.shape[0] // TAIL - slots
+    line = lax.broadcasted_iota(jnp.int32, (blocks + slots, entries), 0)
+    named = jnp.where(
+        line < blocks,
+        jnp.broadcast_to(block_ref[...], line.shape) - seq_ref[0] * blocks,
+        jnp.broadcast_to(slot_ref[...], line.shape) - seq_ref[0] * slots + blocks,
+    )
+    entry = lax.broadcasted_iota(jnp.int32, (entries, HD), 0)
+    adapter = lax.broadcasted_iota(jnp.int32, (entries, HD), 1)
+    owns = jnp.where(entry // PATCHES == adapter, 1.0, 0.0).astype(jnp.bfloat16)
+    hits = jnp.dot(
+        jnp.where(named == line, 1.0, 0.0).astype(jnp.bfloat16),
+        owns,
+        preferred_element_type=jnp.float32,
+    )
+    is_block = lax.broadcasted_iota(jnp.int32, hits.shape, 0) < blocks
+    hidden = jnp.where(is_block, hits, 1.0 - hits) > 0.5
+    bars = jnp.where(hidden, HIDDEN, 0.0)
+    for i in range(blocks + slots):
+        out_ref[i * TAIL : (i + 1) * TAIL, :] = jnp.broadcast_to(
+            bars[i : i + 1, :], (TAIL, HD)
+        ).astype(jnp.bfloat16)
+
+
 def store_part(out_ref, i, mean, logsum):
     lines = mean.shape[0]
     line = lax.broadcasted_iota(jnp.int32, (TAIL, lines), 0)
     out_ref[i, :lines, :] = mean.astype(jnp.bfloat16)
-    flat = jnp.transpose(logsum)[:TAIL, :]
+    flat = logsum
     first = flat.astype(jnp.bfloat16).astype(jnp.float32)
     second = (flat - first).astype(jnp.bfloat16).astype(jnp.float32)
     third = flat - first - second
@@ -47,11 +74,10 @@
     out_ref[i, lines:, :] = tail.astype(jnp.bfloat16)
 
 
-def local_attention(msg_ref, keys_ref, values_ref):
+def local_attention(msg_ref, doc_ref, patch_ref, doc_values_ref, patch_values_ref, bars_ref):
     count = msg_ref.shape[0]
     lines = msg_ref.shape[1] - TAIL
     heads = lines // TAIL
-    tokens = keys_ref.shape[0]
     parts = []
     for i in range(count):
         onehot = msg_ref[i, lines:, :]
@@ -61,43 +87,54 @@
             )
         )
     query = jnp.concatenate(parts, 0)
+    ones = jnp.ones((SPAN, HD), jnp.bfloat16)
     peak = accum = None
-    for start in range(0, tokens, SPAN):
-        scores = lax.dot_general(
-            query,
-            keys_ref[start : start + SPAN, :],
-            (((1,), (1,)), ((), ())),
-            preferred_element_type=jnp.float32,
-        )
-        top = jnp.max(scores, axis=1, keepdims=True)
-        if accum is not None:
-            top = jnp.maximum(peak, top)
-        weights = jnp.exp2((scores - top) * RATE).astype(jnp.bfloat16)
-        added = jnp.dot(
-            weights, values_ref[start : start + SPAN, :], preferred_element_type=jnp.float32
-        )
-        accum = added if accum is None else accum * jnp.exp2((peak - top) * RATE) + added
-        peak = top
+    bar = 0
+    for keys_ref, values_ref in ((doc_ref, doc_values_ref), (patch_ref, patch_values_ref)):
+        for start in range(0, keys_ref.shape[0], SPAN):
+            bars = []
+            for _ in range(SPAN // BLK):
+                bars += [bars_ref[bar * TAIL : (bar + 1) * TAIL, :]] * (BLK // TAIL)
+                bar += 1
+            keys = jnp.concatenate(
+                [keys_ref[start : start + SPAN, :], jnp.concatenate(bars, 0)], 1
+            )
+            values = jnp.concatenate([values_ref[start : start + SPAN, :], ones], 1)
+            scores = lax.dot_general(
+                query, keys, (((1,), (1,)), ((), ())), preferred_element_type=jnp.float32
+            )
+            top = jnp.max(scores, axis=1, keepdims=True)
+            if accum is not None:
+                top = jnp.maximum(peak, top)
+            weights = jnp.exp2((scores - top) * RATE).astype(jnp.bfloat16)
+            added = jnp.dot(weights, values, preferred_element_type=jnp.float32)
+            accum = added if accum is None else accum * jnp.exp2((peak - top) * RATE) + added
+            peak = top
     total = accum[:, HD:]
     mean = accum[:, :HD] / total
     return mean, peak * RATE + jnp.log2(total)
 
 
-def attend_sent(msg_ref, keys_ref, values_ref, out_ref):
-    mean, logsum = local_attention(msg_ref, keys_ref, values_ref)
+def attend_sent(msg_ref, *refs):
+    *local, out_ref = refs
+    mean, logsum = local_attention(msg_ref, *local)
     lines = msg_ref.shape[1] - TAIL
     for i in range(msg_ref.shape[0]):
         store_part(
-            out_ref, i, mean[i * lines : (i + 1) * lines], logsum[i * lines : (i + 1) * lines]
-        )
-
-
-def attend_kept(msg_ref, keys_ref, values_ref, mean_ref, logsum_ref):
-    mean, logsum = local_attention(msg_ref, keys_ref, values_ref)
+            out_ref,
+            i,
+            mean[i * lines : (i + 1) * lines],
+            jnp.transpose(logsum[i * lines : (i + 1) * lines])[:TAIL, :],
+        )
+
+
+def attend_kept(msg_ref, *refs):
+    *local, mean_ref, logsum_ref = refs
+    mean, logsum = local_attention(msg_ref, *local)
     lines = msg_ref.shape[1] - TAIL
     for i in range(msg_ref.shape[0]):
         mean_ref[i] = mean[i * lines : (i + 1) * lines]
-        logsum_ref[i] = logsum[i * lines : (i + 1) * lines]
+        logsum_ref[i : i + 1, :] = jnp.transpose(logsum[i * lines : (i + 1) * lines])[:1, :]
 
 
 def columns(flat, lines):
@@ -110,14 +147,19 @@
 def merge(mean_ref, logsum_ref, two_ref, out_ref):
     count = two_ref.shape[0]
     lines = two_ref.shape[1] - TAIL
-    others = columns(jnp.sum(two_ref[:, lines:, :].astype(jnp.float32), axis=1), lines)
+    one = logsum_ref[...]
+    two = jnp.sum(two_ref[:, lines:, :].astype(jnp.float32), axis=1)
+    top = jnp.maximum(one, two)
+    first, second = jnp.exp2(one - top), jnp.exp2(two - top)
+    both = first + second
+    shares = columns(jnp.concatenate([first / both, second / both], 0), lines)
+    logsum = top + jnp.log2(both)
     for i in range(count):
-        one, two = logsum_ref[i], others[:, i : i + 1]
-        top = jnp.maximum(one, two)
-        first, second = jnp.exp2(one - top), jnp.exp2(two - top)
-        both = first + second
-        mean = (mean_ref[i] * first + two_ref[i, :lines, :].astype(jnp.float32) * second) / both
-        store_part(out_ref, i, mean, top + jnp.log2(both))
+        mean = (
+            mean_ref[i] * shares[:, i : i + 1]
+            + two_ref[i, :lines, :].astype(jnp.float32) * shares[:, count + i : count + i + 1]
+        )
+        store_part(out_ref, i, mean, jnp.broadcast_to(logsum[i : i + 1, :], (TAIL, lines)))
 
 
 def combine(parts_ref, out_ref):
@@ -190,42 +232,36 @@
             pl.BlockSpec(memory_space=pltpu.SMEM),
         ],
         out_shape=part_shape,
-        compiler_params=small,
+        compiler_params=pltpu.CompilerParams(vmem_limit_bytes=60 * 2**20),
         name="pack",
     )(queries, row_adapter)
     with jax.named_scope("gather_queries"):
         near = along_levels(message)
         far = partner(near)
-    with jax.named_scope("local_tokens"):
-        doc_len = doc_keys.shape[0]
-        blocks_here = doc_len // BLK
-        slots_here = patch_keys.shape[0]
-        block_ids = seq_index * blocks_here + jnp.arange(blocks_here, dtype=jnp.int32)
-        replaced = jnp.pad(
-            patch_block.reshape(ADAPTERS, PATCHES),
-            ((0, HD - ADAPTERS), (0, 0)),
-            constant_values=-1,
-        )
-        hides = jnp.any(block_ids[:, None, None] == replaced[None, :, :], axis=2)
-        slot_ids = seq_index * slots_here + jnp.arange(slots_here, dtype=jnp.int32)
-        entry_owner = jnp.arange(patch_slot.shape[0], dtype=jnp.int32) // PATCHES
-        slot_adapter = jnp.sum(
-            jnp.where(slot_ids[:, None] == patch_slot[None, :], entry_owner[None, :], 0), axis=1
-        )
-        hides = jnp.concatenate([hides, slot_adapter[:, None] != adapter_ids[None, :]], 0)
-        bars = jnp.where(hides, HIDDEN, 0.0).astype(jnp.bfloat16)
-        bars = jnp.broadcast_to(bars[:, None, :], (blocks_here + slots_here, BLK, HD))
-        tokens = doc_len + slots_here * BLK
-        keys = jnp.concatenate(
-            [doc_keys.reshape(doc_len, width), patch_keys.reshape(slots_here * BLK, width)], 0
-        )
-        keys = jnp.concatenate([keys, bars.reshape(tokens, HD)], 1)
-        values = jnp.concatenate(
-            [doc_values.reshape(doc_len, width), patch_values.reshape(slots_here * BLK, width)], 0
-        )
-        values = jnp.concatenate([values, jnp.ones((tokens, HD), jnp.bfloat16)], 1)
-
-    kept_shape = jax.ShapeDtypeStruct((pairs, lines, width), jnp.float32)
+    doc_len = doc_keys.shape[0]
+    slots_here = patch_keys.shape[0]
+    tokens = doc_len + slots_here * BLK
+    in_vmem = pl.BlockSpec(memory_space=pltpu.VMEM)
+    in_smem = pl.BlockSpec(memory_space=pltpu.SMEM)
+    local = (
+        doc_keys.reshape(doc_len, width),
+        patch_keys.reshape(slots_here * BLK, width),
+        doc_values.reshape(doc_len, width),
+        patch_values.reshape(slots_here * BLK, width),
+    )
+    bars = pl.pallas_call(
+        functools.partial(bar, slots_here),
+        in_specs=[in_smem] + [in_vmem] * 6,
+        out_shape=jax.ShapeDtypeStruct((tokens // BLK * TAIL, HD), jnp.bfloat16),
+        compiler_params=small,
+        name="bar",
+    )(seq_index.reshape(1), patch_block.reshape(1, -1), patch_slot.reshape(1, -1), *local)
+    local += (bars,)
+
+    kept_shapes = (
+        jax.ShapeDtypeStruct((pairs, lines, width), jnp.float32),
+        jax.ShapeDtypeStruct((pairs, lines), jnp.float32),
+    )
 
     def attend_lines(body, out_shape):
         return pl.pallas_call(
@@ -240,10 +276,10 @@
             name=body.__name__,
         )
 
-    near_part = attend_lines(attend_sent, part_shape)(near, keys, values)
+    near_part = attend_lines(attend_sent, part_shape)(near, *local)
     with jax.named_scope("swap_parts"):
         far_part = partner(near_part)
-    mean, logsum = attend_lines(attend_kept, (kept_shape, kept_shape))(far, keys, values)
+    mean, logsum = attend_lines(attend_kept, kept_shapes)(far, *local)
     merged = pl.pallas_call(merge, out_shape=part_shape, compiler_params=small, name="merge")(
         mean, logsum, far_part
     )
@@ -259,10 +295,9 @@
     )(parts)
     with jax.named_scope("gather_attended"):
         attended = along_levels(copies)
-    in_vmem = pl.BlockSpec(memory_space=pltpu.VMEM)
     products = pl.pallas_call(
         project,
-        in_specs=[pl.BlockSpec(memory_space=pltpu.SMEM), in_vmem, in_vmem, in_vmem],
+        in_specs=[in_smem] + [in_vmem] * 3,
         out_shape=jax.ShapeDtypeStruct((pairs, 2, own, out_weight.shape[1]), jnp.bfloat16),
         compiler_params=small,
         name="project",

time: 89.9 us -> 87.2 us (0.970)
  other arithmetic: 6.15 us -> 0.67 us
  local copies, waits for them, and re-layouts: 4.37 us -> 6.48 us
  waiting for transfers between devices: 16.4 us -> 17.9 us
    concatenate x1 -> x0, other arithmetic: 4.44 us -> none  [per_device(): jnp.concatenate([doc_values.reshape(doc_len, width), patch_values.reshape...]
    unnamed x9 -> x26, local copies, waits for them, and re-layouts: 3.38 us -> 6.48 us
    all_to_all x2, waiting for transfers between devices: 16.4 us -> 17.9 us  [along_levels(): lax.all_to_all(array, 'seq', 0, 0, tiled=True, axis_index_groups=levels)]
    pallas_call x3 -> x4, Pallas kernels: 17 us -> 15.9 us  [the longest x1 7.67 us: per_device(): near_part = attend_lines(attend_sent, part_shape)(near, *local)]
  transfers between devices with their start and end apart: 5 -> 5, of which waited for: 2 -> 2; matrix products, arithmetic and copies ran while one was open for 7% -> 0% of each run, Pallas kernels for 18% -> 19%
where the time goes in v2:
time: 87.2 us; the launch traced here: 86.6 us
  blocking collectives  27.8 us (32%)
  Pallas kernels  19.1 us (22%)
  waiting for transfers between devices  17.9 us (21%)
  starting transfers between devices  14.6 us (17%)
  local copies, waits for them, and re-layouts  6.48 us (7%)
    all_to_all x2, waiting for transfers between devices, along_levels(): lax.all_to_all(array, 'seq', 0, 0, tiled=True, axis_index_groups=levels)  17.9 us
    all_to_all x1, blocking collectives, per_device(): lax.all_to_all(products.reshape(2 * pairs, own, out_weight.shape[1]), ('h...  14.6 us
    all_to_all x1, blocking collectives, along_levels(): lax.all_to_all(array, 'seq', 0, 0, tiled=True, axis_index_groups=levels)  13.2 us
    all_to_all x2, starting transfers between devices, along_levels(): lax.all_to_all(array, 'seq', 0, 0, tiled=True, axis_index_groups=levels)  11.9 us
    pallas_call x1, Pallas kernels, per_device(): near_part = attend_lines(attend_sent, part_shape)(near, *local)  7.67 us
    pallas_call x1, Pallas kernels, per_device(): mean, logsum = attend_lines(attend_kept, kept_shapes)(far, *local)  7.67 us
    unnamed x26, local copies, waits for them, and re-layouts  6.48 us
    ppermute x3, starting transfers between devices, partner(): return lax.ppermute(array, 'seq', [(i, i ^ 1) for i in range(seqs)])  2.73 us
  transfers between devices with their start and end apart: 5, of which 2 were waited for; matrix products, arithmetic and copies ran while one was open for 0% of the time, Pallas kernels for 19%

profile of v2, /device:TPU:8, one launch (start us, length us, event | category | flops | bytes accessed | tf_op | source)
XLA Modules:
  0.0 86.6 jit_solution(11753967647232196562)
XLA Ops:
  0.0 0.0 copy-start.5
  0.0 1.6 %pack.1 = bf16[8,144,128]{2,1,0:T(8,128)(2,1)} custom-call(bf16[16,8,128]{2,1,0:T(8,128)(2,1)} %query_ref.1, s32[16]{0:T(128)} %adapter_ref.1), custom_call_target="tpu_custom_call" | custom-call | tf_op jit(solution)/shard_map/pack/pallas_call | solution.py:228
  1.6 8.5 %all-to-all-start = ((bf16[8,144,128]{2,1,0:T(8,128)(2,1)}), bf16[8,144,128]{2,1,0:T(8,128)(2,1)S(1)}, u32[]{:S(2)}, u32[]{:S(2)}) async-start(bf16[8,144,128]{2,1,0:T(8,128)(2,1)} %pack.1), calls=%async_computation | async-start | bytes 589824 | tf_op jit(solution)/shard_map/gather_queries/all_to_all | solution.py:222
  10.1 0.0 copy-start.12
  10.1 0.0 copy-start.11
  10.1 0.0 copy-done.5
  10.1 0.7 copy-done.12
  10.7 0.0 copy-done.11
  10.7 0.0 copy-start
  10.8 1.2 %copy-done = bf16[4096,1,128]{2,0,1:T(8,128)(2,1)S(1)} copy-done((bf16[4096,1,128]{2,0,1:T(8,128)(2,1)S(1)}, bf16[4096,1,128]{2,0,1:T(8,128)(2,1)}, u32[]{:S(2)}) %copy-start) | copy-done | bytes 1048600
  12.0 0.0 copy-start.2
  12.0 1.2 %copy-done.2 = bf16[4096,1,128]{2,0,1:T(8,128)(2,1)S(1)} copy-done((bf16[4096,1,128]{2,0,1:T(8,128)(2,1)S(1)}, bf16[4096,1,128]{2,0,1:T(8,128)(2,1)}, u32[]{:S(2)}) %copy-start.2) | copy-done | bytes 1048600
  13.2 0.0 copy-start.6
  13.2 1.0 %copy-done.6 = bf16[16,128,1,128]{3,1,2,0:T(8,128)(2,1)S(1)} copy-done((bf16[16,128,1,128]{3,1,2,0:T(8,128)(2,1)S(1)}, bf16[16,128,1,128]{3,1,2,0:T(8,128)(2,1)}, u32[]{:S(2)}) %copy-start.6) | copy-done | bytes 524312
  14.2 0.0 copy-start.1
  14.2 0.0 copy-start.3
  14.2 0.0 copy-start.7
  14.2 0.2 bar.1.refs_4_
  14.4 0.0 copy-start.8
  14.4 0.7 copy-done.8
  15.1 7.6 %all-to-all-done.msg_ref = bf16[8,144,128]{2,1,0:T(8,128)(2,1)S(1)} async-done(((bf16[8,144,128]{2,1,0:T(8,128)(2,1)}), bf16[8,144,128]{2,1,0:T(8,128)(2,1)S(1)}, u32[]{:S(2)}, u32[]{:S(2)}) %all-to-all-start) | async-done | bytes 294944 | tf_op jit(solution)/shard_map/gather_queries/all_to_all | solution.py:222
  22.6 0.4 collective-permute-start
  23.1 0.0 copy-done.1
  23.1 0.0 copy-done.3
  23.1 0.0 copy-done.7
  23.1 0.0 copy-start.9
  23.1 0.9 %copy-done.9 = bf16[768,128]{1,0:T(8,128)(2,1)S(1)} copy-done((bf16[768,128]{1,0:T(8,128)(2,1)S(1)}, bf16[768,128]{1,0:T(8,128)(2,1)}, u32[]{:S(2)}) %copy-start.9) | copy-done | bytes 196632
  24.0 0.0 copy-start.10
  24.0 7.7 %attend_sent.1 = bf16[8,144,128]{2,1,0:T(8,128)(2,1)S(1)} custom-call(bf16[8,144,128]{2,1,0:T(8,128)(2,1)S(1)} %all-to-all-done.msg_ref, bf16[4096,128]{1,0:T(8,128)(2,1)S(1)} %bitcast.14, bf16[2048,128]{1,0:T(8,128)(2,1)S(1)} %bitcast.21, bf16[4096,128]{1,0:T(8,128)(2,1)S(1)} %bitcast.17, bf16[2048,128]{1,0:T(8,128)(2,1)S(1)} %bitcast.24, ...), custom_call_target="tpu_custom_call" | custom-call | flops 6442450944 | bytes 6815744 | tf_op jit(solution)/shard_map/attend_sent/pallas_call | solution.py:279
  31.7 1.8 %collective-permute-start.1 = (bf16[8,144,128]{2,1,0:T(8,128)(2,1)S(1)}, bf16[8,144,128]{2,1,0:T(8,128)(2,1)S(1)}, u32[]{:S(2)}, u32[]{:S(2)}) collective-permute-start(bf16[8,144,128]{2,1,0:T(8,128)(2,1)S(1)} %attend_sent.1), channel_id=1, source_target_pairs={{0,16},{16,0},{32,48},{48,32},{64,80},{80,64},{96,112},{112,96},{1... | collective-permute-start | bytes 884744 | tf_op jit(solution)/shard_map/swap_parts/ppermute | solution.py:219
  33.5 0.0 collective-permute-done.msg_ref
  33.5 0.0 copy-done.10
  33.5 7.7 %attend_kept.1 = (f32[8,128,128]{2,1,0:T(8,128)S(1)}, f32[8,128]{1,0:T(8,128)S(1)}) custom-call(bf16[8,144,128]{2,1,0:T(8,128)(2,1)S(1)} %collective-permute-done.msg_ref, bf16[4096,128]{1,0:T(8,128)(2,1)S(1)} %bitcast.15, bf16[2048,128]{1,0:T(8,128)(2,1)S(1)} %bitcast.22, bf16[4096,128]{1,0:T(8,128)(2,1)S(1)} %bitcast.18, bf16[2048,128]{1,0:T(8,128)(2,1)S(1)} %bitcast.25, ...), custom_call_target="tpu_custom_call" | custom-call | flops 6442450944 | bytes 6815744 | tf_op jit(solution)/shard_map/attend_kept/pallas_call | solution.py:282
  41.2 0.0 copy-start.4
  41.2 0.0 collective-permute-done.1.two_ref
  41.2 0.5 merge.1
  41.7 0.7 copy-done.4
  42.4 0.5 collective-permute-start.2
  42.9 13.2 %all_to_all.20.parts_ref = bf16[8,144,128]{2,1,0:T(8,128)(2,1)S(1)} all-to-all(bf16[8,144,128]{2,1,0:T(8,128)(2,1)S(1)} %merge.1), channel_id=1, replica_groups={{0,32,64,96,128,160,192,224},{16,48,80,112,144,176,208,240},{1,33,65,97..., dimensions={0} | all-to-all | bytes 589824 | tf_op jit(solution)/shard_map/scatter_rows/all_to_all | solution.py:222
  56.1 1.1 %combine.1 = bf16[8,16,1024]{2,1,0:T(8,128)(2,1)} custom-call(bf16[8,144,128]{2,1,0:T(8,128)(2,1)S(1)} %all_to_all.20.parts_ref), custom_call_target="tpu_custom_call" | custom-call | tf_op jit(solution)/shard_map/combine/pallas_call | solution.py:290
  57.1 3.4 %all-to-all-start.2 = ((bf16[8,16,1024]{2,1,0:T(8,128)(2,1)}), bf16[8,16,1024]{2,1,0:T(8,128)(2,1)S(1)}, u32[]{:S(2)}, u32[]{:S(2)}) async-start(bf16[8,16,1024]{2,1,0:T(8,128)(2,1)} %combine.1), calls=%async_computation.2 | async-start | bytes 524288 | tf_op jit(solution)/shard_map/gather_attended/all_to_all | solution.py:222
  60.6 10.4 %all-to-all-done.2.rows_ref = bf16[8,16,1024]{2,1,0:T(8,128)(2,1)S(1)} async-done(((bf16[8,16,1024]{2,1,0:T(8,128)(2,1)}), bf16[8,16,1024]{2,1,0:T(8,128)(2,1)S(1)}, u32[]{:S(2)}, u32[]{:S(2)}) %all-to-all-start.2) | async-done | bytes 262176 | tf_op jit(solution)/shard_map/gather_attended/all_to_all | solution.py:222
  71.0 0.0 collective-permute-done.2.other_ref
  71.0 0.4 project.1
  71.4 14.6 %all_to_all.21 = bf16[16,16,512]{2,1,0:T(8,128)(2,1)S(1)} all-to-all(bf16[16,16,512]{2,1,0:T(8,128)(2,1)S(1)} %bitcast.19), channel_id=1, replica_groups={{16,0,18,2,20,4,22,6,24,8,26,10,28,12,30,14},{48,32,50,34,52,36,54,38,5..., dimensions={0} | all-to-all | bytes 524288 | tf_op jit(solution)/shard_map/sum_heads/all_to_all | solution.py:306
  86.0 0.7 convert_reduce_fusion
Async XLA Ops:
  0.0 10.1 %copy-start.5 = (bf16[16,128,1,128]{3,1,2,0:T(8,128)(2,1)S(1)}, bf16[16,128,1,128]{3,1,2,0:T(8,128)(2,1)}, u32[]{:S(2)}) copy-start(bf16[16,128,1,128]{3,1,2,0:T(8,128)(2,1)} %param.13) | copy-start | bytes 1572868
  1.6 21.0 %all-to-all-start = ((bf16[8,144,128]{2,1,0:T(8,128)(2,1)}), bf16[8,144,128]{2,1,0:T(8,128)(2,1)S(1)}, u32[]{:S(2)}, u32[]{:S(2)}) async-start(bf16[8,144,128]{2,1,0:T(8,128)(2,1)} %pack.1), calls=%async_computation | async-start | bytes 589824 | tf_op jit(solution)/shard_map/gather_queries/all_to_all | solution.py:222
  10.1 0.7 copy-start.12
  10.1 0.7 copy-start.11
  10.7 1.2 %copy-start = (bf16[4096,1,128]{2,0,1:T(8,128)(2,1)S(1)}, bf16[4096,1,128]{2,0,1:T(8,128)(2,1)}, u32[]{:S(2)}) copy-start(bf16[4096,1,128]{2,0,1:T(8,128)(2,1)} %param.11) | copy-start | bytes 3145732
  12.0 1.2 %copy-start.2 = (bf16[4096,1,128]{2,0,1:T(8,128)(2,1)S(1)}, bf16[4096,1,128]{2,0,1:T(8,128)(2,1)}, u32[]{:S(2)}) copy-start(bf16[4096,1,128]{2,0,1:T(8,128)(2,1)} %param.12) | copy-start | bytes 3145732
  13.2 1.0 %copy-start.6 = (bf16[16,128,1,128]{3,1,2,0:T(8,128)(2,1)S(1)}, bf16[16,128,1,128]{3,1,2,0:T(8,128)(2,1)}, u32[]{:S(2)}) copy-start(bf16[16,128,1,128]{3,1,2,0:T(8,128)(2,1)} %param.14) | copy-start | bytes 1572868
  14.2 8.8 %copy-start.1 = (bf16[4096,1,128]{2,0,1:T(8,128)(2,1)S(1)}, bf16[4096,1,128]{2,0,1:T(8,128)(2,1)}, u32[]{:S(2)}) copy-start(bf16[4096,1,128]{2,0,1:T(8,128)(2,1)} %param.11) | copy-start | bytes 3145732
  14.2 8.8 %copy-start.3 = (bf16[4096,1,128]{2,0,1:T(8,128)(2,1)S(1)}, bf16[4096,1,128]{2,0,1:T(8,128)(2,1)}, u32[]{:S(2)}) copy-start(bf16[4096,1,128]{2,0,1:T(8,128)(2,1)} %param.12) | copy-start | bytes 3145732
  14.2 8.8 %copy-start.7 = (bf16[16,128,1,128]{3,1,2,0:T(8,128)(2,1)S(1)}, bf16[16,128,1,128]{3,1,2,0:T(8,128)(2,1)}, u32[]{:S(2)}) copy-start(bf16[16,128,1,128]{3,1,2,0:T(8,128)(2,1)} %param.14) | copy-start | bytes 1572868
  14.4 0.7 copy-start.8
  22.6 10.9 %collective-permute-start = (bf16[8,144,128]{2,1,0:T(8,128)(2,1)S(1)}, bf16[8,144,128]{2,1,0:T(8,128)(2,1)S(1)}, u32[]{:S(2)}, u32[]{:S(2)}) collective-permute-start(bf16[8,144,128]{2,1,0:T(8,128)(2,1)S(1)} %all-to-all-done.msg_ref), channel_id=1, source_target_pairs={{0,16},{16,0},{32,48},{48,32},{64,80},{80,64},{96,112},{112,96},{1... | collective-permute-start | bytes 884744 | tf_op jit(solution)/shard_map/gather_queries/ppermute | solution.py:219
  23.1 0.9 %copy-start.9 = (bf16[768,128]{1,0:T(8,128)(2,1)S(1)}, bf16[768,128]{1,0:T(8,128)(2,1)}, u32[]{:S(2)}) copy-start(bf16[768,128]{1,0:T(8,128)(2,1)} %copy-done.8) | copy-start | bytes 589828
  24.0 9.5 %copy-start.10 = (bf16[768,128]{1,0:T(8,128)(2,1)S(1)}, bf16[768,128]{1,0:T(8,128)(2,1)}, u32[]{:S(2)}) copy-start(bf16[768,128]{1,0:T(8,128)(2,1)} %copy-done.8) | copy-start | bytes 589828
  31.7 9.5 %collective-permute-start.1 = (bf16[8,144,128]{2,1,0:T(8,128)(2,1)S(1)}, bf16[8,144,128]{2,1,0:T(8,128)(2,1)S(1)}, u32[]{:S(2)}, u32[]{:S(2)}) collective-permute-start(bf16[8,144,128]{2,1,0:T(8,128)(2,1)S(1)} %attend_sent.1), channel_id=1, source_target_pairs={{0,16},{16,0},{32,48},{48,32},{64,80},{80,64},{96,112},{112,96},{1... | collective-permute-start | bytes 884744 | tf_op jit(solution)/shard_map/swap_parts/ppermute | solution.py:219
  41.2 1.2 %copy-start.4 = (bf16[1024,512]{1,0:T(8,128)(2,1)S(1)}, bf16[1024,512]{1,0:T(8,128)(2,1)}, u32[]{:S(2)}) copy-start(bf16[1024,512]{1,0:T(8,128)(2,1)} %own_ref.1) | copy-start | bytes 3145732
  42.4 28.5 %collective-permute-start.2 = (bf16[1024,512]{1,0:T(8,128)(2,1)S(1)}, bf16[1024,512]{1,0:T(8,128)(2,1)S(1)}, u32[]{:S(2)}, u32[]{:S(2)}) collective-permute-start(bf16[1024,512]{1,0:T(8,128)(2,1)S(1)} %copy-done.4), channel_id=1, source_target_pairs={{0,16},{16,0},{32,48},{48,32},{64,80},{80,64},{96,112},{112,96},{1... | collective-permute-start | bytes 3145736 | tf_op jit(solution)/shard_map/ppermute | solution.py:219
  57.1 13.8 %all-to-all-start.2 = ((bf16[8,16,1024]{2,1,0:T(8,128)(2,1)}), bf16[8,16,1024]{2,1,0:T(8,128)(2,1)S(1)}, u32[]{:S(2)}, u32[]{:S(2)}) async-start(bf16[8,16,1024]{2,1,0:T(8,128)(2,1)} %combine.1), calls=%async_computation.2 | async-start | bytes 524288 | tf_op jit(solution)/shard_map/gather_attended/all_to_all | solution.py:222

commit v3 on v2

--- a/solution.py
+++ b/solution.py
@@ -34,9 +34,9 @@
 
 
 def bar(slots, seq_ref, block_ref, slot_ref, *refs):
-    out_ref = refs[-1]
+    first_ref, second_ref = refs[-2:]
     entries = block_ref.shape[1]
-    blocks = out_ref.shape[0] // TAIL - slots
+    blocks = first_ref.shape[0] // TAIL - slots
     line = lax.broadcasted_iota(jnp.int32, (blocks + slots, entries), 0)
     named = jnp.where(
         line < blocks,
@@ -55,9 +55,9 @@
     hidden = jnp.where(is_block, hits, 1.0 - hits) > 0.5
     bars = jnp.where(hidden, HIDDEN, 0.0)
     for i in range(blocks + slots):
-        out_ref[i * TAIL : (i + 1) * TAIL, :] = jnp.broadcast_to(
-            bars[i : i + 1, :], (TAIL, HD)
-        ).astype(jnp.bfloat16)
+        tile = jnp.broadcast_to(bars[i : i + 1, :], (TAIL, HD)).astype(jnp.bfloat16)
+        first_ref[i * TAIL : (i + 1) * TAIL, :] = tile
+        second_ref[i * TAIL : (i + 1) * TAIL, :] = tile
 
 
 def store_part(out_ref, i, mean, logsum):
@@ -223,6 +223,10 @@
 
     vmem = pltpu.CompilerParams(vmem_limit_bytes=VMEM)
     small = pltpu.CompilerParams(vmem_limit_bytes=16 * 2**20)
+
+    def cost(flops, size):
+        return pl.CostEstimate(flops=flops, bytes_accessed=size, transcendentals=0)
+
     part_shape = jax.ShapeDtypeStruct((pairs, lines + TAIL, width), jnp.bfloat16)
 
     message = pl.pallas_call(
@@ -249,14 +253,14 @@
         doc_values.reshape(doc_len, width),
         patch_values.reshape(slots_here * BLK, width),
     )
-    bars = pl.pallas_call(
+    first_bars, second_bars = pl.pallas_call(
         functools.partial(bar, slots_here),
         in_specs=[in_smem] + [in_vmem] * 6,
-        out_shape=jax.ShapeDtypeStruct((tokens // BLK * TAIL, HD), jnp.bfloat16),
+        out_shape=[jax.ShapeDtypeStruct((tokens // BLK * TAIL, HD), jnp.bfloat16)] * 2,
         compiler_params=small,
+        cost_estimate=cost(10**7, 10**6),
         name="bar",
     )(seq_index.reshape(1), patch_block.reshape(1, -1), patch_slot.reshape(1, -1), *local)
-    local += (bars,)
 
     kept_shapes = (
         jax.ShapeDtypeStruct((pairs, lines, width), jnp.float32),
@@ -276,13 +280,17 @@
             name=body.__name__,
         )
 
-    near_part = attend_lines(attend_sent, part_shape)(near, *local)
+    near_part = attend_lines(attend_sent, part_shape)(near, *local, first_bars)
     with jax.named_scope("swap_parts"):
         far_part = partner(near_part)
-    mean, logsum = attend_lines(attend_kept, kept_shapes)(far, *local)
-    merged = pl.pallas_call(merge, out_shape=part_shape, compiler_params=small, name="merge")(
-        mean, logsum, far_part
-    )
+    mean, logsum = attend_lines(attend_kept, kept_shapes)(far, *local, second_bars)
+    merged = pl.pallas_call(
+        merge,
+        out_shape=part_shape,
+        compiler_params=small,
+        cost_estimate=cost(10**6, 10**6),
+        name="merge",
+    )(mean, logsum, far_part)
     late_weight, merged = lax.optimization_barrier((out_weight, merged))
     other_weight = partner(late_weight)
     with jax.named_scope("scatter_rows"):
@@ -291,6 +299,7 @@
         combine,
         out_shape=jax.ShapeDtypeStruct((pairs, own, heads * width), jnp.bfloat16),
         compiler_params=small,
+        cost_estimate=cost(10**6, 10**6),
         name="combine",
     )(parts)
     with jax.named_scope("gather_attended"):
@@ -300,6 +309,7 @@
         in_specs=[in_smem] + [in_vmem] * 3,
         out_shape=jax.ShapeDtypeStruct((pairs, 2, own, out_weight.shape[1]), jnp.bfloat16),
         compiler_params=small,
+        cost_estimate=cost(3 * 10**8, 2 * 10**6),
         name="project",
     )(side.reshape(1), attended, out_weight, other_weight)
     with jax.named_scope("sum_heads"):

time: 87.2 us -> 87.2 us (level)
    unnamed x26 -> x28, local copies, waits for them, and re-layouts: 6.48 us -> 7.18 us
where the time goes in v3:
time: 87.2 us; the launch traced here: 86.6 us
  blocking collectives  27.8 us (32%)
  Pallas kernels  19.1 us (22%)
  waiting for transfers between devices  17.2 us (20%)
  starting transfers between devices  14.6 us (17%)
  local copies, waits for them, and re-layouts  7.18 us (8%)
    all_to_all x2, waiting for transfers between devices, along_levels(): lax.all_to_all(array, 'seq', 0, 0, tiled=True, axis_index_groups=levels)  17.2 us
    all_to_all x1, blocking collectives, per_device(): lax.all_to_all(products.reshape(2 * pairs, own, out_weight.shape[1]), ('h...  14.6 us
    all_to_all x1, blocking collectives, along_levels(): lax.all_to_all(array, 'seq', 0, 0, tiled=True, axis_index_groups=levels)  13.2 us
    all_to_all x2, starting transfers between devices, along_levels(): lax.all_to_all(array, 'seq', 0, 0, tiled=True, axis_index_groups=levels)  11.9 us
    pallas_call x1, Pallas kernels, per_device(): near_part = attend_lines(attend_sent, part_shape)(near, *local, first_bars)  7.67 us
    pallas_call x1, Pallas kernels, per_device(): attend_lines(attend_kept, kept_shapes)(far, *local, second_bars)  7.65 us
    unnamed x28, local copies, waits for them, and re-layouts  7.18 us
    ppermute x3, starting transfers between devices, partner(): return lax.ppermute(array, 'seq', [(i, i ^ 1) for i in range(seqs)])  2.73 us
  transfers between devices with their start and end apart: 5, of which 2 were waited for; matrix products, arithmetic and copies ran while one was open for 0% of the time, Pallas kernels for 19%

profile of v3, /device:TPU:8, one launch (start us, length us, event | category | flops | bytes accessed | tf_op | source)
XLA Modules:
  0.0 86.6 jit_solution(14907941028740975930)
XLA Ops:
  0.0 0.0 copy-start.5
  0.0 1.6 %pack.1 = bf16[8,144,128]{2,1,0:T(8,128)(2,1)} custom-call(bf16[16,8,128]{2,1,0:T(8,128)(2,1)} %query_ref.1, s32[16]{0:T(128)} %adapter_ref.1), custom_call_target="tpu_custom_call" | custom-call | tf_op jit(solution)/shard_map/pack/pallas_call | solution.py:232
  1.6 8.5 %all-to-all-start = ((bf16[8,144,128]{2,1,0:T(8,128)(2,1)}), bf16[8,144,128]{2,1,0:T(8,128)(2,1)S(1)}, u32[]{:S(2)}, u32[]{:S(2)}) async-start(bf16[8,144,128]{2,1,0:T(8,128)(2,1)} %pack.1), calls=%async_computation | async-start | bytes 589824 | tf_op jit(solution)/shard_map/gather_queries/all_to_all | solution.py:222
  10.1 0.0 copy-start.9
  10.1 0.0 copy-start.8
  10.1 0.0 copy-done.5
  10.1 0.7 copy-done.9
  10.7 0.0 copy-done.8
  10.7 0.0 copy-start
  10.7 1.2 %copy-done = bf16[4096,1,128]{2,0,1:T(8,128)(2,1)S(1)} copy-done((bf16[4096,1,128]{2,0,1:T(8,128)(2,1)S(1)}, bf16[4096,1,128]{2,0,1:T(8,128)(2,1)}, u32[]{:S(2)}) %copy-start) | copy-done | bytes 1048600
  12.0 0.0 copy-start.2
  12.0 1.2 %copy-done.2 = bf16[4096,1,128]{2,0,1:T(8,128)(2,1)S(1)} copy-done((bf16[4096,1,128]{2,0,1:T(8,128)(2,1)S(1)}, bf16[4096,1,128]{2,0,1:T(8,128)(2,1)}, u32[]{:S(2)}) %copy-start.2) | copy-done | bytes 1048600
  13.2 0.0 copy-start.6
  13.2 1.0 %copy-done.6 = bf16[16,128,1,128]{3,1,2,0:T(8,128)(2,1)S(1)} copy-done((bf16[16,128,1,128]{3,1,2,0:T(8,128)(2,1)S(1)}, bf16[16,128,1,128]{3,1,2,0:T(8,128)(2,1)}, u32[]{:S(2)}) %copy-start.6) | copy-done | bytes 524312
  14.2 0.0 copy-start.1
  14.2 0.0 copy-start.3
  14.2 0.0 copy-start.7
  14.2 0.2 bar.1
  14.4 0.0 copy-start.10
  14.4 0.7 copy-done.10
  15.1 0.0 copy-start.12
  15.1 0.7 copy-done.12
  15.8 6.8 %all-to-all-done.msg_ref = bf16[8,144,128]{2,1,0:T(8,128)(2,1)S(1)} async-done(((bf16[8,144,128]{2,1,0:T(8,128)(2,1)}), bf16[8,144,128]{2,1,0:T(8,128)(2,1)S(1)}, u32[]{:S(2)}, u32[]{:S(2)}) %all-to-all-start) | async-done | bytes 294944 | tf_op jit(solution)/shard_map/gather_queries/all_to_all | solution.py:222
  22.6 0.4 collective-permute-start
  23.1 0.0 copy-done.1
  23.1 0.0 copy-done.3
  23.1 0.0 copy-done.7
  23.1 0.0 copy-start.13
  23.1 0.9 %copy-done.13 = bf16[768,128]{1,0:T(8,128)(2,1)S(1)} copy-done((bf16[768,128]{1,0:T(8,128)(2,1)S(1)}, bf16[768,128]{1,0:T(8,128)(2,1)}, u32[]{:S(2)}) %copy-start.13) | copy-done | bytes 196632
  24.0 0.0 copy-start.11
  24.0 7.7 %attend_sent.1 = bf16[8,144,128]{2,1,0:T(8,128)(2,1)S(1)} custom-call(bf16[8,144,128]{2,1,0:T(8,128)(2,1)S(1)} %all-to-all-done.msg_ref, bf16[4096,128]{1,0:T(8,128)(2,1)S(1)} %bitcast.14, bf16[2048,128]{1,0:T(8,128)(2,1)S(1)} %bitcast.21, bf16[4096,128]{1,0:T(8,128)(2,1)S(1)} %bitcast.17, bf16[2048,128]{1,0:T(8,128)(2,1)S(1)} %bitcast.24, ...), custom_call_target="tpu_custom_call" | custom-call | flops 6442450944 | bytes 6815744 | tf_op jit(solution)/shard_map/attend_sent/pallas_call | solution.py:283
  31.7 1.8 %collective-permute-start.1 = (bf16[8,144,128]{2,1,0:T(8,128)(2,1)S(1)}, bf16[8,144,128]{2,1,0:T(8,128)(2,1)S(1)}, u32[]{:S(2)}, u32[]{:S(2)}) collective-permute-start(bf16[8,144,128]{2,1,0:T(8,128)(2,1)S(1)} %attend_sent.1), channel_id=1, source_target_pairs={{0,16},{16,0},{32,48},{48,32},{64,80},{80,64},{96,112},{112,96},{1... | collective-permute-start | bytes 884744 | tf_op jit(solution)/shard_map/swap_parts/ppermute | solution.py:219
  33.5 0.0 collective-permute-done.msg_ref
  33.5 0.0 copy-done.11
  33.5 7.6 %attend_kept.1 = (f32[8,128,128]{2,1,0:T(8,128)S(1)}, f32[8,128]{1,0:T(8,128)S(1)}) custom-call(bf16[8,144,128]{2,1,0:T(8,128)(2,1)S(1)} %collective-permute-done.msg_ref, bf16[4096,128]{1,0:T(8,128)(2,1)S(1)} %bitcast.15, bf16[2048,128]{1,0:T(8,128)(2,1)S(1)} %bitcast.22, bf16[4096,128]{1,0:T(8,128)(2,1)S(1)} %bitcast.18, bf16[2048,128]{1,0:T(8,128)(2,1)S(1)} %bitcast.25, ...), custom_call_target="tpu_custom_call" | custom-call | flops 6442450944 | bytes 6815744 | tf_op jit(solution)/shard_map/attend_kept/pallas_call | solution.py:286
  41.2 0.0 copy-start.4
  41.2 0.0 collective-permute-done.1.two_ref
  41.2 0.5 merge.1
  41.7 0.7 copy-done.4
  42.4 0.5 collective-permute-start.2
  42.9 13.2 %all_to_all.20.parts_ref = bf16[8,144,128]{2,1,0:T(8,128)(2,1)S(1)} all-to-all(bf16[8,144,128]{2,1,0:T(8,128)(2,1)S(1)} %merge.1), channel_id=1, replica_groups={{0,32,64,96,128,160,192,224},{16,48,80,112,144,176,208,240},{1,33,65,97..., dimensions={0} | all-to-all | bytes 589824 | tf_op jit(solution)/shard_map/scatter_rows/all_to_all | solution.py:222
  56.0 1.1 %combine.1 = bf16[8,16,1024]{2,1,0:T(8,128)(2,1)} custom-call(bf16[8,144,128]{2,1,0:T(8,128)(2,1)S(1)} %all_to_all.20.parts_ref), custom_call_target="tpu_custom_call" | custom-call | flops 1000000 | bytes 1000000 | tf_op jit(solution)/shard_map/combine/pallas_call | solution.py:298
  57.1 3.4 %all-to-all-start.2 = ((bf16[8,16,1024]{2,1,0:T(8,128)(2,1)}), bf16[8,16,1024]{2,1,0:T(8,128)(2,1)S(1)}, u32[]{:S(2)}, u32[]{:S(2)}) async-start(bf16[8,16,1024]{2,1,0:T(8,128)(2,1)} %combine.1), calls=%async_computation.2 | async-start | bytes 524288 | tf_op jit(solution)/shard_map/gather_attended/all_to_all | solution.py:222
  60.5 10.4 %all-to-all-done.2.rows_ref = bf16[8,16,1024]{2,1,0:T(8,128)(2,1)S(1)} async-done(((bf16[8,16,1024]{2,1,0:T(8,128)(2,1)}), bf16[8,16,1024]{2,1,0:T(8,128)(2,1)S(1)}, u32[]{:S(2)}, u32[]{:S(2)}) %all-to-all-start.2) | async-done | bytes 262176 | tf_op jit(solution)/shard_map/gather_attended/all_to_all | solution.py:222
  70.9 0.0 collective-permute-done.2.other_ref
  70.9 0.4 project.1
  71.4 14.6 %all_to_all.21 = bf16[16,16,512]{2,1,0:T(8,128)(2,1)S(1)} all-to-all(bf16[16,16,512]{2,1,0:T(8,128)(2,1)S(1)} %bitcast.19), channel_id=1, replica_groups={{16,0,18,2,20,4,22,6,24,8,26,10,28,12,30,14},{48,32,50,34,52,36,54,38,5..., dimensions={0} | all-to-all | bytes 524288 | tf_op jit(solution)/shard_map/sum_heads/all_to_all | solution.py:316
  86.0 0.7 convert_reduce_fusion
Async XLA Ops:
  0.0 10.1 %copy-start.5 = (bf16[16,128,1,128]{3,1,2,0:T(8,128)(2,1)S(1)}, bf16[16,128,1,128]{3,1,2,0:T(8,128)(2,1)}, u32[]{:S(2)}) copy-start(bf16[16,128,1,128]{3,1,2,0:T(8,128)(2,1)} %param.13) | copy-start | bytes 1572868
  1.6 21.0 %all-to-all-start = ((bf16[8,144,128]{2,1,0:T(8,128)(2,1)}), bf16[8,144,128]{2,1,0:T(8,128)(2,1)S(1)}, u32[]{:S(2)}, u32[]{:S(2)}) async-start(bf16[8,144,128]{2,1,0:T(8,128)(2,1)} %pack.1), calls=%async_computation | async-start | bytes 589824 | tf_op jit(solution)/shard_map/gather_queries/all_to_all | solution.py:222
  10.1 0.7 copy-start.9
  10.1 0.7 copy-start.8
  10.7 1.2 %copy-start = (bf16[4096,1,128]{2,0,1:T(8,128)(2,1)S(1)}, bf16[4096,1,128]{2,0,1:T(8,128)(2,1)}, u32[]{:S(2)}) copy-start(bf16[4096,1,128]{2,0,1:T(8,128)(2,1)} %param.11) | copy-start | bytes 3145732
  12.0 1.2 %copy-start.2 = (bf16[4096,1,128]{2,0,1:T(8,128)(2,1)S(1)}, bf16[4096,1,128]{2,0,1:T(8,128)(2,1)}, u32[]{:S(2)}) copy-start(bf16[4096,1,128]{2,0,1:T(8,128)(2,1)} %param.12) | copy-start | bytes 3145732
  13.2 1.0 %copy-start.6 = (bf16[16,128,1,128]{3,1,2,0:T(8,128)(2,1)S(1)}, bf16[16,128,1,128]{3,1,2,0:T(8,128)(2,1)}, u32[]{:S(2)}) copy-start(bf16[16,128,1,128]{3,1,2,0:T(8,128)(2,1)} %param.14) | copy-start | bytes 1572868
  14.2 8.8 %copy-start.1 = (bf16[4096,1,128]{2,0,1:T(8,128)(2,1)S(1)}, bf16[4096,1,128]{2,0,1:T(8,128)(2,1)}, u32[]{:S(2)}) copy-start(bf16[4096,1,128]{2,0,1:T(8,128)(2,1)} %param.11) | copy-start | bytes 3145732
  14.2 8.8 %copy-start.3 = (bf16[4096,1,128]{2,0,1:T(8,128)(2,1)S(1)}, bf16[4096,1,128]{2,0,1:T(8,128)(2,1)}, u32[]{:S(2)}) copy-start(bf16[4096,1,128]{2,0,1:T(8,128)(2,1)} %param.12) | copy-start | bytes 3145732
  14.2 8.8 %copy-start.7 = (bf16[16,128,1,128]{3,1,2,0:T(8,128)(2,1)S(1)}, bf16[16,128,1,128]{3,1,2,0:T(8,128)(2,1)}, u32[]{:S(2)}) copy-start(bf16[16,128,1,128]{3,1,2,0:T(8,128)(2,1)} %param.14) | copy-start | bytes 1572868
  14.4 0.7 copy-start.10
  15.1 0.7 copy-start.12
  22.6 10.9 %collective-permute-start = (bf16[8,144,128]{2,1,0:T(8,128)(2,1)S(1)}, bf16[8,144,128]{2,1,0:T(8,128)(2,1)S(1)}, u32[]{:S(2)}, u32[]{:S(2)}) collective-permute-start(bf16[8,144,128]{2,1,0:T(8,128)(2,1)S(1)} %all-to-all-done.msg_ref), channel_id=1, source_target_pairs={{0,16},{16,0},{32,48},{48,32},{64,80},{80,64},{96,112},{112,96},{1... | collective-permute-start | bytes 884744 | tf_op jit(solution)/shard_map/gather_queries/ppermute | solution.py:219
  23.1 0.9 %copy-start.13 = (bf16[768,128]{1,0:T(8,128)(2,1)S(1)}, bf16[768,128]{1,0:T(8,128)(2,1)}, u32[]{:S(2)}) copy-start(bf16[768,128]{1,0:T(8,128)(2,1)} %copy-done.12) | copy-start | bytes 589828
  24.0 9.5 %copy-start.11 = (bf16[768,128]{1,0:T(8,128)(2,1)S(1)}, bf16[768,128]{1,0:T(8,128)(2,1)}, u32[]{:S(2)}) copy-start(bf16[768,128]{1,0:T(8,128)(2,1)} %copy-done.10) | copy-start | bytes 589828
  31.7 9.5 %collective-permute-start.1 = (bf16[8,144,128]{2,1,0:T(8,128)(2,1)S(1)}, bf16[8,144,128]{2,1,0:T(8,128)(2,1)S(1)}, u32[]{:S(2)}, u32[]{:S(2)}) collective-permute-start(bf16[8,144,128]{2,1,0:T(8,128)(2,1)S(1)} %attend_sent.1), channel_id=1, source_target_pairs={{0,16},{16,0},{32,48},{48,32},{64,80},{80,64},{96,112},{112,96},{1... | collective-permute-start | bytes 884744 | tf_op jit(solution)/shard_map/swap_parts/ppermute | solution.py:219
  41.2 1.2 %copy-start.4 = (bf16[1024,512]{1,0:T(8,128)(2,1)S(1)}, bf16[1024,512]{1,0:T(8,128)(2,1)}, u32[]{:S(2)}) copy-start(bf16[1024,512]{1,0:T(8,128)(2,1)} %own_ref.1) | copy-start | bytes 3145732
  42.4 28.5 %collective-permute-start.2 = (bf16[1024,512]{1,0:T(8,128)(2,1)S(1)}, bf16[1024,512]{1,0:T(8,128)(2,1)S(1)}, u32[]{:S(2)}, u32[]{:S(2)}) collective-permute-start(bf16[1024,512]{1,0:T(8,128)(2,1)S(1)} %copy-done.4), channel_id=1, source_target_pairs={{0,16},{16,0},{32,48},{48,32},{64,80},{80,64},{96,112},{112,96},{1... | collective-permute-start | bytes 3145736 | tf_op jit(solution)/shard_map/ppermute | solution.py:219
  57.1 13.8 %all-to-all-start.2 = ((bf16[8,16,1024]{2,1,0:T(8,128)(2,1)}), bf16[8,16,1024]{2,1,0:T(8,128)(2,1)S(1)}, u32[]{:S(2)}, u32[]{:S(2)}) async-start(bf16[8,16,1024]{2,1,0:T(8,128)(2,1)} %combine.1), calls=%async_computation.2 | async-start | bytes 524288 | tf_op jit(solution)/shard_map/gather_attended/all_to_all | solution.py:222

commit v4 on v3

--- a/solution.py
+++ b/solution.py
@@ -36,7 +36,7 @@
 def bar(slots, seq_ref, block_ref, slot_ref, *refs):
     first_ref, second_ref = refs[-2:]
     entries = block_ref.shape[1]
-    blocks = first_ref.shape[0] // TAIL - slots
+    blocks = first_ref.shape[0] - slots
     line = lax.broadcasted_iota(jnp.int32, (blocks + slots, entries), 0)
     named = jnp.where(
         line < blocks,
@@ -54,10 +54,8 @@
     is_block = lax.broadcasted_iota(jnp.int32, hits.shape, 0) < blocks
     hidden = jnp.where(is_block, hits, 1.0 - hits) > 0.5
     bars = jnp.where(hidden, HIDDEN, 0.0)
-    for i in range(blocks + slots):
-        tile = jnp.broadcast_to(bars[i : i + 1, :], (TAIL, HD)).astype(jnp.bfloat16)
-        first_ref[i * TAIL : (i + 1) * TAIL, :] = tile
-        second_ref[i * TAIL : (i + 1) * TAIL, :] = tile
+    first_ref[...] = bars
+    second_ref[...] = bars
 
 
 def store_part(out_ref, i, mean, logsum):
@@ -74,7 +72,7 @@
     out_ref[i, lines:, :] = tail.astype(jnp.bfloat16)
 
 
-def local_attention(msg_ref, doc_ref, patch_ref, doc_values_ref, patch_values_ref, bars_ref):
+def local_attention(msg_ref, doc_ref, doc_values_ref, patches_ref, bars_ref):
     count = msg_ref.shape[0]
     lines = msg_ref.shape[1] - TAIL
     heads = lines // TAIL
@@ -90,11 +88,15 @@
     ones = jnp.ones((SPAN, HD), jnp.bfloat16)
     peak = accum = None
     bar = 0
+    patch_len = patches_ref.shape[0] // 2
+    patch_ref = patches_ref.at[pl.ds(0, patch_len)]
+    patch_values_ref = patches_ref.at[pl.ds(patch_len, patch_len)]
     for keys_ref, values_ref in ((doc_ref, doc_values_ref), (patch_ref, patch_values_ref)):
         for start in range(0, keys_ref.shape[0], SPAN):
             bars = []
             for _ in range(SPAN // BLK):
-                bars += [bars_ref[bar * TAIL : (bar + 1) * TAIL, :]] * (BLK // TAIL)
+                tile = jnp.broadcast_to(bars_ref[bar : bar + 1, :], (TAIL, HD))
+                bars += [tile.astype(jnp.bfloat16)] * (BLK // TAIL)
                 bar += 1
             keys = jnp.concatenate(
                 [keys_ref[start : start + SPAN, :], jnp.concatenate(bars, 0)], 1
@@ -249,14 +251,19 @@
     in_smem = pl.BlockSpec(memory_space=pltpu.SMEM)
     local = (
         doc_keys.reshape(doc_len, width),
-        patch_keys.reshape(slots_here * BLK, width),
         doc_values.reshape(doc_len, width),
-        patch_values.reshape(slots_here * BLK, width),
+        jnp.concatenate(
+            [
+                patch_keys.reshape(slots_here * BLK, width),
+                patch_values.reshape(slots_here * BLK, width),
+            ],
+            0,
+        ),
     )
     first_bars, second_bars = pl.pallas_call(
         functools.partial(bar, slots_here),
-        in_specs=[in_smem] + [in_vmem] * 6,
-        out_shape=[jax.ShapeDtypeStruct((tokens // BLK * TAIL, HD), jnp.bfloat16)] * 2,
+        in_specs=[in_smem] + [in_vmem] * 5,
+        out_shape=[jax.ShapeDtypeStruct((tokens // BLK, HD), jnp.float32)] * 2,
         compiler_params=small,
         cost_estimate=cost(10**7, 10**6),
         name="bar",

time: 87.2 us -> 86.1 us (0.987)
  local copies, waits for them, and re-layouts: 7.18 us -> 1.13 us
  waiting for transfers between devices: 17.2 us -> 21 us
  other arithmetic: 0.67 us -> 2.08 us
    unnamed x28 -> x10, local copies, waits for them, and re-layouts: 7.18 us -> 1.13 us
    all_to_all x2, waiting for transfers between devices: 17.2 us -> 21 us  [along_levels(): lax.all_to_all(array, 'seq', 0, 0, tiled=True, axis_index_groups=levels)]
    concatenate x0 -> x1, other arithmetic: none -> 1.41 us  [per_device(): jnp.concatenate([patch_keys.reshape(slots_here * BLK, width), patch_value...]
  transfers between devices with their start and end apart: 5 -> 5, of which waited for: 2 -> 2; matrix products, arithmetic and copies ran while one was open for 0% -> 2% of each run, Pallas kernels for 19% -> 19%
where the time goes in v4:
time: 86.1 us; the launch traced here: 85.6 us
  blocking collectives  27.8 us (32%)
  waiting for transfers between devices  21 us (24%)
  Pallas kernels  19 us (22%)
  starting transfers between devices  14.6 us (17%)
  other arithmetic  2.08 us (2%)
  local copies, waits for them, and re-layouts  1.13 us (1%)
    all_to_all x2, waiting for transfers between devices, along_levels(): lax.all_to_all(array, 'seq', 0, 0, tiled=True, axis_index_groups=levels)  21 us
    all_to_all x1, blocking collectives, per_device(): lax.all_to_all(products.reshape(2 * pairs, own, out_weight.shape[1]), ('h...  14.6 us
    all_to_all x1, blocking collectives, along_levels(): lax.all_to_all(array, 'seq', 0, 0, tiled=True, axis_index_groups=levels)  13.2 us
    all_to_all x2, starting transfers between devices, along_levels(): lax.all_to_all(array, 'seq', 0, 0, tiled=True, axis_index_groups=levels)  11.9 us
    pallas_call x1, Pallas kernels, per_device(): near_part = attend_lines(attend_sent, part_shape)(near, *local, first_bars)  7.64 us
    pallas_call x1, Pallas kernels, per_device(): attend_lines(attend_kept, kept_shapes)(far, *local, second_bars)  7.62 us
    ppermute x3, starting transfers between devices, partner(): return lax.ppermute(array, 'seq', [(i, i ^ 1) for i in range(seqs)])  2.73 us
  transfers between devices with their start and end apart: 5, of which 2 were waited for; matrix products, arithmetic and copies ran while one was open for 2% of the time, Pallas kernels for 19%

profile of v4, /device:TPU:8, one launch (start us, length us, event | category | flops | bytes accessed | tf_op | source)
XLA Modules:
  0.0 85.6 jit_solution(1972793453833249842)
XLA Ops:
  0.0 1.6 %pack.1 = bf16[8,144,128]{2,1,0:T(8,128)(2,1)} custom-call(bf16[16,8,128]{2,1,0:T(8,128)(2,1)} %query_ref.1, s32[16]{0:T(128)} %adapter_ref.1), custom_call_target="tpu_custom_call" | custom-call | tf_op jit(solution)/shard_map/pack/pallas_call | solution.py:234
  1.6 8.5 %all-to-all-start = ((bf16[8,144,128]{2,1,0:T(8,128)(2,1)}), bf16[8,144,128]{2,1,0:T(8,128)(2,1)S(1)}, u32[]{:S(2)}, u32[]{:S(2)}) async-start(bf16[8,144,128]{2,1,0:T(8,128)(2,1)} %pack.1), calls=%async_computation | async-start | bytes 589824 | tf_op jit(solution)/shard_map/gather_queries/all_to_all | solution.py:224
  10.0 0.0 copy-start
  10.0 0.0 copy-start.1
  10.0 0.0 copy-start.3
  10.0 0.0 copy-start.4
  10.1 1.4 %pad_maximum_fusion.refs_2_ = bf16[4096,128]{1,0:T(8,128)(2,1)S(1)} fusion(bf16[2048,128]{1,0:T(8,128)(2,1)} %bitcast.23, bf16[2048,128]{1,0:T(8,128)(2,1)} %bitcast.24), kind=kLoop, calls=%fused_computation | loop fusion | flops 2097152 | bytes 2097152 | tf_op jit(solution)/shard_map/concatenate | solution.py:255
  11.5 0.1 copy-done
  11.6 0.3 copy-done.1
  11.9 0.0 copy-done.3
  11.9 0.0 copy-done.4
  11.9 0.1 bar.1
  12.0 10.6 %all-to-all-done.msg_ref = bf16[8,144,128]{2,1,0:T(8,128)(2,1)S(1)} async-done(((bf16[8,144,128]{2,1,0:T(8,128)(2,1)}), bf16[8,144,128]{2,1,0:T(8,128)(2,1)S(1)}, u32[]{:S(2)}, u32[]{:S(2)}) %all-to-all-start) | async-done | bytes 294944 | tf_op jit(solution)/shard_map/gather_queries/all_to_all | solution.py:224
  22.6 0.4 collective-permute-start
  23.0 7.6 %attend_sent.1 = bf16[8,144,128]{2,1,0:T(8,128)(2,1)S(1)} custom-call(bf16[8,144,128]{2,1,0:T(8,128)(2,1)S(1)} %all-to-all-done.msg_ref, bf16[4096,128]{1,0:T(8,128)(2,1)S(1)} %bitcast.14, bf16[4096,128]{1,0:T(8,128)(2,1)S(1)} %bitcast.17, bf16[4096,128]{1,0:T(8,128)(2,1)S(1)} %pad_maximum_fusion.refs_2_, f32[48,128]{1,0:T(8,128)S(1)} %get-tuple-element.14.refs_3_), custom_call_target="tpu_custom_call" | custom-call | flops 6442450944 | bytes 6815744 | tf_op jit(solution)/shard_map/attend_sent/pallas_call | solution.py:290
  30.7 1.8 %collective-permute-start.1 = (bf16[8,144,128]{2,1,0:T(8,128)(2,1)S(1)}, bf16[8,144,128]{2,1,0:T(8,128)(2,1)S(1)}, u32[]{:S(2)}, u32[]{:S(2)}) collective-permute-start(bf16[8,144,128]{2,1,0:T(8,128)(2,1)S(1)} %attend_sent.1), channel_id=1, source_target_pairs={{0,16},{16,0},{32,48},{48,32},{64,80},{80,64},{96,112},{112,96},{1... | collective-permute-start | bytes 884744 | tf_op jit(solution)/shard_map/swap_parts/ppermute | solution.py:221
  32.5 0.0 collective-permute-done.msg_ref
  32.5 7.6 %attend_kept.1 = (f32[8,128,128]{2,1,0:T(8,128)S(1)}, f32[8,128]{1,0:T(8,128)S(1)}) custom-call(bf16[8,144,128]{2,1,0:T(8,128)(2,1)S(1)} %collective-permute-done.msg_ref, bf16[4096,128]{1,0:T(8,128)(2,1)S(1)} %bitcast.15, bf16[4096,128]{1,0:T(8,128)(2,1)S(1)} %bitcast.18, bf16[4096,128]{1,0:T(8,128)(2,1)S(1)} %pad_maximum_fusion.refs_2_, ...), custom_call_target="tpu_custom_call" | custom-call | flops 6442450944 | bytes 6815744 | tf_op jit(solution)/shard_map/attend_kept/pallas_call | solution.py:293
  40.1 0.0 copy-start.2
  40.1 0.0 collective-permute-done.1.two_ref
  40.1 0.5 merge.1
  40.7 0.7 copy-done.2
  41.4 0.4 collective-permute-start.2
  41.8 13.2 %all_to_all.20.parts_ref = bf16[8,144,128]{2,1,0:T(8,128)(2,1)S(1)} all-to-all(bf16[8,144,128]{2,1,0:T(8,128)(2,1)S(1)} %merge.1), channel_id=1, replica_groups={{0,32,64,96,128,160,192,224},{16,48,80,112,144,176,208,240},{1,33,65,97..., dimensions={0} | all-to-all | bytes 589824 | tf_op jit(solution)/shard_map/scatter_rows/all_to_all | solution.py:224
  55.0 1.1 %combine.1 = bf16[8,16,1024]{2,1,0:T(8,128)(2,1)} custom-call(bf16[8,144,128]{2,1,0:T(8,128)(2,1)S(1)} %all_to_all.20.parts_ref), custom_call_target="tpu_custom_call" | custom-call | flops 1000000 | bytes 1000000 | tf_op jit(solution)/shard_map/combine/pallas_call | solution.py:305
  56.1 3.4 %all-to-all-start.2 = ((bf16[8,16,1024]{2,1,0:T(8,128)(2,1)}), bf16[8,16,1024]{2,1,0:T(8,128)(2,1)S(1)}, u32[]{:S(2)}, u32[]{:S(2)}) async-start(bf16[8,16,1024]{2,1,0:T(8,128)(2,1)} %combine.1), calls=%async_computation.2 | async-start | bytes 524288 | tf_op jit(solution)/shard_map/gather_attended/all_to_all | solution.py:224
  59.5 10.4 %all-to-all-done.2.rows_ref = bf16[8,16,1024]{2,1,0:T(8,128)(2,1)S(1)} async-done(((bf16[8,16,1024]{2,1,0:T(8,128)(2,1)}), bf16[8,16,1024]{2,1,0:T(8,128)(2,1)S(1)}, u32[]{:S(2)}, u32[]{:S(2)}) %all-to-all-start.2) | async-done | bytes 262176 | tf_op jit(solution)/shard_map/gather_attended/all_to_all | solution.py:224
  69.9 0.0 collective-permute-done.2.other_ref
  69.9 0.4 project.1
  70.3 14.6 %all_to_all.21 = bf16[16,16,512]{2,1,0:T(8,128)(2,1)S(1)} all-to-all(bf16[16,16,512]{2,1,0:T(8,128)(2,1)S(1)} %bitcast.19), channel_id=1, replica_groups={{16,0,18,2,20,4,22,6,24,8,26,10,28,12,30,14},{48,32,50,34,52,36,54,38,5..., dimensions={0} | all-to-all | bytes 524288 | tf_op jit(solution)/shard_map/sum_heads/all_to_all | solution.py:323
  84.9 0.7 convert_reduce_fusion
Async XLA Ops:
  1.6 21.0 %all-to-all-start = ((bf16[8,144,128]{2,1,0:T(8,128)(2,1)}), bf16[8,144,128]{2,1,0:T(8,128)(2,1)S(1)}, u32[]{:S(2)}, u32[]{:S(2)}) async-start(bf16[8,144,128]{2,1,0:T(8,128)(2,1)} %pack.1), calls=%async_computation | async-start | bytes 589824 | tf_op jit(solution)/shard_map/gather_queries/all_to_all | solution.py:224
  10.0 1.5 %copy-start = (bf16[4096,1,128]{2,0,1:T(8,128)(2,1)S(1)}, bf16[4096,1,128]{2,0,1:T(8,128)(2,1)}, u32[]{:S(2)}) copy-start(bf16[4096,1,128]{2,0,1:T(8,128)(2,1)} %param.11) | copy-start | bytes 3145732
  10.0 1.9 %copy-start.1 = (bf16[4096,1,128]{2,0,1:T(8,128)(2,1)S(1)}, bf16[4096,1,128]{2,0,1:T(8,128)(2,1)}, u32[]{:S(2)}) copy-start(bf16[4096,1,128]{2,0,1:T(8,128)(2,1)} %param.12) | copy-start | bytes 3145732
  10.0 1.8 %copy-start.3 = (s32[256]{0:T(256)S(1)}, s32[256]{0:T(256)}, u32[]{:S(2)}) copy-start(s32[256]{0:T(256)} %param.15) | copy-start | bytes 3076
  10.0 1.8 %copy-start.4 = (s32[256]{0:T(256)S(1)}, s32[256]{0:T(256)}, u32[]{:S(2)}) copy-start(s32[256]{0:T(256)} %param.16) | copy-start | bytes 3076
  22.6 9.9 %collective-permute-start = (bf16[8,144,128]{2,1,0:T(8,128)(2,1)S(1)}, bf16[8,144,128]{2,1,0:T(8,128)(2,1)S(1)}, u32[]{:S(2)}, u32[]{:S(2)}) collective-permute-start(bf16[8,144,128]{2,1,0:T(8,128)(2,1)S(1)} %all-to-all-done.msg_ref), channel_id=1, source_target_pairs={{0,16},{16,0},{32,48},{48,32},{64,80},{80,64},{96,112},{112,96},{1... | collective-permute-start | bytes 884744 | tf_op jit(solution)/shard_map/gather_queries/ppermute | solution.py:221
  30.7 9.5 %collective-permute-start.1 = (bf16[8,144,128]{2,1,0:T(8,128)(2,1)S(1)}, bf16[8,144,128]{2,1,0:T(8,128)(2,1)S(1)}, u32[]{:S(2)}, u32[]{:S(2)}) collective-permute-start(bf16[8,144,128]{2,1,0:T(8,128)(2,1)S(1)} %attend_sent.1), channel_id=1, source_target_pairs={{0,16},{16,0},{32,48},{48,32},{64,80},{80,64},{96,112},{112,96},{1... | collective-permute-start | bytes 884744 | tf_op jit(solution)/shard_map/swap_parts/ppermute | solution.py:221
  40.1 1.2 %copy-start.2 = (bf16[1024,512]{1,0:T(8,128)(2,1)S(1)}, bf16[1024,512]{1,0:T(8,128)(2,1)}, u32[]{:S(2)}) copy-start(bf16[1024,512]{1,0:T(8,128)(2,1)} %own_ref.1) | copy-start | bytes 3145732
  41.4 28.5 %collective-permute-start.2 = (bf16[1024,512]{1,0:T(8,128)(2,1)S(1)}, bf16[1024,512]{1,0:T(8,128)(2,1)S(1)}, u32[]{:S(2)}, u32[]{:S(2)}) collective-permute-start(bf16[1024,512]{1,0:T(8,128)(2,1)S(1)} %copy-done.2), channel_id=1, source_target_pairs={{0,16},{16,0},{32,48},{48,32},{64,80},{80,64},{96,112},{112,96},{1... | collective-permute-start | bytes 3145736 | tf_op jit(solution)/shard_map/ppermute | solution.py:221
  56.1 13.8 %all-to-all-start.2 = ((bf16[8,16,1024]{2,1,0:T(8,128)(2,1)}), bf16[8,16,1024]{2,1,0:T(8,128)(2,1)S(1)}, u32[]{:S(2)}, u32[]{:S(2)}) async-start(bf16[8,16,1024]{2,1,0:T(8,128)(2,1)} %combine.1), calls=%async_computation.2 | async-start | bytes 524288 | tf_op jit(solution)/shard_map/gather_attended/all_to_all | solution.py:224

commit v5 on v4

--- a/solution.py
+++ b/solution.py
@@ -16,10 +16,11 @@
 HIDDEN = -1e30
 TAIL = 16
 SPAN = 512
+OWN_SPAN = 2048
 VMEM = 24 * 2**20
 
 
-def pack(query_ref, adapter_ref, out_ref):
+def pack(query_ref, adapter_ref, out_ref, own_ref):
     rows, heads, width = query_ref.shape
     query = query_ref[...].astype(jnp.float32)
     line = lax.broadcasted_iota(jnp.int32, (rows, width), 0)
@@ -31,12 +32,13 @@
     message = jnp.concatenate(lines, 0).astype(jnp.bfloat16)
     for i in range(out_ref.shape[0]):
         out_ref[i] = message
+    own_ref[0] = message
 
 
 def bar(slots, seq_ref, block_ref, slot_ref, *refs):
-    first_ref, second_ref = refs[-2:]
+    bars_refs = refs[-3:]
     entries = block_ref.shape[1]
-    blocks = first_ref.shape[0] - slots
+    blocks = bars_refs[0].shape[0] - slots
     line = lax.broadcasted_iota(jnp.int32, (blocks + slots, entries), 0)
     named = jnp.where(
         line < blocks,
@@ -54,8 +56,8 @@
     is_block = lax.broadcasted_iota(jnp.int32, hits.shape, 0) < blocks
     hidden = jnp.where(is_block, hits, 1.0 - hits) > 0.5
     bars = jnp.where(hidden, HIDDEN, 0.0)
-    first_ref[...] = bars
-    second_ref[...] = bars
+    for bars_ref in bars_refs:
+        bars_ref[...] = bars
 
 
 def store_part(out_ref, i, mean, logsum):
@@ -72,12 +74,11 @@
     out_ref[i, lines:, :] = tail.astype(jnp.bfloat16)
 
 
-def local_attention(msg_ref, doc_ref, doc_values_ref, patches_ref, bars_ref):
-    count = msg_ref.shape[0]
+def local_attention(places, span, msg_ref, doc_ref, doc_values_ref, patches_ref, bars_ref):
     lines = msg_ref.shape[1] - TAIL
     heads = lines // TAIL
     parts = []
-    for i in range(count):
+    for i in places:
         onehot = msg_ref[i, lines:, :]
         parts.append(
             jnp.concatenate(
@@ -85,23 +86,23 @@
             )
         )
     query = jnp.concatenate(parts, 0)
-    ones = jnp.ones((SPAN, HD), jnp.bfloat16)
+    ones = jnp.ones((span, HD), jnp.bfloat16)
     peak = accum = None
     bar = 0
     patch_len = patches_ref.shape[0] // 2
     patch_ref = patches_ref.at[pl.ds(0, patch_len)]
     patch_values_ref = patches_ref.at[pl.ds(patch_len, patch_len)]
     for keys_ref, values_ref in ((doc_ref, doc_values_ref), (patch_ref, patch_values_ref)):
-        for start in range(0, keys_ref.shape[0], SPAN):
+        for start in range(0, keys_ref.shape[0], span):
             bars = []
-            for _ in range(SPAN // BLK):
+            for _ in range(span // BLK):
                 tile = jnp.broadcast_to(bars_ref[bar : bar + 1, :], (TAIL, HD))
                 bars += [tile.astype(jnp.bfloat16)] * (BLK // TAIL)
                 bar += 1
             keys = jnp.concatenate(
-                [keys_ref[start : start + SPAN, :], jnp.concatenate(bars, 0)], 1
+                [keys_ref[start : start + span, :], jnp.concatenate(bars, 0)], 1
             )
-            values = jnp.concatenate([values_ref[start : start + SPAN, :], ones], 1)
+            values = jnp.concatenate([values_ref[start : start + span, :], ones], 1)
             scores = lax.dot_general(
                 query, keys, (((1,), (1,)), ((), ())), preferred_element_type=jnp.float32
             )
@@ -117,14 +118,26 @@
     return mean, peak * RATE + jnp.log2(total)
 
 
-def attend_sent(msg_ref, *refs):
+def attend_own(msg_ref, *refs):
     *local, out_ref = refs
-    mean, logsum = local_attention(msg_ref, *local)
+    send(range(msg_ref.shape[0]), OWN_SPAN, msg_ref, local, out_ref)
+
+
+def attend_rest(level_ref, own_ref, msg_ref, *refs):
+    *local, out_ref = refs
+    count = msg_ref.shape[0]
+    out_ref[level_ref[0]] = own_ref[0]
+    places = [lax.rem(level_ref[0] + i, count) for i in range(1, count)]
+    send(places, SPAN, msg_ref, local, out_ref)
+
+
+def send(places, span, msg_ref, local, out_ref):
+    mean, logsum = local_attention(places, span, msg_ref, *local)
     lines = msg_ref.shape[1] - TAIL
-    for i in range(msg_ref.shape[0]):
+    for i, place in enumerate(places):
         store_part(
             out_ref,
-            i,
+            place,
             mean[i * lines : (i + 1) * lines],
             jnp.transpose(logsum[i * lines : (i + 1) * lines])[:TAIL, :],
         )
@@ -132,7 +145,7 @@
 
 def attend_kept(msg_ref, *refs):
     *local, mean_ref, logsum_ref = refs
-    mean, logsum = local_attention(msg_ref, *local)
+    mean, logsum = local_attention(range(msg_ref.shape[0]), SPAN, msg_ref, *local)
     lines = msg_ref.shape[1] - TAIL
     for i in range(msg_ref.shape[0]):
         mean_ref[i] = mean[i * lines : (i + 1) * lines]
@@ -230,14 +243,15 @@
         return pl.CostEstimate(flops=flops, bytes_accessed=size, transcendentals=0)
 
     part_shape = jax.ShapeDtypeStruct((pairs, lines + TAIL, width), jnp.bfloat16)
-
-    message = pl.pallas_call(
+    own_shape = jax.ShapeDtypeStruct((1, lines + TAIL, width), jnp.bfloat16)
+
+    message, own_message = pl.pallas_call(
         pack,
         in_specs=[
             pl.BlockSpec(memory_space=pltpu.VMEM),
             pl.BlockSpec(memory_space=pltpu.SMEM),
         ],
-        out_shape=part_shape,
+        out_shape=(part_shape, own_shape),
         compiler_params=pltpu.CompilerParams(vmem_limit_bytes=60 * 2**20),
         name="pack",
     )(queries, row_adapter)
@@ -260,10 +274,10 @@
             0,
         ),
     )
-    first_bars, second_bars = pl.pallas_call(
+    own_bars, first_bars, second_bars = pl.pallas_call(
         functools.partial(bar, slots_here),
         in_specs=[in_smem] + [in_vmem] * 5,
-        out_shape=[jax.ShapeDtypeStruct((tokens // BLK, HD), jnp.float32)] * 2,
+        out_shape=[jax.ShapeDtypeStruct((tokens // BLK, HD), jnp.float32)] * 3,
         compiler_params=small,
         cost_estimate=cost(10**7, 10**6),
         name="bar",
@@ -274,23 +288,27 @@
         jax.ShapeDtypeStruct((pairs, lines), jnp.float32),
     )
 
-    def attend_lines(body, out_shape):
+    def attend_lines(body, out_shape, messages, first_specs=()):
         return pl.pallas_call(
             body,
+            in_specs=list(first_specs) + [in_vmem] * 5,
             out_shape=out_shape,
             compiler_params=vmem,
             cost_estimate=pl.CostEstimate(
-                flops=8 * pairs * lines * tokens * HD,
-                bytes_accessed=8 * tokens * HD + 4 * pairs * lines * width,
-                transcendentals=pairs * lines * tokens,
+                flops=8 * messages * lines * tokens * HD,
+                bytes_accessed=4 * tokens * HD + 4 * messages * lines * width,
+                transcendentals=messages * lines * tokens,
             ),
             name=body.__name__,
         )
 
-    near_part = attend_lines(attend_sent, part_shape)(near, *local, first_bars)
+    own_part = attend_lines(attend_own, own_shape, 1)(own_message, *local, own_bars)
+    near_part = attend_lines(attend_rest, part_shape, pairs - 1, (in_smem, in_vmem))(
+        (seq_index // 2).reshape(1), own_part, near, *local, first_bars
+    )
     with jax.named_scope("swap_parts"):
         far_part = partner(near_part)
-    mean, logsum = attend_lines(attend_kept, kept_shapes)(far, *local, second_bars)
+    mean, logsum = attend_lines(attend_kept, kept_shapes, pairs)(far, *local, second_bars)
     merged = pl.pallas_call(
         merge,
         out_shape=part_shape,

time: 86.1 us -> 83.8 us (0.973)
  waiting for transfers between devices: 21 us -> 7.66 us
  blocking collectives: 27.8 us -> 40.6 us
  starting transfers between devices: 14.6 us -> 11.2 us
  Pallas kernels: 19 us -> 19.9 us
    all_to_all x2 -> x1, waiting for transfers between devices: 21 us -> 7.65 us  [along_levels(): lax.all_to_all(array, 'seq', 0, 0, tiled=True, axis_index_groups=levels)]
    all_to_all x1 -> x2, blocking collectives: 13.2 us -> 26.1 us  [along_levels(): lax.all_to_all(array, 'seq', 0, 0, tiled=True, axis_index_groups=levels)]
    all_to_all x2 -> x1, starting transfers between devices: 11.9 us -> 8.47 us  [along_levels(): lax.all_to_all(array, 'seq', 0, 0, tiled=True, axis_index_groups=levels)]
    pallas_call x2 -> x3, Pallas kernels: 15.3 us -> 16.9 us  [the longest x1 7.62 us: per_device(): attend_lines(attend_kept, kept_shapes, pairs)(far, *local, second_bars)]
    unnamed x10 -> x12, local copies, waits for them, and re-layouts: 1.13 us -> 1.75 us
  transfers between devices with their start and end apart: 5 -> 4, of which waited for: 2 -> 1; matrix products, arithmetic and copies ran while one was open for 2% -> 2% of each run, Pallas kernels for 19% -> 21%
where the time goes in v5:
time: 83.8 us; the launch traced here: 83.3 us
  blocking collectives  40.6 us (48%)
  Pallas kernels  19.9 us (24%)
  starting transfers between devices  11.2 us (13%)
  waiting for transfers between devices  7.66 us (9%)
  other arithmetic  2.08 us (2%)
  local copies, waits for them, and re-layouts  1.75 us (2%)
    all_to_all x2, blocking collectives, along_levels(): lax.all_to_all(array, 'seq', 0, 0, tiled=True, axis_index_groups=levels)  26.1 us
    all_to_all x1, blocking collectives, per_device(): lax.all_to_all(products.reshape(2 * pairs, own, out_weight.shape[1]), ('h...  14.6 us
    all_to_all x1, starting transfers between devices, along_levels(): lax.all_to_all(array, 'seq', 0, 0, tiled=True, axis_index_groups=levels)  8.47 us
    all_to_all x1, waiting for transfers between devices, along_levels(): lax.all_to_all(array, 'seq', 0, 0, tiled=True, axis_index_groups=levels)  7.65 us
    pallas_call x1, Pallas kernels, per_device(): attend_lines(attend_kept, kept_shapes, pairs)(far, *local, second_bars)  7.62 us
    pallas_call x1, Pallas kernels, per_device(): attend_lines(attend_rest, part_shape, pairs - 1, (in_smem, in_vmem))  6.98 us
    ppermute x3, starting transfers between devices, partner(): return lax.ppermute(array, 'seq', [(i, i ^ 1) for i in range(seqs)])  2.73 us
    pallas_call x1, Pallas kernels, per_device(): attend_lines(attend_own, own_shape, 1)(own_message, *local, own_bars)  2.3 us
  transfers between devices with their start and end apart: 4, of which 1 were waited for; matrix products, arithmetic and copies ran while one was open for 2% of the time, Pallas kernels for 21%

profile of v5, /device:TPU:8, one launch (start us, length us, event | category | flops | bytes accessed | tf_op | source)
XLA Modules:
  0.0 83.3 jit_solution(12217396974119827810)
XLA Ops:
  0.0 1.6 %pack.1 = (bf16[8,144,128]{2,1,0:T(8,128)(2,1)}, bf16[1,144,128]{2,1,0:T(8,128)(2,1)}) custom-call(bf16[16,8,128]{2,1,0:T(8,128)(2,1)} %query_ref.1, s32[16]{0:T(128)} %adapter_ref.1), custom_call_target="tpu_custom_call" | custom-call | tf_op jit(solution)/shard_map/pack/pallas_call | solution.py:248
  1.6 8.5 %all-to-all-start = ((bf16[8,144,128]{2,1,0:T(8,128)(2,1)}), bf16[8,144,128]{2,1,0:T(8,128)(2,1)S(1)}, u32[]{:S(2)}, u32[]{:S(2)}) async-start(bf16[8,144,128]{2,1,0:T(8,128)(2,1)} %get-tuple-element.14), calls=%async_computation | async-start | bytes 589824 | tf_op jit(solution)/shard_map/gather_queries/all_to_all | solution.py:237
  10.0 0.0 copy-start
  10.0 0.0 copy-start.1
  10.0 0.0 copy-start.4
  10.1 0.0 copy-start.5
  10.1 1.4 %pad_maximum_fusion.refs_2_ = bf16[4096,128]{1,0:T(8,128)(2,1)S(1)} fusion(bf16[2048,128]{1,0:T(8,128)(2,1)} %bitcast.26, bf16[2048,128]{1,0:T(8,128)(2,1)} %bitcast.27), kind=kLoop, calls=%fused_computation | loop fusion | flops 2097152 | bytes 2097152 | tf_op jit(solution)/shard_map/concatenate | solution.py:269
  11.5 0.1 copy-done
  11.6 0.3 copy-done.1
  11.9 0.0 copy-done.4
  11.9 0.0 copy-done.5
  11.9 0.0 copy-start.3
  11.9 0.1 bar.1
  12.0 0.6 copy-done.3
  12.7 2.3 %attend_own.1.own_ref = bf16[1,144,128]{2,1,0:T(8,128)(2,1)S(1)} custom-call(bf16[1,144,128]{2,1,0:T(8,128)(2,1)S(1)} %copy-done.3, bf16[4096,128]{1,0:T(8,128)(2,1)S(1)} %bitcast.15, bf16[4096,128]{1,0:T(8,128)(2,1)S(1)} %bitcast.19, bf16[4096,128]{1,0:T(8,128)(2,1)S(1)} %pad_maximum_fusion.refs_2_, f32[48,128]{1,0:T(8,128)S(1)} %get-tuple-element.19.refs_3_), custom_call_target="tpu_custom_call" | custom-call | flops 805306368 | bytes 3211264 | tf_op jit(solution)/shard_map/attend_own/pallas_call | solution.py:305
  15.0 7.7 %all-to-all-done.msg_ref = bf16[8,144,128]{2,1,0:T(8,128)(2,1)S(1)} async-done(((bf16[8,144,128]{2,1,0:T(8,128)(2,1)}), bf16[8,144,128]{2,1,0:T(8,128)(2,1)S(1)}, u32[]{:S(2)}, u32[]{:S(2)}) %all-to-all-start) | async-done | bytes 294944 | tf_op jit(solution)/shard_map/gather_queries/all_to_all | solution.py:237
  22.6 0.4 collective-permute-start
  23.1 7.0 %attend_rest.1 = bf16[8,144,128]{2,1,0:T(8,128)(2,1)S(1)} custom-call(s32[1]{0:T(128)} %bitcast.8.level_ref, bf16[1,144,128]{2,1,0:T(8,128)(2,1)S(1)} %attend_own.1.own_ref, bf16[8,144,128]{2,1,0:T(8,128)(2,1)S(1)} %all-to-all-done.msg_ref, bf16[4096,128]{1,0:T(8,128)(2,1)S(1)} %bitcast.16, bf16[4096,128]{1,0:T(8,128)(2,1)S(1)} %bitcast.20, ...), custom_call_target="tpu_custom_call" | custom-call | flops 5637144576 | bytes 3604480 | tf_op jit(solution)/shard_map/attend_rest/pallas_call | solution.py:306
  30.0 1.8 %collective-permute-start.1 = (bf16[8,144,128]{2,1,0:T(8,128)(2,1)S(1)}, bf16[8,144,128]{2,1,0:T(8,128)(2,1)S(1)}, u32[]{:S(2)}, u32[]{:S(2)}) collective-permute-start(bf16[8,144,128]{2,1,0:T(8,128)(2,1)S(1)} %attend_rest.1), channel_id=1, source_target_pairs={{0,16},{16,0},{32,48},{48,32},{64,80},{80,64},{96,112},{112,96},{1... | collective-permute-start | bytes 884744 | tf_op jit(solution)/shard_map/swap_parts/ppermute | solution.py:234
  31.9 0.0 collective-permute-done.msg_ref
  31.9 7.6 %attend_kept.1 = (f32[8,128,128]{2,1,0:T(8,128)S(1)}, f32[8,128]{1,0:T(8,128)S(1)}) custom-call(bf16[8,144,128]{2,1,0:T(8,128)(2,1)S(1)} %collective-permute-done.msg_ref, bf16[4096,128]{1,0:T(8,128)(2,1)S(1)} %bitcast.17, bf16[4096,128]{1,0:T(8,128)(2,1)S(1)} %bitcast.21, bf16[4096,128]{1,0:T(8,128)(2,1)S(1)} %pad_maximum_fusion.refs_2_, ...), custom_call_target="tpu_custom_call" | custom-call | flops 6442450944 | bytes 3670016 | tf_op jit(solution)/shard_map/attend_kept/pallas_call | solution.py:311
  39.5 0.0 copy-start.2
  39.5 0.0 collective-permute-done.1.two_ref
  39.5 0.5 merge.1
  40.0 0.7 copy-done.2
  40.7 0.4 collective-permute-start.2
  41.2 13.2 %all_to_all.20.parts_ref = bf16[8,144,128]{2,1,0:T(8,128)(2,1)S(1)} all-to-all(bf16[8,144,128]{2,1,0:T(8,128)(2,1)S(1)} %merge.1), channel_id=1, replica_groups={{0,32,64,96,128,160,192,224},{16,48,80,112,144,176,208,240},{1,33,65,97..., dimensions={0} | all-to-all | bytes 589824 | tf_op jit(solution)/shard_map/scatter_rows/all_to_all | solution.py:237
  54.4 0.4 combine.1
  54.7 12.9 %all_to_all.21.rows_ref = bf16[8,16,1024]{2,1,0:T(8,128)(2,1)S(1)} all-to-all(bf16[8,16,1024]{2,1,0:T(8,128)(2,1)S(1)} %combine.1), channel_id=1, replica_groups={{0,32,64,96,128,160,192,224},{16,48,80,112,144,176,208,240},{1,33,65,97..., dimensions={0} | all-to-all | bytes 524288 | tf_op jit(solution)/shard_map/gather_attended/all_to_all | solution.py:237
  67.6 0.0 collective-permute-done.2.other_ref
  67.6 0.4 project.1
  68.1 14.6 %all_to_all.22 = bf16[16,16,512]{2,1,0:T(8,128)(2,1)S(1)} all-to-all(bf16[16,16,512]{2,1,0:T(8,128)(2,1)S(1)} %bitcast.22), channel_id=1, replica_groups={{16,0,18,2,20,4,22,6,24,8,26,10,28,12,30,14},{48,32,50,34,52,36,54,38,5..., dimensions={0} | all-to-all | bytes 524288 | tf_op jit(solution)/shard_map/sum_heads/all_to_all | solution.py:341
  82.6 0.7 convert_reduce_fusion
Async XLA Ops:
  1.6 21.0 %all-to-all-start = ((bf16[8,144,128]{2,1,0:T(8,128)(2,1)}), bf16[8,144,128]{2,1,0:T(8,128)(2,1)S(1)}, u32[]{:S(2)}, u32[]{:S(2)}) async-start(bf16[8,144,128]{2,1,0:T(8,128)(2,1)} %get-tuple-element.14), calls=%async_computation | async-start | bytes 589824 | tf_op jit(solution)/shard_map/gather_queries/all_to_all | solution.py:237
  10.0 1.5 %copy-start = (bf16[4096,1,128]{2,0,1:T(8,128)(2,1)S(1)}, bf16[4096,1,128]{2,0,1:T(8,128)(2,1)}, u32[]{:S(2)}) copy-start(bf16[4096,1,128]{2,0,1:T(8,128)(2,1)} %param.11) | copy-start | bytes 3145732
  10.0 1.9 %copy-start.1 = (bf16[4096,1,128]{2,0,1:T(8,128)(2,1)S(1)}, bf16[4096,1,128]{2,0,1:T(8,128)(2,1)}, u32[]{:S(2)}) copy-start(bf16[4096,1,128]{2,0,1:T(8,128)(2,1)} %param.12) | copy-start | bytes 3145732
  10.0 1.8 %copy-start.4 = (s32[256]{0:T(256)S(1)}, s32[256]{0:T(256)}, u32[]{:S(2)}) copy-start(s32[256]{0:T(256)} %param.15) | copy-start | bytes 3076
  10.1 1.8 %copy-start.5 = (s32[256]{0:T(256)S(1)}, s32[256]{0:T(256)}, u32[]{:S(2)}) copy-start(s32[256]{0:T(256)} %param.16) | copy-start | bytes 3076
  11.9 0.8 copy-start.3
  22.6 9.3 %collective-permute-start = (bf16[8,144,128]{2,1,0:T(8,128)(2,1)S(1)}, bf16[8,144,128]{2,1,0:T(8,128)(2,1)S(1)}, u32[]{:S(2)}, u32[]{:S(2)}) collective-permute-start(bf16[8,144,128]{2,1,0:T(8,128)(2,1)S(1)} %all-to-all-done.msg_ref), channel_id=1, source_target_pairs={{0,16},{16,0},{32,48},{48,32},{64,80},{80,64},{96,112},{112,96},{1... | collective-permute-start | bytes 884744 | tf_op jit(solution)/shard_map/gather_queries/ppermute | solution.py:234
  30.0 9.5 %collective-permute-start.1 = (bf16[8,144,128]{2,1,0:T(8,128)(2,1)S(1)}, bf16[8,144,128]{2,1,0:T(8,128)(2,1)S(1)}, u32[]{:S(2)}, u32[]{:S(2)}) collective-permute-start(bf16[8,144,128]{2,1,0:T(8,128)(2,1)S(1)} %attend_rest.1), channel_id=1, source_target_pairs={{0,16},{16,0},{32,48},{48,32},{64,80},{80,64},{96,112},{112,96},{1... | collective-permute-start | bytes 884744 | tf_op jit(solution)/shard_map/swap_parts/ppermute | solution.py:234
  39.5 1.2 %copy-start.2 = (bf16[1024,512]{1,0:T(8,128)(2,1)S(1)}, bf16[1024,512]{1,0:T(8,128)(2,1)}, u32[]{:S(2)}) copy-start(bf16[1024,512]{1,0:T(8,128)(2,1)} %own_ref.1) | copy-start | bytes 3145732
  40.7 26.9 %collective-permute-start.2 = (bf16[1024,512]{1,0:T(8,128)(2,1)S(1)}, bf16[1024,512]{1,0:T(8,128)(2,1)S(1)}, u32[]{:S(2)}, u32[]{:S(2)}) collective-permute-start(bf16[1024,512]{1,0:T(8,128)(2,1)S(1)} %copy-done.2), channel_id=1, source_target_pairs={{0,16},{16,0},{32,48},{48,32},{64,80},{80,64},{96,112},{112,96},{1... | collective-permute-start | bytes 3145736 | tf_op jit(solution)/shard_map/ppermute | solution.py:234

commit v6 on v5

--- a/solution.py
+++ b/solution.py
@@ -143,7 +143,7 @@
         )
 
 
-def attend_kept(msg_ref, *refs):
+def attend_kept(_, msg_ref, *refs):
     *local, mean_ref, logsum_ref = refs
     mean, logsum = local_attention(range(msg_ref.shape[0]), SPAN, msg_ref, *local)
     lines = msg_ref.shape[1] - TAIL
@@ -308,7 +308,9 @@
     )
     with jax.named_scope("swap_parts"):
         far_part = partner(near_part)
-    mean, logsum = attend_lines(attend_kept, kept_shapes, pairs)(far, *local, second_bars)
+    mean, logsum = attend_lines(attend_kept, kept_shapes, pairs, (in_vmem,))(
+        out_weight, far, *local, second_bars
+    )
     merged = pl.pallas_call(
         merge,
         out_shape=part_shape,

time: 83.8 us -> 83.1 us (level)
  no operation moved by 1% of the time
where the time goes in v6:
time: 83.1 us; the launch traced here: 82.7 us
  blocking collectives  40.6 us (49%)
  Pallas kernels  19.9 us (24%)
  starting transfers between devices  11.3 us (14%)
  waiting for transfers between devices  7.66 us (9%)
  other arithmetic  2.08 us (3%)
  local copies, waits for them, and re-layouts  1.04 us (1%)
    all_to_all x2, blocking collectives, along_levels(): lax.all_to_all(array, 'seq', 0, 0, tiled=True, axis_index_groups=levels)  26.1 us
    all_to_all x1, blocking collectives, per_device(): lax.all_to_all(products.reshape(2 * pairs, own, out_weight.shape[1]), ('h...  14.6 us
    all_to_all x1, starting transfers between devices, along_levels(): lax.all_to_all(array, 'seq', 0, 0, tiled=True, axis_index_groups=levels)  8.47 us
    all_to_all x1, waiting for transfers between devices, along_levels(): lax.all_to_all(array, 'seq', 0, 0, tiled=True, axis_index_groups=levels)  7.65 us
    pallas_call x1, Pallas kernels, per_device(): attend_lines(attend_kept, kept_shapes, pairs, (in_vmem,))  7.62 us
    pallas_call x1, Pallas kernels, per_device(): attend_lines(attend_rest, part_shape, pairs - 1, (in_smem, in_vmem))  6.98 us
    ppermute x3, starting transfers between devices, partner(): return lax.ppermute(array, 'seq', [(i, i ^ 1) for i in range(seqs)])  2.82 us
    pallas_call x1, Pallas kernels, per_device(): attend_lines(attend_own, own_shape, 1)(own_message, *local, own_bars)  2.3 us
  transfers between devices with their start and end apart: 4, of which 1 were waited for; matrix products, arithmetic and copies ran while one was open for 2% of the time, Pallas kernels for 21%

profile of v6, /device:TPU:8, one launch (start us, length us, event | category | flops | bytes accessed | tf_op | source)
XLA Modules:
  0.0 82.7 jit_solution(8215051238106533706)
XLA Ops:
  0.0 1.6 %pack.1 = (bf16[8,144,128]{2,1,0:T(8,128)(2,1)}, bf16[1,144,128]{2,1,0:T(8,128)(2,1)}) custom-call(bf16[16,8,128]{2,1,0:T(8,128)(2,1)} %query_ref.1, s32[16]{0:T(128)} %adapter_ref.1), custom_call_target="tpu_custom_call" | custom-call | tf_op jit(solution)/shard_map/pack/pallas_call | solution.py:248
  1.6 8.5 %all-to-all-start = ((bf16[8,144,128]{2,1,0:T(8,128)(2,1)}), bf16[8,144,128]{2,1,0:T(8,128)(2,1)S(1)}, u32[]{:S(2)}, u32[]{:S(2)}) async-start(bf16[8,144,128]{2,1,0:T(8,128)(2,1)} %get-tuple-element.14), calls=%async_computation | async-start | bytes 589824 | tf_op jit(solution)/shard_map/gather_queries/all_to_all | solution.py:237
  10.0 0.0 copy-start
  10.0 0.0 copy-start.1
  10.0 0.0 copy-start.4
  10.1 0.0 copy-start.5
  10.1 1.4 %pad_maximum_fusion.refs_2_ = bf16[4096,128]{1,0:T(8,128)(2,1)S(1)} fusion(bf16[2048,128]{1,0:T(8,128)(2,1)} %bitcast.26, bf16[2048,128]{1,0:T(8,128)(2,1)} %bitcast.27), kind=kLoop, calls=%fused_computation | loop fusion | flops 2097152 | bytes 2097152 | tf_op jit(solution)/shard_map/concatenate | solution.py:269
  11.5 0.1 copy-done
  11.6 0.3 copy-done.1
  11.9 0.0 copy-done.4
  11.9 0.0 copy-done.5
  11.9 0.0 copy-start.3
  11.9 0.1 bar.1
  12.0 0.6 copy-done.3
  12.7 2.3 %attend_own.1.own_ref = bf16[1,144,128]{2,1,0:T(8,128)(2,1)S(1)} custom-call(bf16[1,144,128]{2,1,0:T(8,128)(2,1)S(1)} %copy-done.3, bf16[4096,128]{1,0:T(8,128)(2,1)S(1)} %bitcast.15, bf16[4096,128]{1,0:T(8,128)(2,1)S(1)} %bitcast.19, bf16[4096,128]{1,0:T(8,128)(2,1)S(1)} %pad_maximum_fusion.refs_2_, f32[48,128]{1,0:T(8,128)S(1)} %get-tuple-element.19.refs_3_), custom_call_target="tpu_custom_call" | custom-call | flops 805306368 | bytes 3211264 | tf_op jit(solution)/shard_map/attend_own/pallas_call | solution.py:305
  15.0 7.7 %all-to-all-done.msg_ref = bf16[8,144,128]{2,1,0:T(8,128)(2,1)S(1)} async-done(((bf16[8,144,128]{2,1,0:T(8,128)(2,1)}), bf16[8,144,128]{2,1,0:T(8,128)(2,1)S(1)}, u32[]{:S(2)}, u32[]{:S(2)}) %all-to-all-start) | async-done | bytes 294944 | tf_op jit(solution)/shard_map/gather_queries/all_to_all | solution.py:237
  22.6 0.4 collective-permute-start
  23.1 0.0 copy-start.2
  23.1 7.0 %attend_rest.1 = bf16[8,144,128]{2,1,0:T(8,128)(2,1)S(1)} custom-call(s32[1]{0:T(128)} %bitcast.8.level_ref, bf16[1,144,128]{2,1,0:T(8,128)(2,1)S(1)} %attend_own.1.own_ref, bf16[8,144,128]{2,1,0:T(8,128)(2,1)S(1)} %all-to-all-done.msg_ref, bf16[4096,128]{1,0:T(8,128)(2,1)S(1)} %bitcast.16, bf16[4096,128]{1,0:T(8,128)(2,1)S(1)} %bitcast.20, ...), custom_call_target="tpu_custom_call" | custom-call | flops 5637144576 | bytes 3604480 | tf_op jit(solution)/shard_map/attend_rest/pallas_call | solution.py:306
  30.0 1.8 %collective-permute-start.1 = (bf16[8,144,128]{2,1,0:T(8,128)(2,1)S(1)}, bf16[8,144,128]{2,1,0:T(8,128)(2,1)S(1)}, u32[]{:S(2)}, u32[]{:S(2)}) collective-permute-start(bf16[8,144,128]{2,1,0:T(8,128)(2,1)S(1)} %attend_rest.1), channel_id=1, source_target_pairs={{0,16},{16,0},{32,48},{48,32},{64,80},{80,64},{96,112},{112,96},{1... | collective-permute-start | bytes 884744 | tf_op jit(solution)/shard_map/swap_parts/ppermute | solution.py:234
  31.9 0.0 collective-permute-done.msg_ref
  31.9 0.0 copy-done.2
  31.9 7.6 %attend_kept.1 = (f32[8,128,128]{2,1,0:T(8,128)S(1)}, f32[8,128]{1,0:T(8,128)S(1)}) custom-call(bf16[1024,512]{1,0:T(8,128)(2,1)S(1)} %copy-done.2, bf16[8,144,128]{2,1,0:T(8,128)(2,1)S(1)} %collective-permute-done.msg_ref, bf16[4096,128]{1,0:T(8,128)(2,1)S(1)} %bitcast.17, bf16[4096,128]{1,0:T(8,128)(2,1)S(1)} %bitcast.21, ...), custom_call_target="tpu_custom_call" | custom-call | flops 6442450944 | bytes 3670016 | tf_op jit(solution)/shard_map/attend_kept/pallas_call | solution.py:311
  39.5 0.0 collective-permute-done.1.two_ref
  39.5 0.5 merge.1
  40.0 0.5 collective-permute-start.2
  40.6 13.2 %all_to_all.20.parts_ref = bf16[8,144,128]{2,1,0:T(8,128)(2,1)S(1)} all-to-all(bf16[8,144,128]{2,1,0:T(8,128)(2,1)S(1)} %merge.1), channel_id=1, replica_groups={{0,32,64,96,128,160,192,224},{16,48,80,112,144,176,208,240},{1,33,65,97..., dimensions={0} | all-to-all | bytes 589824 | tf_op jit(solution)/shard_map/scatter_rows/all_to_all | solution.py:237
  53.7 0.4 combine.1
  54.1 12.9 %all_to_all.21.rows_ref = bf16[8,16,1024]{2,1,0:T(8,128)(2,1)S(1)} all-to-all(bf16[8,16,1024]{2,1,0:T(8,128)(2,1)S(1)} %combine.1), channel_id=1, replica_groups={{0,32,64,96,128,160,192,224},{16,48,80,112,144,176,208,240},{1,33,65,97..., dimensions={0} | all-to-all | bytes 524288 | tf_op jit(solution)/shard_map/gather_attended/all_to_all | solution.py:237
  67.0 0.0 collective-permute-done.2.other_ref
  67.0 0.4 project.1
  67.5 14.6 %all_to_all.22 = bf16[16,16,512]{2,1,0:T(8,128)(2,1)S(1)} all-to-all(bf16[16,16,512]{2,1,0:T(8,128)(2,1)S(1)} %bitcast.22), channel_id=1, replica_groups={{16,0,18,2,20,4,22,6,24,8,26,10,28,12,30,14},{48,32,50,34,52,36,54,38,5..., dimensions={0} | all-to-all | bytes 524288 | tf_op jit(solution)/shard_map/sum_heads/all_to_all | solution.py:343
  82.0 0.7 convert_reduce_fusion
Async XLA Ops:
  1.6 21.0 %all-to-all-start = ((bf16[8,144,128]{2,1,0:T(8,128)(2,1)}), bf16[8,144,128]{2,1,0:T(8,128)(2,1)S(1)}, u32[]{:S(2)}, u32[]{:S(2)}) async-start(bf16[8,144,128]{2,1,0:T(8,128)(2,1)} %get-tuple-element.14), calls=%async_computation | async-start | bytes 589824 | tf_op jit(solution)/shard_map/gather_queries/all_to_all | solution.py:237
  10.0 1.5 %copy-start = (bf16[4096,1,128]{2,0,1:T(8,128)(2,1)S(1)}, bf16[4096,1,128]{2,0,1:T(8,128)(2,1)}, u32[]{:S(2)}) copy-start(bf16[4096,1,128]{2,0,1:T(8,128)(2,1)} %param.11) | copy-start | bytes 3145732
  10.0 1.9 %copy-start.1 = (bf16[4096,1,128]{2,0,1:T(8,128)(2,1)S(1)}, bf16[4096,1,128]{2,0,1:T(8,128)(2,1)}, u32[]{:S(2)}) copy-start(bf16[4096,1,128]{2,0,1:T(8,128)(2,1)} %param.12) | copy-start | bytes 3145732
  10.0 1.8 %copy-start.4 = (s32[256]{0:T(256)S(1)}, s32[256]{0:T(256)}, u32[]{:S(2)}) copy-start(s32[256]{0:T(256)} %param.15) | copy-start | bytes 3076
  10.1 1.8 %copy-start.5 = (s32[256]{0:T(256)S(1)}, s32[256]{0:T(256)}, u32[]{:S(2)}) copy-start(s32[256]{0:T(256)} %param.16) | copy-start | bytes 3076
  11.9 0.8 copy-start.3
  22.6 9.3 %collective-permute-start = (bf16[8,144,128]{2,1,0:T(8,128)(2,1)S(1)}, bf16[8,144,128]{2,1,0:T(8,128)(2,1)S(1)}, u32[]{:S(2)}, u32[]{:S(2)}) collective-permute-start(bf16[8,144,128]{2,1,0:T(8,128)(2,1)S(1)} %all-to-all-done.msg_ref), channel_id=1, source_target_pairs={{0,16},{16,0},{32,48},{48,32},{64,80},{80,64},{96,112},{112,96},{1... | collective-permute-start | bytes 884744 | tf_op jit(solution)/shard_map/gather_queries/ppermute | solution.py:234
  23.1 8.8 %copy-start.2 = (bf16[1024,512]{1,0:T(8,128)(2,1)S(1)}, bf16[1024,512]{1,0:T(8,128)(2,1)}, u32[]{:S(2)}) copy-start(bf16[1024,512]{1,0:T(8,128)(2,1)} %own_ref.1) | copy-start | bytes 3145732
  30.0 9.5 %collective-permute-start.1 = (bf16[8,144,128]{2,1,0:T(8,128)(2,1)S(1)}, bf16[8,144,128]{2,1,0:T(8,128)(2,1)S(1)}, u32[]{:S(2)}, u32[]{:S(2)}) collective-permute-start(bf16[8,144,128]{2,1,0:T(8,128)(2,1)S(1)} %attend_rest.1), channel_id=1, source_target_pairs={{0,16},{16,0},{32,48},{48,32},{64,80},{80,64},{96,112},{112,96},{1... | collective-permute-start | bytes 884744 | tf_op jit(solution)/shard_map/swap_parts/ppermute | solution.py:234
  40.0 27.0 %collective-permute-start.2 = (bf16[1024,512]{1,0:T(8,128)(2,1)S(1)}, bf16[1024,512]{1,0:T(8,128)(2,1)S(1)}, u32[]{:S(2)}, u32[]{:S(2)}) collective-permute-start(bf16[1024,512]{1,0:T(8,128)(2,1)S(1)} %copy-done.2), channel_id=1, source_target_pairs={{0,16},{16,0},{32,48},{48,32},{64,80},{80,64},{96,112},{112,96},{1... | collective-permute-start | bytes 3145736 | tf_op jit(solution)/shard_map/ppermute | solution.py:234

commit v7 on v6

--- a/solution.py
+++ b/solution.py
@@ -36,7 +36,7 @@
 
 
 def bar(slots, seq_ref, block_ref, slot_ref, *refs):
-    bars_refs = refs[-3:]
+    bars_refs = refs[-4:]
     entries = block_ref.shape[1]
     blocks = bars_refs[0].shape[0] - slots
     line = lax.broadcasted_iota(jnp.int32, (blocks + slots, entries), 0)
@@ -143,13 +143,27 @@
         )
 
 
-def attend_kept(_, msg_ref, *refs):
+def keep(places, span, msg_ref, local, mean_ref, logsum_ref):
+    mean, logsum = local_attention(places, span, msg_ref, *local)
+    lines = msg_ref.shape[1] - TAIL
+    for i, place in enumerate(places):
+        mean_ref[place] = mean[i * lines : (i + 1) * lines]
+        logsum_ref[pl.ds(place, 1), :] = jnp.transpose(logsum[i * lines : (i + 1) * lines])[:1, :]
+
+
+def attend_early(msg_ref, *refs):
     *local, mean_ref, logsum_ref = refs
-    mean, logsum = local_attention(range(msg_ref.shape[0]), SPAN, msg_ref, *local)
-    lines = msg_ref.shape[1] - TAIL
-    for i in range(msg_ref.shape[0]):
-        mean_ref[i] = mean[i * lines : (i + 1) * lines]
-        logsum_ref[i : i + 1, :] = jnp.transpose(logsum[i * lines : (i + 1) * lines])[:1, :]
+    keep([0], OWN_SPAN, msg_ref, local, mean_ref, logsum_ref)
+
+
+def attend_kept(level_ref, _, early_mean_ref, early_logsum_ref, msg_ref, *refs):
+    *local, mean_ref, logsum_ref = refs
+    count = msg_ref.shape[0]
+    level = level_ref[0]
+    mean_ref[level] = early_mean_ref[0]
+    logsum_ref[pl.ds(level, 1), :] = early_logsum_ref[...]
+    places = [lax.rem(level + i, count) for i in range(1, count)]
+    keep(places, SPAN, msg_ref, local, mean_ref, logsum_ref)
 
 
 def columns(flat, lines):
@@ -255,6 +269,7 @@
         compiler_params=pltpu.CompilerParams(vmem_limit_bytes=60 * 2**20),
         name="pack",
     )(queries, row_adapter)
+    early_message = partner(own_message)
     with jax.named_scope("gather_queries"):
         near = along_levels(message)
         far = partner(near)
@@ -274,10 +289,10 @@
             0,
         ),
     )
-    own_bars, first_bars, second_bars = pl.pallas_call(
+    own_bars, early_bars, first_bars, second_bars = pl.pallas_call(
         functools.partial(bar, slots_here),
         in_specs=[in_smem] + [in_vmem] * 5,
-        out_shape=[jax.ShapeDtypeStruct((tokens // BLK, HD), jnp.float32)] * 3,
+        out_shape=[jax.ShapeDtypeStruct((tokens // BLK, HD), jnp.float32)] * 4,
         compiler_params=small,
         cost_estimate=cost(10**7, 10**6),
         name="bar",
@@ -303,13 +318,19 @@
         )
 
     own_part = attend_lines(attend_own, own_shape, 1)(own_message, *local, own_bars)
+    early_shapes = tuple(
+        jax.ShapeDtypeStruct((1, *shape.shape[1:]), shape.dtype) for shape in kept_shapes
+    )
+    early = attend_lines(attend_early, early_shapes, 1)(early_message, *local, early_bars)
+    near, *early = lax.optimization_barrier((near, *early))
+    level = (seq_index // 2).reshape(1)
     near_part = attend_lines(attend_rest, part_shape, pairs - 1, (in_smem, in_vmem))(
-        (seq_index // 2).reshape(1), own_part, near, *local, first_bars
+        level, own_part, near, *local, first_bars
     )
     with jax.named_scope("swap_parts"):
         far_part = partner(near_part)
-    mean, logsum = attend_lines(attend_kept, kept_shapes, pairs, (in_vmem,))(
-        out_weight, far, *local, second_bars
+    mean, logsum = attend_lines(attend_kept, kept_shapes, pairs - 1, (in_smem,) + (in_vmem,) * 3)(
+        level, out_weight, *early, far, *local, second_bars
     )
     merged = pl.pallas_call(
         merge,

time: 83.1 us -> 86.5 us (1.041)
  waiting for transfers between devices: 7.66 us -> 2.52 us
  local copies, waits for them, and re-layouts: 1.04 us -> 4.33 us
  blocking collectives: 40.6 us -> 42.5 us
  Pallas kernels: 19.9 us -> 21.5 us
  starting transfers between devices: 11.3 us -> 12.9 us
    all_to_all x1, waiting for transfers between devices: 7.65 us -> 2.51 us  [along_levels(): lax.all_to_all(array, 'seq', 0, 0, tiled=True, axis_index_groups=levels)]
    ppermute x3 -> x4, starting transfers between devices: 2.82 us -> 6.13 us  [partner(): return lax.ppermute(array, 'seq', [(i, i ^ 1) for i in range(seqs)])]
    unnamed x12 -> x28, local copies, waits for them, and re-layouts: 1.04 us -> 4.33 us
    all_to_all x2, blocking collectives: 26.1 us -> 28.3 us  [along_levels(): lax.all_to_all(array, 'seq', 0, 0, tiled=True, axis_index_groups=levels)]
    all_to_all x1, starting transfers between devices: 8.47 us -> 6.73 us  [along_levels(): lax.all_to_all(array, 'seq', 0, 0, tiled=True, axis_index_groups=levels)]
    pallas_call x1 -> x2, Pallas kernels: 7.62 us -> 9.23 us  [the longest x1 6.95 us: per_device(): attend_lines(attend_kept, kept_shapes, pairs - 1, (in_smem,) + (in_vmem,)...]
  transfers between devices with their start and end apart: 4 -> 5, of which waited for: 1 -> 1; matrix products, arithmetic and copies ran while one was open for 2% -> 2% of each run, Pallas kernels for 21% -> 22%
where the time goes in v7:
time: 86.5 us; the launch traced here: 86 us
  blocking collectives  42.5 us (49%)
  Pallas kernels  21.5 us (25%)
  starting transfers between devices  12.9 us (15%)
  local copies, waits for them, and re-layouts  4.33 us (5%)
  waiting for transfers between devices  2.52 us (3%)
  other arithmetic  2.08 us (2%)
    all_to_all x2, blocking collectives, along_levels(): lax.all_to_all(array, 'seq', 0, 0, tiled=True, axis_index_groups=levels)  28.3 us
    all_to_all x1, blocking collectives, per_device(): lax.all_to_all(products.reshape(2 * pairs, own, out_weight.shape[1]), ('h...  14.3 us
    pallas_call x1, Pallas kernels, per_device(): attend_lines(attend_rest, part_shape, pairs - 1, (in_smem, in_vmem))  6.98 us
    pallas_call x1, Pallas kernels, per_device(): attend_lines(attend_kept, kept_shapes, pairs - 1, (in_smem,) + (in_vmem,)...  6.95 us
    all_to_all x1, starting transfers between devices, along_levels(): lax.all_to_all(array, 'seq', 0, 0, tiled=True, axis_index_groups=levels)  6.73 us
    ppermute x4, starting transfers between devices, partner(): return lax.ppermute(array, 'seq', [(i, i ^ 1) for i in range(seqs)])  6.13 us
    unnamed x28, local copies, waits for them, and re-layouts  4.33 us
    all_to_all x1, waiting for transfers between devices, along_levels(): lax.all_to_all(array, 'seq', 0, 0, tiled=True, axis_index_groups=levels)  2.51 us
  transfers between devices with their start and end apart: 5, of which 1 were waited for; matrix products, arithmetic and copies ran while one was open for 2% of the time, Pallas kernels for 22%

profile of v7, /device:TPU:8, one launch (start us, length us, event | category | flops | bytes accessed | tf_op | source)
XLA Modules:
  0.0 86.0 jit_solution(6971395410438391549)
XLA Ops:
  0.0 1.6 %pack.1 = (bf16[8,144,128]{2,1,0:T(8,128)(2,1)}, bf16[1,144,128]{2,1,0:T(8,128)(2,1)}) custom-call(bf16[16,8,128]{2,1,0:T(8,128)(2,1)} %query_ref.1, s32[16]{0:T(128)} %adapter_ref.1), custom_call_target="tpu_custom_call" | custom-call | tf_op jit(solution)/shard_map/pack/pallas_call | solution.py:262
  1.6 2.2 %collective-permute-start = (bf16[1,144,128]{2,1,0:T(8,128)(2,1)}, bf16[1,144,128]{2,1,0:T(8,128)(2,1)S(1)}, u32[]{:S(2)}, u32[]{:S(2)}) collective-permute-start(bf16[1,144,128]{2,1,0:T(8,128)(2,1)} %get-tuple-element.21.msg_ref), channel_id=1, source_target_pairs={{0,16},{16,0},{32,48},{48,32},{64,80},{80,64},{96,112},{112,96},{1... | collective-permute-start | bytes 110600 | tf_op jit(solution)/shard_map/ppermute | solution.py:248
  3.7 6.7 %all-to-all-start = ((bf16[8,144,128]{2,1,0:T(8,128)(2,1)}), bf16[8,144,128]{2,1,0:T(8,128)(2,1)S(1)}, u32[]{:S(2)}, u32[]{:S(2)}) async-start(bf16[8,144,128]{2,1,0:T(8,128)(2,1)} %get-tuple-element.20), calls=%async_computation | async-start | bytes 589824 | tf_op jit(solution)/shard_map/gather_queries/all_to_all | solution.py:251
  10.5 0.0 copy-start
  10.5 0.0 copy-start.1
  10.5 0.0 copy-start.6
  10.5 0.0 copy-start.7
  10.5 1.4 %pad_maximum_fusion.refs_2_ = bf16[4096,128]{1,0:T(8,128)(2,1)S(1)} fusion(bf16[2048,128]{1,0:T(8,128)(2,1)} %bitcast.28, bf16[2048,128]{1,0:T(8,128)(2,1)} %bitcast.29), kind=kLoop, calls=%fused_computation | loop fusion | flops 2097152 | bytes 2097152 | tf_op jit(solution)/shard_map/concatenate | solution.py:284
  11.9 0.1 copy-done
  12.0 0.3 copy-done.1
  12.3 0.0 copy-done.6
  12.3 0.0 copy-done.7
  12.3 0.0 copy-start.3
  12.3 0.1 bar.1
  12.5 0.0 copy-start.4
  12.5 0.6 copy-done.4
  13.1 0.0 copy-start.10
  13.1 0.6 copy-done.10
  13.7 0.0 copy-start.12
  13.7 0.6 copy-done.12
  14.3 0.0 copy-done.3
  14.3 2.3 %attend_own.1.own_ref = bf16[1,144,128]{2,1,0:T(8,128)(2,1)S(1)} custom-call(bf16[1,144,128]{2,1,0:T(8,128)(2,1)S(1)} %copy-done.3, bf16[4096,128]{1,0:T(8,128)(2,1)S(1)} %bitcast.15, bf16[4096,128]{1,0:T(8,128)(2,1)S(1)} %bitcast.20, bf16[4096,128]{1,0:T(8,128)(2,1)S(1)} %pad_maximum_fusion.refs_2_, f32[48,128]{1,0:T(8,128)S(1)} %get-tuple-element.30.refs_3_), custom_call_target="tpu_custom_call" | custom-call | flops 805306368 | bytes 3211264 | tf_op jit(solution)/shard_map/attend_own/pallas_call | solution.py:320
  16.6 0.0 collective-permute-done.msg_ref
  16.6 0.0 copy-start.5
  16.6 0.7 copy-done.5
  17.3 2.3 %attend_early.1 = (f32[1,128,128]{2,1,0:T(8,128)S(1)}, f32[1,128]{1,0:T(1,128)S(1)}) custom-call(bf16[1,144,128]{2,1,0:T(8,128)(2,1)S(1)} %collective-permute-done.msg_ref, bf16[4096,128]{1,0:T(8,128)(2,1)S(1)} %bitcast.16, bf16[4096,128]{1,0:T(8,128)(2,1)S(1)} %bitcast.21, bf16[4096,128]{1,0:T(8,128)(2,1)S(1)} %pad_maximum_fusion.refs_2_, ...), custom_call_target="tpu_custom_call" | custom-call | flops 805306368 | bytes 3211264 | tf_op jit(solution)/shard_map/attend_early/pallas_call | solution.py:324
  19.6 0.0 copy-start.8
  19.6 0.6 copy-done.8
  20.3 2.5 %all-to-all-done.msg_ref = bf16[8,144,128]{2,1,0:T(8,128)(2,1)S(1)} async-done(((bf16[8,144,128]{2,1,0:T(8,128)(2,1)}), bf16[8,144,128]{2,1,0:T(8,128)(2,1)S(1)}, u32[]{:S(2)}, u32[]{:S(2)}) %all-to-all-start) | async-done | bytes 294944 | tf_op jit(solution)/shard_map/gather_queries/all_to_all | solution.py:251
  22.8 1.6 %collective-permute-start.1 = (bf16[8,144,128]{2,1,0:T(8,128)(2,1)S(1)}, bf16[8,144,128]{2,1,0:T(8,128)(2,1)S(1)}, u32[]{:S(2)}, u32[]{:S(2)}) collective-permute-start(bf16[8,144,128]{2,1,0:T(8,128)(2,1)S(1)} %all-to-all-done.msg_ref), channel_id=1, source_target_pairs={{0,16},{16,0},{32,48},{48,32},{64,80},{80,64},{96,112},{112,96},{1... | collective-permute-start | bytes 884744 | tf_op jit(solution)/shard_map/gather_queries/ppermute | solution.py:248
  24.4 0.0 copy-start.13
  24.4 0.7 copy-done.13
  25.1 0.0 copy-start.2
  25.1 0.0 copy-start.9
  25.1 0.0 copy-start.11
  25.1 7.0 %attend_rest.1 = bf16[8,144,128]{2,1,0:T(8,128)(2,1)S(1)} custom-call(s32[1]{0:T(128)} %bitcast.1.level_ref, bf16[1,144,128]{2,1,0:T(8,128)(2,1)S(1)} %attend_own.1.own_ref, bf16[8,144,128]{2,1,0:T(8,128)(2,1)S(1)} %all-to-all-done.msg_ref, bf16[4096,128]{1,0:T(8,128)(2,1)S(1)} %bitcast.17, bf16[4096,128]{1,0:T(8,128)(2,1)S(1)} %bitcast.22, ...), custom_call_target="tpu_custom_call" | custom-call | flops 5637144576 | bytes 3604480 | tf_op jit(solution)/shard_map/attend_rest/pallas_call | solution.py:327
  32.1 0.7 collective-permute-start.2
  32.8 0.0 collective-permute-done.1.msg_ref
  32.8 0.0 copy-done.2
  32.8 0.0 copy-done.9
  32.8 0.0 copy-done.11
  32.8 6.9 %attend_kept.1 = (f32[8,128,128]{2,1,0:T(8,128)S(1)}, f32[8,128]{1,0:T(8,128)S(1)}) custom-call(s32[1]{0:T(128)} %bitcast.1.level_ref, bf16[1024,512]{1,0:T(8,128)(2,1)S(1)} %copy-done.2, f32[1,128,128]{2,1,0:T(8,128)S(1)} %copy-done.9, f32[1,128]{1,0:T(1,128)S(1)} %get-tuple-element.26.early_logsum_ref, ...), custom_call_target="tpu_custom_call" | custom-call | flops 5637144576 | bytes 3604480 | tf_op jit(solution)/shard_map/attend_kept/pallas_call | solution.py:332
  39.7 0.0 collective-permute-done.2.two_ref
  39.8 0.5 merge.1
  40.3 1.7 %collective-permute-start.3 = (bf16[1024,512]{1,0:T(8,128)(2,1)S(1)}, bf16[1024,512]{1,0:T(8,128)(2,1)S(1)}, u32[]{:S(2)}, u32[]{:S(2)}) collective-permute-start(bf16[1024,512]{1,0:T(8,128)(2,1)S(1)} %copy-done.2), channel_id=1, source_target_pairs={{0,16},{16,0},{32,48},{48,32},{64,80},{80,64},{96,112},{112,96},{1... | collective-permute-start | bytes 3145736 | tf_op jit(solution)/shard_map/ppermute | solution.py:248
  41.9 15.4 %all_to_all.20.parts_ref = bf16[8,144,128]{2,1,0:T(8,128)(2,1)S(1)} all-to-all(bf16[8,144,128]{2,1,0:T(8,128)(2,1)S(1)} %merge.1), channel_id=1, replica_groups={{0,32,64,96,128,160,192,224},{16,48,80,112,144,176,208,240},{1,33,65,97..., dimensions={0} | all-to-all | bytes 589824 | tf_op jit(solution)/shard_map/scatter_rows/all_to_all | solution.py:251
  57.3 0.4 combine.1
  57.7 12.9 %all_to_all.21.rows_ref = bf16[8,16,1024]{2,1,0:T(8,128)(2,1)S(1)} all-to-all(bf16[8,16,1024]{2,1,0:T(8,128)(2,1)S(1)} %combine.1), channel_id=1, replica_groups={{0,32,64,96,128,160,192,224},{16,48,80,112,144,176,208,240},{1,33,65,97..., dimensions={0} | all-to-all | bytes 524288 | tf_op jit(solution)/shard_map/gather_attended/all_to_all | solution.py:251
  70.6 0.0 collective-permute-done.3.other_ref
  70.6 0.4 project.1
  71.0 14.3 %all_to_all.22 = bf16[16,16,512]{2,1,0:T(8,128)(2,1)S(1)} all-to-all(bf16[16,16,512]{2,1,0:T(8,128)(2,1)S(1)} %bitcast.24), channel_id=1, replica_groups={{16,0,18,2,20,4,22,6,24,8,26,10,28,12,30,14},{48,32,50,34,52,36,54,38,5..., dimensions={0} | all-to-all | bytes 524288 | tf_op jit(solution)/shard_map/sum_heads/all_to_all | solution.py:364
  85.3 0.7 convert_reduce_fusion
Async XLA Ops:
  1.6 15.0 %collective-permute-start = (bf16[1,144,128]{2,1,0:T(8,128)(2,1)}, bf16[1,144,128]{2,1,0:T(8,128)(2,1)S(1)}, u32[]{:S(2)}, u32[]{:S(2)}) collective-permute-start(bf16[1,144,128]{2,1,0:T(8,128)(2,1)} %get-tuple-element.21.msg_ref), channel_id=1, source_target_pairs={{0,16},{16,0},{32,48},{48,32},{64,80},{80,64},{96,112},{112,96},{1... | collective-permute-start | bytes 110600 | tf_op jit(solution)/shard_map/ppermute | solution.py:248
  3.7 19.0 %all-to-all-start = ((bf16[8,144,128]{2,1,0:T(8,128)(2,1)}), bf16[8,144,128]{2,1,0:T(8,128)(2,1)S(1)}, u32[]{:S(2)}, u32[]{:S(2)}) async-start(bf16[8,144,128]{2,1,0:T(8,128)(2,1)} %get-tuple-element.20), calls=%async_computation | async-start | bytes 589824 | tf_op jit(solution)/shard_map/gather_queries/all_to_all | solution.py:251
  10.5 1.5 %copy-start = (bf16[4096,1,128]{2,0,1:T(8,128)(2,1)S(1)}, bf16[4096,1,128]{2,0,1:T(8,128)(2,1)}, u32[]{:S(2)}) copy-start(bf16[4096,1,128]{2,0,1:T(8,128)(2,1)} %param.11) | copy-start | bytes 3145732
  10.5 1.9 %copy-start.1 = (bf16[4096,1,128]{2,0,1:T(8,128)(2,1)S(1)}, bf16[4096,1,128]{2,0,1:T(8,128)(2,1)}, u32[]{:S(2)}) copy-start(bf16[4096,1,128]{2,0,1:T(8,128)(2,1)} %param.12) | copy-start | bytes 3145732
  10.5 1.8 %copy-start.6 = (s32[256]{0:T(256)S(1)}, s32[256]{0:T(256)}, u32[]{:S(2)}) copy-start(s32[256]{0:T(256)} %param.15) | copy-start | bytes 3076
  10.5 1.8 %copy-start.7 = (s32[256]{0:T(256)S(1)}, s32[256]{0:T(256)}, u32[]{:S(2)}) copy-start(s32[256]{0:T(256)} %param.16) | copy-start | bytes 3076
  12.3 2.0 %copy-start.3 = (bf16[1,144,128]{2,1,0:T(8,128)(2,1)S(1)}, bf16[1,144,128]{2,1,0:T(8,128)(2,1)}, u32[]{:S(2)}) copy-start(bf16[1,144,128]{2,1,0:T(8,128)(2,1)} %get-tuple-element.21.msg_ref) | copy-start | bytes 110596
  12.5 0.6 copy-start.4
  13.1 0.6 copy-start.10
  13.7 0.6 copy-start.12
  16.6 0.7 copy-start.5
  19.6 0.6 copy-start.8
  22.8 10.0 %collective-permute-start.1 = (bf16[8,144,128]{2,1,0:T(8,128)(2,1)S(1)}, bf16[8,144,128]{2,1,0:T(8,128)(2,1)S(1)}, u32[]{:S(2)}, u32[]{:S(2)}) collective-permute-start(bf16[8,144,128]{2,1,0:T(8,128)(2,1)S(1)} %all-to-all-done.msg_ref), channel_id=1, source_target_pairs={{0,16},{16,0},{32,48},{48,32},{64,80},{80,64},{96,112},{112,96},{1... | collective-permute-start | bytes 884744 | tf_op jit(solution)/shard_map/gather_queries/ppermute | solution.py:248
  24.4 0.7 copy-start.13
  25.1 7.7 %copy-start.2 = (bf16[1024,512]{1,0:T(8,128)(2,1)S(1)}, bf16[1024,512]{1,0:T(8,128)(2,1)}, u32[]{:S(2)}) copy-start(bf16[1024,512]{1,0:T(8,128)(2,1)} %own_ref.1) | copy-start | bytes 3145732
  25.1 7.7 %copy-start.9 = (f32[1,128,128]{2,1,0:T(8,128)S(1)}, f32[1,128,128]{2,1,0:T(8,128)}, u32[]{:S(2)}) copy-start(f32[1,128,128]{2,1,0:T(8,128)} %copy-done.8) | copy-start | bytes 196612
  25.1 7.7 %copy-start.11 = (f32[48,128]{1,0:T(8,128)S(1)}, f32[48,128]{1,0:T(8,128)}, u32[]{:S(2)}) copy-start(f32[48,128]{1,0:T(8,128)} %copy-done.10) | copy-start | bytes 73732
  32.1 7.7 %collective-permute-start.2 = (bf16[8,144,128]{2,1,0:T(8,128)(2,1)S(1)}, bf16[8,144,128]{2,1,0:T(8,128)(2,1)S(1)}, u32[]{:S(2)}, u32[]{:S(2)}) collective-permute-start(bf16[8,144,128]{2,1,0:T(8,128)(2,1)S(1)} %attend_rest.1), channel_id=1, source_target_pairs={{0,16},{16,0},{32,48},{48,32},{64,80},{80,64},{96,112},{112,96},{1... | collective-permute-start | bytes 884744 | tf_op jit(solution)/shard_map/swap_parts/ppermute | solution.py:248
  40.3 30.3 %collective-permute-start.3 = (bf16[1024,512]{1,0:T(8,128)(2,1)S(1)}, bf16[1024,512]{1,0:T(8,128)(2,1)S(1)}, u32[]{:S(2)}, u32[]{:S(2)}) collective-permute-start(bf16[1024,512]{1,0:T(8,128)(2,1)S(1)} %copy-done.2), channel_id=1, source_target_pairs={{0,16},{16,0},{32,48},{48,32},{64,80},{80,64},{96,112},{112,96},{1... | collective-permute-start | bytes 3145736 | tf_op jit(solution)/shard_map/ppermute | solution.py:248

commit v8 on v6

--- a/solution.py
+++ b/solution.py
@@ -203,6 +203,13 @@
         product = product.astype(jnp.bfloat16)
         for i in range(count):
             out_ref[i, place] = product[i * own : (i + 1) * own]
+
+
+def add_shares(shares_ref, out_ref):
+    total = shares_ref[0].astype(jnp.float32)
+    for i in range(1, shares_ref.shape[0]):
+        total = total + shares_ref[i].astype(jnp.float32)
+    out_ref[...] = total
 
 
 def per_device(
@@ -349,7 +356,13 @@
             axis_index_groups=corners,
         )
         shares = shares.reshape(groups, 2 * own, out_weight.shape[1])
-        return jnp.sum(shares.astype(jnp.float32), axis=0)
+        return pl.pallas_call(
+            add_shares,
+            out_shape=jax.ShapeDtypeStruct(shares.shape[1:], jnp.float32),
+            compiler_params=small,
+            cost_estimate=cost(10**6, 10**6),
+            name="add_shares",
+        )(shares)
 
 
 def solution(mesh):

time: 83.1 us -> 83.1 us (level)
  no operation moved by 1% of the time
where the time goes in v8:
time: 83.1 us; the launch traced here: 82.7 us
  blocking collectives  40.6 us (49%)
  Pallas kernels  20.6 us (25%)
  starting transfers between devices  11.3 us (14%)
  waiting for transfers between devices  7.65 us (9%)
  other arithmetic  1.41 us (2%)
  local copies, waits for them, and re-layouts  1.04 us (1%)
    all_to_all x2, blocking collectives, along_levels(): lax.all_to_all(array, 'seq', 0, 0, tiled=True, axis_index_groups=levels)  26.1 us
    all_to_all x1, blocking collectives, per_device(): lax.all_to_all(products.reshape(2 * pairs, own, out_weight.shape[1]), ('h...  14.6 us
    all_to_all x1, starting transfers between devices, along_levels(): lax.all_to_all(array, 'seq', 0, 0, tiled=True, axis_index_groups=levels)  8.47 us
    all_to_all x1, waiting for transfers between devices, along_levels(): lax.all_to_all(array, 'seq', 0, 0, tiled=True, axis_index_groups=levels)  7.64 us
    pallas_call x1, Pallas kernels, per_device(): attend_lines(attend_kept, kept_shapes, pairs, (in_vmem,))  7.62 us
    pallas_call x1, Pallas kernels, per_device(): attend_lines(attend_rest, part_shape, pairs - 1, (in_smem, in_vmem))  6.98 us
    ppermute x3, starting transfers between devices, partner(): return lax.ppermute(array, 'seq', [(i, i ^ 1) for i in range(seqs)])  2.82 us
    pallas_call x1, Pallas kernels, per_device(): attend_lines(attend_own, own_shape, 1)(own_message, *local, own_bars)  2.31 us
  transfers between devices with their start and end apart: 4, of which 1 were waited for; matrix products, arithmetic and copies ran while one was open for 2% of the time, Pallas kernels for 21%

profile of v8, /device:TPU:8, one launch (start us, length us, event | category | flops | bytes accessed | tf_op | source)
XLA Modules:
  0.0 82.7 jit_solution(4039903888805367227)
XLA Ops:
  0.0 1.6 %pack.1 = (bf16[8,144,128]{2,1,0:T(8,128)(2,1)}, bf16[1,144,128]{2,1,0:T(8,128)(2,1)}) custom-call(bf16[16,8,128]{2,1,0:T(8,128)(2,1)} %query_ref.1, s32[16]{0:T(128)} %adapter_ref.1), custom_call_target="tpu_custom_call" | custom-call | tf_op jit(solution)/shard_map/pack/pallas_call | solution.py:255
  1.6 8.5 %all-to-all-start = ((bf16[8,144,128]{2,1,0:T(8,128)(2,1)}), bf16[8,144,128]{2,1,0:T(8,128)(2,1)S(1)}, u32[]{:S(2)}, u32[]{:S(2)}) async-start(bf16[8,144,128]{2,1,0:T(8,128)(2,1)} %get-tuple-element.14), calls=%async_computation | async-start | bytes 589824 | tf_op jit(solution)/shard_map/gather_queries/all_to_all | solution.py:244
  10.0 0.0 copy-start
  10.0 0.0 copy-start.1
  10.0 0.0 copy-start.4
  10.1 0.0 copy-start.5
  10.1 1.4 %pad_maximum_fusion.refs_2_ = bf16[4096,128]{1,0:T(8,128)(2,1)S(1)} fusion(bf16[2048,128]{1,0:T(8,128)(2,1)} %bitcast.23, bf16[2048,128]{1,0:T(8,128)(2,1)} %bitcast.24), kind=kLoop, calls=%fused_computation | loop fusion | flops 2097152 | bytes 2097152 | tf_op jit(solution)/shard_map/concatenate | solution.py:276
  11.5 0.1 copy-done
  11.6 0.3 copy-done.1
  11.9 0.0 copy-done.4
  11.9 0.0 copy-done.5
  11.9 0.0 copy-start.3
  11.9 0.1 bar.1
  12.0 0.6 copy-done.3
  12.7 2.3 %attend_own.1.own_ref = bf16[1,144,128]{2,1,0:T(8,128)(2,1)S(1)} custom-call(bf16[1,144,128]{2,1,0:T(8,128)(2,1)S(1)} %copy-done.3, bf16[4096,128]{1,0:T(8,128)(2,1)S(1)} %bitcast.12, bf16[4096,128]{1,0:T(8,128)(2,1)S(1)} %bitcast.16, bf16[4096,128]{1,0:T(8,128)(2,1)S(1)} %pad_maximum_fusion.refs_2_, f32[48,128]{1,0:T(8,128)S(1)} %get-tuple-element.19.refs_3_), custom_call_target="tpu_custom_call" | custom-call | flops 805306368 | bytes 3211264 | tf_op jit(solution)/shard_map/attend_own/pallas_call | solution.py:312
  15.0 7.6 %all-to-all-done.msg_ref = bf16[8,144,128]{2,1,0:T(8,128)(2,1)S(1)} async-done(((bf16[8,144,128]{2,1,0:T(8,128)(2,1)}), bf16[8,144,128]{2,1,0:T(8,128)(2,1)S(1)}, u32[]{:S(2)}, u32[]{:S(2)}) %all-to-all-start) | async-done | bytes 294944 | tf_op jit(solution)/shard_map/gather_queries/all_to_all | solution.py:244
  22.6 0.4 collective-permute-start
  23.1 0.0 copy-start.2
  23.1 7.0 %attend_rest.1 = bf16[8,144,128]{2,1,0:T(8,128)(2,1)S(1)} custom-call(s32[1]{0:T(128)} %bitcast.8.level_ref, bf16[1,144,128]{2,1,0:T(8,128)(2,1)S(1)} %attend_own.1.own_ref, bf16[8,144,128]{2,1,0:T(8,128)(2,1)S(1)} %all-to-all-done.msg_ref, bf16[4096,128]{1,0:T(8,128)(2,1)S(1)} %bitcast.13, bf16[4096,128]{1,0:T(8,128)(2,1)S(1)} %bitcast.17, ...), custom_call_target="tpu_custom_call" | custom-call | flops 5637144576 | bytes 3604480 | tf_op jit(solution)/shard_map/attend_rest/pallas_call | solution.py:313
  30.0 1.8 %collective-permute-start.1 = (bf16[8,144,128]{2,1,0:T(8,128)(2,1)S(1)}, bf16[8,144,128]{2,1,0:T(8,128)(2,1)S(1)}, u32[]{:S(2)}, u32[]{:S(2)}) collective-permute-start(bf16[8,144,128]{2,1,0:T(8,128)(2,1)S(1)} %attend_rest.1), channel_id=1, source_target_pairs={{0,16},{16,0},{32,48},{48,32},{64,80},{80,64},{96,112},{112,96},{1... | collective-permute-start | bytes 884744 | tf_op jit(solution)/shard_map/swap_parts/ppermute | solution.py:241
  31.9 0.0 collective-permute-done.msg_ref
  31.9 0.0 copy-done.2
  31.9 7.6 %attend_kept.1 = (f32[8,128,128]{2,1,0:T(8,128)S(1)}, f32[8,128]{1,0:T(8,128)S(1)}) custom-call(bf16[1024,512]{1,0:T(8,128)(2,1)S(1)} %copy-done.2, bf16[8,144,128]{2,1,0:T(8,128)(2,1)S(1)} %collective-permute-done.msg_ref, bf16[4096,128]{1,0:T(8,128)(2,1)S(1)} %bitcast.14, bf16[4096,128]{1,0:T(8,128)(2,1)S(1)} %bitcast.18, ...), custom_call_target="tpu_custom_call" | custom-call | flops 6442450944 | bytes 3670016 | tf_op jit(solution)/shard_map/attend_kept/pallas_call | solution.py:318
  39.5 0.0 collective-permute-done.1.two_ref
  39.5 0.5 merge.1
  40.0 0.5 collective-permute-start.2
  40.6 13.2 %all_to_all.20.parts_ref = bf16[8,144,128]{2,1,0:T(8,128)(2,1)S(1)} all-to-all(bf16[8,144,128]{2,1,0:T(8,128)(2,1)S(1)} %merge.1), channel_id=1, replica_groups={{0,32,64,96,128,160,192,224},{16,48,80,112,144,176,208,240},{1,33,65,97..., dimensions={0} | all-to-all | bytes 589824 | tf_op jit(solution)/shard_map/scatter_rows/all_to_all | solution.py:244
  53.8 0.4 combine.1
  54.1 12.9 %all_to_all.21.rows_ref = bf16[8,16,1024]{2,1,0:T(8,128)(2,1)S(1)} all-to-all(bf16[8,16,1024]{2,1,0:T(8,128)(2,1)S(1)} %combine.1), channel_id=1, replica_groups={{0,32,64,96,128,160,192,224},{16,48,80,112,144,176,208,240},{1,33,65,97..., dimensions={0} | all-to-all | bytes 524288 | tf_op jit(solution)/shard_map/gather_attended/all_to_all | solution.py:244
  67.0 0.0 collective-permute-done.2.other_ref
  67.0 0.4 project.1
  67.5 14.6 %all_to_all.22 = bf16[16,16,512]{2,1,0:T(8,128)(2,1)S(1)} all-to-all(bf16[16,16,512]{2,1,0:T(8,128)(2,1)S(1)} %bitcast.20), channel_id=1, replica_groups={{16,0,18,2,20,4,22,6,24,8,26,10,28,12,30,14},{48,32,50,34,52,36,54,38,5..., dimensions={0} | all-to-all | bytes 524288 | tf_op jit(solution)/shard_map/sum_heads/all_to_all | solution.py:350
  82.0 0.7 add_shares.1
Async XLA Ops:
  1.6 21.0 %all-to-all-start = ((bf16[8,144,128]{2,1,0:T(8,128)(2,1)}), bf16[8,144,128]{2,1,0:T(8,128)(2,1)S(1)}, u32[]{:S(2)}, u32[]{:S(2)}) async-start(bf16[8,144,128]{2,1,0:T(8,128)(2,1)} %get-tuple-element.14), calls=%async_computation | async-start | bytes 589824 | tf_op jit(solution)/shard_map/gather_queries/all_to_all | solution.py:244
  10.0 1.5 %copy-start = (bf16[4096,1,128]{2,0,1:T(8,128)(2,1)S(1)}, bf16[4096,1,128]{2,0,1:T(8,128)(2,1)}, u32[]{:S(2)}) copy-start(bf16[4096,1,128]{2,0,1:T(8,128)(2,1)} %param.11) | copy-start | bytes 3145732
  10.0 1.9 %copy-start.1 = (bf16[4096,1,128]{2,0,1:T(8,128)(2,1)S(1)}, bf16[4096,1,128]{2,0,1:T(8,128)(2,1)}, u32[]{:S(2)}) copy-start(bf16[4096,1,128]{2,0,1:T(8,128)(2,1)} %param.12) | copy-start | bytes 3145732
  10.0 1.8 %copy-start.4 = (s32[256]{0:T(256)S(1)}, s32[256]{0:T(256)}, u32[]{:S(2)}) copy-start(s32[256]{0:T(256)} %param.15) | copy-start | bytes 3076
  10.1 1.8 %copy-start.5 = (s32[256]{0:T(256)S(1)}, s32[256]{0:T(256)}, u32[]{:S(2)}) copy-start(s32[256]{0:T(256)} %param.16) | copy-start | bytes 3076
  11.9 0.8 copy-start.3
  22.6 9.3 %collective-permute-start = (bf16[8,144,128]{2,1,0:T(8,128)(2,1)S(1)}, bf16[8,144,128]{2,1,0:T(8,128)(2,1)S(1)}, u32[]{:S(2)}, u32[]{:S(2)}) collective-permute-start(bf16[8,144,128]{2,1,0:T(8,128)(2,1)S(1)} %all-to-all-done.msg_ref), channel_id=1, source_target_pairs={{0,16},{16,0},{32,48},{48,32},{64,80},{80,64},{96,112},{112,96},{1... | collective-permute-start | bytes 884744 | tf_op jit(solution)/shard_map/gather_queries/ppermute | solution.py:241
  23.1 8.8 %copy-start.2 = (bf16[1024,512]{1,0:T(8,128)(2,1)S(1)}, bf16[1024,512]{1,0:T(8,128)(2,1)}, u32[]{:S(2)}) copy-start(bf16[1024,512]{1,0:T(8,128)(2,1)} %own_ref.1) | copy-start | bytes 3145732
  30.0 9.5 %collective-permute-start.1 = (bf16[8,144,128]{2,1,0:T(8,128)(2,1)S(1)}, bf16[8,144,128]{2,1,0:T(8,128)(2,1)S(1)}, u32[]{:S(2)}, u32[]{:S(2)}) collective-permute-start(bf16[8,144,128]{2,1,0:T(8,128)(2,1)S(1)} %attend_rest.1), channel_id=1, source_target_pairs={{0,16},{16,0},{32,48},{48,32},{64,80},{80,64},{96,112},{112,96},{1... | collective-permute-start | bytes 884744 | tf_op jit(solution)/shard_map/swap_parts/ppermute | solution.py:241
  40.0 27.0 %collective-permute-start.2 = (bf16[1024,512]{1,0:T(8,128)(2,1)S(1)}, bf16[1024,512]{1,0:T(8,128)(2,1)S(1)}, u32[]{:S(2)}, u32[]{:S(2)}) collective-permute-start(bf16[1024,512]{1,0:T(8,128)(2,1)S(1)} %copy-done.2), channel_id=1, source_target_pairs={{0,16},{16,0},{32,48},{48,32},{64,80},{80,64},{96,112},{112,96},{1... | collective-permute-start | bytes 3145736 | tf_op jit(solution)/shard_map/ppermute | solution.py:241

commit v9 on v8

--- a/solution.py
+++ b/solution.py
@@ -15,7 +15,7 @@
 RATE = math.log2(math.e) / math.sqrt(HD)
 HIDDEN = -1e30
 TAIL = 16
-SPAN = 512
+SPAN = 1024
 OWN_SPAN = 2048
 VMEM = 24 * 2**20
 

time: 83.1 us -> 84.1 us (1.012)
  Pallas kernels: 20.6 us -> 21.5 us
  transfers between devices with their start and end apart: 4 -> 4, of which waited for: 1 -> 1; matrix products, arithmetic and copies ran while one was open for 2% -> 2% of each run, Pallas kernels for 21% -> 22%
where the time goes in v9:
time: 84.1 us; the launch traced here: 83.6 us
  blocking collectives  40.6 us (48%)
  Pallas kernels  21.5 us (26%)
  starting transfers between devices  11.3 us (13%)
  waiting for transfers between devices  7.65 us (9%)
  other arithmetic  1.41 us (2%)
  local copies, waits for them, and re-layouts  1.04 us (1%)
    all_to_all x2, blocking collectives, along_levels(): lax.all_to_all(array, 'seq', 0, 0, tiled=True, axis_index_groups=levels)  26.1 us
    all_to_all x1, blocking collectives, per_device(): lax.all_to_all(products.reshape(2 * pairs, own, out_weight.shape[1]), ('h...  14.6 us
    all_to_all x1, starting transfers between devices, along_levels(): lax.all_to_all(array, 'seq', 0, 0, tiled=True, axis_index_groups=levels)  8.47 us
    pallas_call x1, Pallas kernels, per_device(): attend_lines(attend_kept, kept_shapes, pairs, (in_vmem,))  8.21 us
    all_to_all x1, waiting for transfers between devices, along_levels(): lax.all_to_all(array, 'seq', 0, 0, tiled=True, axis_index_groups=levels)  7.64 us
    pallas_call x1, Pallas kernels, per_device(): attend_lines(attend_rest, part_shape, pairs - 1, (in_smem, in_vmem))  7.34 us
    ppermute x3, starting transfers between devices, partner(): return lax.ppermute(array, 'seq', [(i, i ^ 1) for i in range(seqs)])  2.82 us
    pallas_call x1, Pallas kernels, per_device(): attend_lines(attend_own, own_shape, 1)(own_message, *local, own_bars)  2.31 us
  transfers between devices with their start and end apart: 4, of which 1 were waited for; matrix products, arithmetic and copies ran while one was open for 2% of the time, Pallas kernels for 22%

profile of v9, /device:TPU:8, one launch (start us, length us, event | category | flops | bytes accessed | tf_op | source)
XLA Modules:
  0.0 83.6 jit_solution(16443204773046888205)
XLA Ops:
  0.0 1.6 %pack.1 = (bf16[8,144,128]{2,1,0:T(8,128)(2,1)}, bf16[1,144,128]{2,1,0:T(8,128)(2,1)}) custom-call(bf16[16,8,128]{2,1,0:T(8,128)(2,1)} %query_ref.1, s32[16]{0:T(128)} %adapter_ref.1), custom_call_target="tpu_custom_call" | custom-call | tf_op jit(solution)/shard_map/pack/pallas_call | solution.py:255
  1.6 8.5 %all-to-all-start = ((bf16[8,144,128]{2,1,0:T(8,128)(2,1)}), bf16[8,144,128]{2,1,0:T(8,128)(2,1)S(1)}, u32[]{:S(2)}, u32[]{:S(2)}) async-start(bf16[8,144,128]{2,1,0:T(8,128)(2,1)} %get-tuple-element.14), calls=%async_computation | async-start | bytes 589824 | tf_op jit(solution)/shard_map/gather_queries/all_to_all | solution.py:244
  10.0 0.0 copy-start
  10.0 0.0 copy-start.1
  10.0 0.0 copy-start.4
  10.1 0.0 copy-start.5
  10.1 1.4 %pad_maximum_fusion.refs_2_ = bf16[4096,128]{1,0:T(8,128)(2,1)S(1)} fusion(bf16[2048,128]{1,0:T(8,128)(2,1)} %bitcast.23, bf16[2048,128]{1,0:T(8,128)(2,1)} %bitcast.24), kind=kLoop, calls=%fused_computation | loop fusion | flops 2097152 | bytes 2097152 | tf_op jit(solution)/shard_map/concatenate | solution.py:276
  11.5 0.1 copy-done
  11.6 0.3 copy-done.1
  11.9 0.0 copy-done.4
  11.9 0.0 copy-done.5
  11.9 0.0 copy-start.3
  11.9 0.1 bar.1
  12.0 0.6 copy-done.3
  12.7 2.3 %attend_own.1.own_ref = bf16[1,144,128]{2,1,0:T(8,128)(2,1)S(1)} custom-call(bf16[1,144,128]{2,1,0:T(8,128)(2,1)S(1)} %copy-done.3, bf16[4096,128]{1,0:T(8,128)(2,1)S(1)} %bitcast.12, bf16[4096,128]{1,0:T(8,128)(2,1)S(1)} %bitcast.16, bf16[4096,128]{1,0:T(8,128)(2,1)S(1)} %pad_maximum_fusion.refs_2_, f32[48,128]{1,0:T(8,128)S(1)} %get-tuple-element.19.refs_3_), custom_call_target="tpu_custom_call" | custom-call | flops 805306368 | bytes 3211264 | tf_op jit(solution)/shard_map/attend_own/pallas_call | solution.py:312
  15.0 7.6 %all-to-all-done.msg_ref = bf16[8,144,128]{2,1,0:T(8,128)(2,1)S(1)} async-done(((bf16[8,144,128]{2,1,0:T(8,128)(2,1)}), bf16[8,144,128]{2,1,0:T(8,128)(2,1)S(1)}, u32[]{:S(2)}, u32[]{:S(2)}) %all-to-all-start) | async-done | bytes 294944 | tf_op jit(solution)/shard_map/gather_queries/all_to_all | solution.py:244
  22.6 0.4 collective-permute-start
  23.1 0.0 copy-start.2
  23.1 7.3 %attend_rest.1 = bf16[8,144,128]{2,1,0:T(8,128)(2,1)S(1)} custom-call(s32[1]{0:T(128)} %bitcast.8.level_ref, bf16[1,144,128]{2,1,0:T(8,128)(2,1)S(1)} %attend_own.1.own_ref, bf16[8,144,128]{2,1,0:T(8,128)(2,1)S(1)} %all-to-all-done.msg_ref, bf16[4096,128]{1,0:T(8,128)(2,1)S(1)} %bitcast.13, bf16[4096,128]{1,0:T(8,128)(2,1)S(1)} %bitcast.17, ...), custom_call_target="tpu_custom_call" | custom-call | flops 5637144576 | bytes 3604480 | tf_op jit(solution)/shard_map/attend_rest/pallas_call | solution.py:313
  30.4 1.8 %collective-permute-start.1 = (bf16[8,144,128]{2,1,0:T(8,128)(2,1)S(1)}, bf16[8,144,128]{2,1,0:T(8,128)(2,1)S(1)}, u32[]{:S(2)}, u32[]{:S(2)}) collective-permute-start(bf16[8,144,128]{2,1,0:T(8,128)(2,1)S(1)} %attend_rest.1), channel_id=1, source_target_pairs={{0,16},{16,0},{32,48},{48,32},{64,80},{80,64},{96,112},{112,96},{1... | collective-permute-start | bytes 884744 | tf_op jit(solution)/shard_map/swap_parts/ppermute | solution.py:241
  32.2 0.0 collective-permute-done.msg_ref
  32.2 0.0 copy-done.2
  32.2 8.2 %attend_kept.1 = (f32[8,128,128]{2,1,0:T(8,128)S(1)}, f32[8,128]{1,0:T(8,128)S(1)}) custom-call(bf16[1024,512]{1,0:T(8,128)(2,1)S(1)} %copy-done.2, bf16[8,144,128]{2,1,0:T(8,128)(2,1)S(1)} %collective-permute-done.msg_ref, bf16[4096,128]{1,0:T(8,128)(2,1)S(1)} %bitcast.14, bf16[4096,128]{1,0:T(8,128)(2,1)S(1)} %bitcast.18, ...), custom_call_target="tpu_custom_call" | custom-call | flops 6442450944 | bytes 3670016 | tf_op jit(solution)/shard_map/attend_kept/pallas_call | solution.py:318
  40.4 0.0 collective-permute-done.1.two_ref
  40.4 0.5 merge.1
  41.0 0.5 collective-permute-start.2
  41.5 13.2 %all_to_all.20.parts_ref = bf16[8,144,128]{2,1,0:T(8,128)(2,1)S(1)} all-to-all(bf16[8,144,128]{2,1,0:T(8,128)(2,1)S(1)} %merge.1), channel_id=1, replica_groups={{0,32,64,96,128,160,192,224},{16,48,80,112,144,176,208,240},{1,33,65,97..., dimensions={0} | all-to-all | bytes 589824 | tf_op jit(solution)/shard_map/scatter_rows/all_to_all | solution.py:244
  54.7 0.4 combine.1
  55.1 12.9 %all_to_all.21.rows_ref = bf16[8,16,1024]{2,1,0:T(8,128)(2,1)S(1)} all-to-all(bf16[8,16,1024]{2,1,0:T(8,128)(2,1)S(1)} %combine.1), channel_id=1, replica_groups={{0,32,64,96,128,160,192,224},{16,48,80,112,144,176,208,240},{1,33,65,97..., dimensions={0} | all-to-all | bytes 524288 | tf_op jit(solution)/shard_map/gather_attended/all_to_all | solution.py:244
  67.9 0.0 collective-permute-done.2.other_ref
  67.9 0.4 project.1
  68.4 14.6 %all_to_all.22 = bf16[16,16,512]{2,1,0:T(8,128)(2,1)S(1)} all-to-all(bf16[16,16,512]{2,1,0:T(8,128)(2,1)S(1)} %bitcast.20), channel_id=1, replica_groups={{16,0,18,2,20,4,22,6,24,8,26,10,28,12,30,14},{48,32,50,34,52,36,54,38,5..., dimensions={0} | all-to-all | bytes 524288 | tf_op jit(solution)/shard_map/sum_heads/all_to_all | solution.py:350
  83.0 0.7 add_shares.1
Async XLA Ops:
  1.6 21.0 %all-to-all-start = ((bf16[8,144,128]{2,1,0:T(8,128)(2,1)}), bf16[8,144,128]{2,1,0:T(8,128)(2,1)S(1)}, u32[]{:S(2)}, u32[]{:S(2)}) async-start(bf16[8,144,128]{2,1,0:T(8,128)(2,1)} %get-tuple-element.14), calls=%async_computation | async-start | bytes 589824 | tf_op jit(solution)/shard_map/gather_queries/all_to_all | solution.py:244
  10.0 1.5 %copy-start = (bf16[4096,1,128]{2,0,1:T(8,128)(2,1)S(1)}, bf16[4096,1,128]{2,0,1:T(8,128)(2,1)}, u32[]{:S(2)}) copy-start(bf16[4096,1,128]{2,0,1:T(8,128)(2,1)} %param.11) | copy-start | bytes 3145732
  10.0 1.9 %copy-start.1 = (bf16[4096,1,128]{2,0,1:T(8,128)(2,1)S(1)}, bf16[4096,1,128]{2,0,1:T(8,128)(2,1)}, u32[]{:S(2)}) copy-start(bf16[4096,1,128]{2,0,1:T(8,128)(2,1)} %param.12) | copy-start | bytes 3145732
  10.0 1.8 %copy-start.4 = (s32[256]{0:T(256)S(1)}, s32[256]{0:T(256)}, u32[]{:S(2)}) copy-start(s32[256]{0:T(256)} %param.15) | copy-start | bytes 3076
  10.1 1.8 %copy-start.5 = (s32[256]{0:T(256)S(1)}, s32[256]{0:T(256)}, u32[]{:S(2)}) copy-start(s32[256]{0:T(256)} %param.16) | copy-start | bytes 3076
  11.9 0.8 copy-start.3
  22.6 9.6 %collective-permute-start = (bf16[8,144,128]{2,1,0:T(8,128)(2,1)S(1)}, bf16[8,144,128]{2,1,0:T(8,128)(2,1)S(1)}, u32[]{:S(2)}, u32[]{:S(2)}) collective-permute-start(bf16[8,144,128]{2,1,0:T(8,128)(2,1)S(1)} %all-to-all-done.msg_ref), channel_id=1, source_target_pairs={{0,16},{16,0},{32,48},{48,32},{64,80},{80,64},{96,112},{112,96},{1... | collective-permute-start | bytes 884744 | tf_op jit(solution)/shard_map/gather_queries/ppermute | solution.py:241
  23.1 9.2 %copy-start.2 = (bf16[1024,512]{1,0:T(8,128)(2,1)S(1)}, bf16[1024,512]{1,0:T(8,128)(2,1)}, u32[]{:S(2)}) copy-start(bf16[1024,512]{1,0:T(8,128)(2,1)} %own_ref.1) | copy-start | bytes 3145732
  30.4 10.0 %collective-permute-start.1 = (bf16[8,144,128]{2,1,0:T(8,128)(2,1)S(1)}, bf16[8,144,128]{2,1,0:T(8,128)(2,1)S(1)}, u32[]{:S(2)}, u32[]{:S(2)}) collective-permute-start(bf16[8,144,128]{2,1,0:T(8,128)(2,1)S(1)} %attend_rest.1), channel_id=1, source_target_pairs={{0,16},{16,0},{32,48},{48,32},{64,80},{80,64},{96,112},{112,96},{1... | collective-permute-start | bytes 884744 | tf_op jit(solution)/shard_map/swap_parts/ppermute | solution.py:241
  41.0 27.0 %collective-permute-start.2 = (bf16[1024,512]{1,0:T(8,128)(2,1)S(1)}, bf16[1024,512]{1,0:T(8,128)(2,1)S(1)}, u32[]{:S(2)}, u32[]{:S(2)}) collective-permute-start(bf16[1024,512]{1,0:T(8,128)(2,1)S(1)} %copy-done.2), channel_id=1, source_target_pairs={{0,16},{16,0},{32,48},{48,32},{64,80},{80,64},{96,112},{112,96},{1... | collective-permute-start | bytes 3145736 | tf_op jit(solution)/shard_map/ppermute | solution.py:241
